TPU v7x, 32 devices: a whole 2x2x4 slice. The times are simulated.
32 devices in a mesh: graph: 2 (over x), blk: 16 (over z, y, core).
Axes of the slice: x: 2, y: 2, z: 4, core: 2. Of those that a mesh axis runs over, the one named last changes fastest.
Arguments:
- node_state: float32 [32, 2048, 128], P('graph', 'blk'), may hold values from -120 to 120
- field_window: float32 [32, 2048, 25], P('graph', 'blk'), may hold values from -6 to 6
- edge_offset: int32 [32, 2048, 6], P('graph', 'blk'), may hold values from -3 to 3
- pde_id: int32 [32], P('graph'), may hold values from 0 to 7
- pde_table: float32 [8, 3], replicated, may hold values from -2 to 2
- cotangent: float32 [32, 2048, 128], P('graph', 'blk'), may hold values from -70 to 70
- edge_w1: float32 [2, 285, 128], replicated, may hold values from -0.375 to 0.375
- edge_b1: float32 [2, 128], replicated, may hold values from -3 to 3
- edge_w2: float32 [2, 128, 128], replicated, may hold values from -0.5 to 0.5
- edge_b2: float32 [2, 128], replicated, may hold values from -3 to 3
- node_w1: float32 [2, 259, 128], replicated, may hold values from -0.375 to 0.375
- node_b1: float32 [2, 128], replicated, may hold values from -3 to 3
- node_w2: float32 [2, 128, 128], replicated, may hold values from -0.5 to 0.5
- node_b2: float32 [2, 128], replicated, may hold values from -3 to 3
Outputs:
- state_out: float32 [32, 2048, 128], P('graph', 'blk')
- grad_state: float32 [32, 2048, 128], P('graph', 'blk')
- grad_edge_w1: float32 [2, 285, 128], replicated
- grad_edge_b1: float32 [2, 128], replicated
- grad_edge_w2: float32 [2, 128, 128], replicated
- grad_edge_b2: float32 [2, 128], replicated
- grad_node_w1: float32 [2, 259, 128], replicated
- grad_node_b1: float32 [2, 128], replicated
- grad_node_w2: float32 [2, 128, 128], replicated
- grad_node_b2: float32 [2, 128], replicated
Inputs may be any that keep to these rules, and one draw needn't show every extreme that they name: `edge_offset`: 0 marks an empty slot; any other value o joins node i to node i + o of the same trajectory, taken around the periodic domain.
All inputs are finite; a program needn't handle non-finite values.
Results may differ from a plain program's by a relative error of at most 0.0003.
Values sent between devices are 32-bit elements; how exact they have to be, the bound alone decides.
A program may use at most 192 MiB of HBM per device.

v0:
```python
import jax
import jax.numpy as jnp
from jax import lax
from jax.sharding import PartitionSpec as P

D = 128
TW = 25
K = 6
HALO = 3
NPDE = 8
LAYERS = 2


EPSILON = 1e-05
PRECISE = lax.Precision.HIGHEST


def padded(cells, sides, width):
    for axis, dim in sides:
        count = lax.axis_size(axis)
        head = lax.slice_in_dim(cells, 0, width, axis=dim)
        tail = lax.slice_in_dim(cells, cells.shape[dim] - width, cells.shape[dim], axis=dim)
        cells = jnp.concatenate(
            [
                lax.ppermute(tail, axis, [(i, (i + 1) % count) for i in range(count)]),
                cells,
                lax.ppermute(head, axis, [((i + 1) % count, i) for i in range(count)]),
            ],
            axis=dim,
        )
    return cells


def swish_act(value):
    return value * jax.nn.sigmoid(value)


def swish_slope(value):
    sigma = jax.nn.sigmoid(value)
    return sigma + value * sigma * (1.0 - sigma)


def project(left, right):
    return jnp.dot(left, right, precision=PRECISE)


def outer_sum(left, right):
    flat_left = left.reshape(-1, left.shape[-1])
    flat_right = right.reshape(-1, right.shape[-1])
    return jnp.dot(flat_left.T, flat_right, precision=PRECISE)


def offset_table():
    return [shift for shift in range(-HALO, HALO + 1) if shift != 0]


def norm_stats(update, node_total):
    center = lax.psum(jnp.sum(update, 1, keepdims=True), "blk") / node_total
    centred = update - center
    variance = lax.psum(jnp.sum(centred * centred, 1, keepdims=True), "blk") / node_total
    return (center, variance)


def forward_layer(
    level, state, state_ext, field_ext, one_hot, slot_mask, pde_theta, params, node_total
):
    weight_edge1 = params[0][level]
    row_count = state.shape[1]
    w_self = weight_edge1[:D]
    w_far = weight_edge1[D : 2 * D]
    w_field = weight_edge1[2 * D : 2 * D + TW]
    w_place = weight_edge1[2 * D + TW]
    w_theta = weight_edge1[2 * D + TW + 1 :]
    field_proj = project(field_ext, w_field)
    anchor = (
        project(state, w_self)
        + field_proj[:, HALO : HALO + row_count]
        + (project(pde_theta, w_theta) + params[1][level])[:, None, :]
    )
    remote = project(state_ext, w_far) - field_proj
    windows = jnp.stack(
        [
            remote[:, HALO + shift : HALO + shift + row_count] - shift / HALO * w_place
            for shift in offset_table()
        ],
        2,
    )
    edge_pre1 = anchor[:, :, None, :] + jnp.einsum(
        "tnks,tnsd->tnkd", one_hot, windows, precision=PRECISE
    )
    edge_pre2 = project(swish_act(edge_pre1), params[2][level]) + params[3][level]
    aggregate = jnp.sum(swish_act(edge_pre2) * slot_mask[..., None], 2) / K
    weight_node1 = params[4][level]
    node_pre1 = (
        project(state, weight_node1[:D])
        + project(aggregate, weight_node1[D : 2 * D])
        + (project(pde_theta, weight_node1[2 * D :]) + params[5][level])[:, None, :]
    )
    node_pre2 = project(swish_act(node_pre1), params[6][level]) + params[7][level]
    update = state + swish_act(node_pre2)
    center, variance = norm_stats(update, node_total)
    inverse = lax.rsqrt(variance + EPSILON)
    normed = (update - center) * inverse
    kept = (
        state,
        state_ext,
        field_ext,
        edge_pre1,
        edge_pre2,
        aggregate,
        node_pre1,
        node_pre2,
        normed,
        inverse,
    )
    return (kept, normed)


def backward_layer(level, upstream, kept, one_hot, slot_mask, pde_theta, params, node_total):
    (
        state,
        state_ext,
        field_ext,
        edge_pre1,
        edge_pre2,
        aggregate,
        node_pre1,
        node_pre2,
        normed,
        inverse,
    ) = kept
    row_count = state.shape[1]
    weight_edge1 = params[0][level]
    weight_node1 = params[4][level]
    grad_total, grad_cross = lax.psum(
        (jnp.sum(upstream, 1, keepdims=True), jnp.sum(upstream * normed, 1, keepdims=True)), "blk"
    )
    delta_update = (upstream - grad_total / node_total - normed * grad_cross / node_total) * inverse
    delta_node2 = delta_update * swish_slope(node_pre2)
    grad_node_w2 = outer_sum(swish_act(node_pre1), delta_node2)
    grad_node_b2 = jnp.sum(delta_node2, (0, 1))
    delta_node1 = project(delta_node2, params[6][level].T) * swish_slope(node_pre1)
    grad_node_w1 = jnp.concatenate(
        [
            outer_sum(state, delta_node1),
            outer_sum(aggregate, delta_node1),
            outer_sum(pde_theta, jnp.sum(delta_node1, 1)),
        ],
        0,
    )
    grad_node_b1 = jnp.sum(delta_node1, (0, 1))
    delta_state = delta_update + project(delta_node1, weight_node1[:D].T)
    delta_aggregate = project(delta_node1, weight_node1[D : 2 * D].T)
    delta_edge2 = (
        (slot_mask / K)[..., None] * delta_aggregate[:, :, None, :] * swish_slope(edge_pre2)
    )
    grad_edge_w2 = outer_sum(swish_act(edge_pre1), delta_edge2)
    grad_edge_b2 = jnp.sum(delta_edge2, (0, 1, 2))
    delta_edge1 = project(delta_edge2, params[2][level].T) * swish_slope(edge_pre1)
    delta_anchor = jnp.sum(delta_edge1, 2)
    delta_windows = jnp.einsum("tnks,tnkd->tnsd", one_hot, delta_edge1, precision=PRECISE)
    delta_remote = jnp.zeros(state_ext.shape, jnp.float32)
    place_grad = jnp.zeros((state.shape[2],), jnp.float32)
    for index, shift in enumerate(offset_table()):
        piece = delta_windows[:, :, index]
        delta_remote = delta_remote + jnp.pad(piece, ((0, 0), (HALO + shift, HALO - shift), (0, 0)))
        place_grad = place_grad - shift / HALO * jnp.sum(piece, (0, 1))
    grad_edge_w1 = jnp.concatenate(
        [
            outer_sum(state, delta_anchor),
            outer_sum(state_ext, delta_remote),
            outer_sum(field_ext[:, HALO : HALO + row_count], delta_anchor)
            - outer_sum(field_ext, delta_remote),
            place_grad[None, :],
            outer_sum(pde_theta, jnp.sum(delta_anchor, 1)),
        ],
        0,
    )
    grad_edge_b1 = jnp.sum(delta_anchor, (0, 1))
    delta_state = delta_state + project(delta_anchor, weight_edge1[:D].T)
    delta_ext = project(delta_remote, weight_edge1[D : 2 * D].T)
    delta_state = delta_state + delta_ext[:, HALO : HALO + row_count]
    rim_grads = jnp.concatenate([delta_ext[:, :HALO], delta_ext[:, HALO + row_count :]], 1)
    returned = padded(rim_grads, (("blk", 1),), HALO)
    delta_state = delta_state.at[:, :HALO].add(returned[:, :HALO])
    delta_state = delta_state.at[:, row_count - HALO :].add(returned[:, 3 * HALO :])
    layer_grads = (
        grad_edge_w1,
        grad_edge_b1,
        grad_edge_w2,
        grad_edge_b2,
        grad_node_w1,
        grad_node_b1,
        grad_node_w2,
        grad_node_b2,
    )
    return (delta_state, layer_grads)


def on_device(
    node_state,
    field_window,
    edge_offset,
    pde_id,
    pde_table,
    cotangent,
    edge_w1,
    edge_b1,
    edge_w2,
    edge_b2,
    node_w1,
    node_b1,
    node_w2,
    node_b2,
):
    params = (edge_w1, edge_b1, edge_w2, edge_b2, node_w1, node_b1, node_w2, node_b2)
    picks = (pde_id[:, None] == jnp.arange(NPDE, dtype=jnp.int32)[None, :]).astype(jnp.float32)
    pde_theta = project(picks, pde_table)
    shift_values = jnp.array(offset_table(), jnp.int32)
    one_hot = (edge_offset[..., None] == shift_values).astype(jnp.float32)
    slot_mask = (edge_offset != 0).astype(jnp.float32)
    node_total = float(node_state.shape[1] * lax.axis_size("blk"))
    state = node_state
    field_ext = None
    saved = []
    for level in range(LAYERS):
        if level == 0:
            joined = padded(jnp.concatenate([state, field_window], 2), (("blk", 1),), HALO)
            state_ext = joined[:, :, :D]
            field_ext = joined[:, :, D:]
        else:
            state_ext = padded(state, (("blk", 1),), HALO)
        kept, state = forward_layer(
            level, state, state_ext, field_ext, one_hot, slot_mask, pde_theta, params, node_total
        )
        saved.append(kept)
    upstream = cotangent
    gathered_grads = [None] * LAYERS
    for level in reversed(range(LAYERS)):
        upstream, layer_grads = backward_layer(
            level, upstream, saved[level], one_hot, slot_mask, pde_theta, params, node_total
        )
        gathered_grads[level] = layer_grads
    stacked = tuple(
        (
            jnp.stack([gathered_grads[level][index] for level in range(LAYERS)], 0)
            for index in range(8)
        )
    )
    stacked = lax.psum(stacked, ("graph", "blk"))
    return (
        state,
        upstream,
        stacked[0],
        stacked[1],
        stacked[2],
        stacked[3],
        stacked[4],
        stacked[5],
        stacked[6],
        stacked[7],
    )


def solution(mesh):
    return jax.shard_map(
        on_device,
        mesh=mesh,
        in_specs=(
            P("graph", "blk", None),
            P("graph", "blk", None),
            P("graph", "blk", None),
            P("graph"),
            P(),
            P("graph", "blk", None),
            P(),
            P(),
            P(),
            P(),
            P(),
            P(),
            P(),
            P(),
        ),
        out_specs=(
            P("graph", "blk", None),
            P("graph", "blk", None),
            P(),
            P(),
            P(),
            P(),
            P(),
            P(),
            P(),
            P(),
        ),
        check_vma=False,
    )
```

profile of v0, /device:TPU:0, one launch (start us, length us, event | category | flops | bytes accessed | tf_op | source)
XLA Modules:
  0.0 786.9 jit_solution(9073263026771022576)
XLA Ops:
  12.1 2.5 copy.140
  14.6 5.4 collective-permute-start.1
  36.3 2.4 copy.142
  40.2 3.9 fusion.108
  44.1 2.9 fusion.109
  47.1 4.2 convolution_subtract_fusion.1
  54.0 14.4 %add_multiply_fusion.3 = (f32[16,128,6,128]{3,2,1,0:T(8,128)}, f32[16,128,6,128]{3,2,1,0:T(8,128)}) fusion(f32[16,128,128]{2,1,0:T(8,128)S(1)} %fusion.73, f32[16,128,6,128]{3,1,0,2:T(8,128)S(1)} %fusion.62, s32[16,128,6]{2,1,0:T(8,128)S(1)} %copy-done.16, s32[6]{0:T(128)S(1)} %copy-done.85), kind=kOutput, calls=%fused_computation.31 | convolution fusion | flops 121184256 | bytes 19972120 | tf_op jit(solution)/shard_map/tnks,tnsd->tnkd/dot_general | solution.py:88
  68.4 8.3 %copy.182 = f32[16,128,6,128]{1,3,2,0:T(8,128)} copy(f32[16,128,6,128]{3,2,1,0:T(8,128)} %get-tuple-element.187) | data formatting | bytes 12582912 | tf_op jit(solution)/shard_map/mul | solution.py:35
  76.7 12.4 %fusion.89 = f32[16,128,6,128]{3,1,2,0:T(8,128)S(1)} fusion(f32[16,128,6,128]{1,3,2,0:T(8,128)} %copy.182, f32[2,128,128]{2,1,0:T(8,128)S(1)} %copy-done.59), kind=kOutput, calls=%fused_computation.170 | convolution fusion | flops 2415919104 | bytes 12648448 | tf_op jit(solution)/shard_map/dot_general | solution.py:44
  89.2 7.2 multiply_reduce_fusion.1
  97.5 2.3 fusion.144
  99.8 34.6 %psum.112 = f32[16,1,128]{2,0,1:T(8,128)S(1)} all-reduce(f32[16,1,128]{2,0,1:T(8,128)S(1)} %bitcast.423), channel_id=1, replica_groups=mesh['graph'=2,'blk'=16] {'blk'}, use_global_device_ids=true, to_apply=%region_2.0 | all-reduce | flops 2048 | bytes 16384 | tf_op jit(solution)/shard_map/psum | solution.py:58
  134.6 30.0 %psum.113 = f32[16,1,128]{2,0,1:T(8,128)S(1)} all-reduce(f32[16,1,128]{2,0,1:T(8,128)S(1)} %bitcast.421), channel_id=1, replica_groups=mesh['graph'=2,'blk'=16] {'blk'}, use_global_device_ids=true, to_apply=%region_4.0 | all-reduce | flops 2048 | bytes 16384 | tf_op jit(solution)/shard_map/psum | solution.py:60
  164.8 4.4 collective-permute-start.3
  169.2 2.2 fusion.60
  173.5 2.3 convolution_subtract_fusion
  177.5 14.6 %add_multiply_fusion.2 = (f32[16,128,6,128]{3,2,1,0:T(8,128)}, f32[16,128,6,128]{3,2,1,0:T(8,128)}) fusion(f32[16,128,128]{2,1,0:T(8,128)S(1)} %fusion.60, f32[16,128,6,128]{3,1,0,2:T(8,128)S(1)} %fusion.49, s32[16,128,6]{2,1,0:T(8,128)S(1)} %copy-done.17, s32[6]{0:T(128)S(1)} %copy-done.85), kind=kOutput, calls=%fused_computation.30 | convolution fusion | flops 121184256 | bytes 19972120 | tf_op jit(solution)/shard_map/tnks,tnsd->tnkd/dot_general | solution.py:88
  192.1 8.3 %copy.184 = f32[16,128,6,128]{1,3,2,0:T(8,128)} copy(f32[16,128,6,128]{3,2,1,0:T(8,128)} %get-tuple-element.190) | data formatting | bytes 12582912 | tf_op jit(solution)/shard_map/mul | solution.py:35
  200.3 12.4 %fusion.92 = f32[16,128,6,128]{3,1,2,0:T(8,128)S(1)} fusion(f32[16,128,6,128]{1,3,2,0:T(8,128)} %copy.184, f32[2,128,128]{2,1,0:T(8,128)S(1)} %copy-done.59), kind=kOutput, calls=%fused_computation.173 | convolution fusion | flops 2415919104 | bytes 12648448 | tf_op jit(solution)/shard_map/dot_general | solution.py:44
  212.8 6.8 multiply_reduce_fusion
  220.7 2.6 fusion.142
  223.3 31.8 %psum.114 = f32[16,1,128]{2,0,1:T(8,128)S(1)} all-reduce(f32[16,1,128]{2,0,1:T(8,128)S(1)} %bitcast.424), channel_id=1, replica_groups=mesh['graph'=2,'blk'=16] {'blk'}, use_global_device_ids=true, to_apply=%region_7.0 | all-reduce | flops 2048 | bytes 16384 | tf_op jit(solution)/shard_map/psum | solution.py:58
  256.4 30.0 %psum.115 = f32[16,1,128]{2,0,1:T(8,128)S(1)} all-reduce(f32[16,1,128]{2,0,1:T(8,128)S(1)} %bitcast.422), channel_id=1, replica_groups=mesh['graph'=2,'blk'=16] {'blk'}, use_global_device_ids=true, to_apply=%region_9.0 | all-reduce | flops 2048 | bytes 16384 | tf_op jit(solution)/shard_map/psum | solution.py:60
  286.5 2.8 fusion.137
  289.3 58.0 %all-reduce.15 = (f32[16,128]{1,0:T(8,128)S(1)}, f32[16,1,128]{2,0,1:T(8,128)S(1)}) all-reduce(f32[16,128]{1,0:T(8,128)S(1)} %get-tuple-element.101, f32[16,1,128]{2,0,1:T(8,128)S(1)} %bitcast.419), channel_id=1, replica_groups=mesh['graph'=2,'blk'=16] {'blk'}, use_global_device_ids=true, to_apply=%region_13.0 | all-reduce | flops 4096 | bytes 32768 | tf_op jit(solution)/shard_map/psum | solution.py:135
  347.3 3.0 fusion.139
  350.3 3.8 convolution_bitcast_fusion
  357.8 2.5 convolution_bitcast_fusion.3
  360.3 2.0 convolution_add_fusion.3
  363.4 7.3 fusion.141
  370.7 7.3 fusion.40
  378.1 5.5 fusion.26
  383.6 11.5 %fusion.133 = (f32[128]{0:T(128)}, f32[16,128]{1,0:T(8,128)S(1)}, f32[16,128,128]{2,1,0:T(8,128)S(1)}, f32[16,128,6,128]{3,2,1,0:T(8,128)S(1)}) fusion(f32[16,128,6,128]{3,2,1,0:T(8,128)} %get-tuple-element.191, f32[16,128,128]{2,1,0:T(8,128)S(1)} %copy-done.36, f32[16,128,6,128]{3,1,2,0:T(8,128)S(1)} %fusion.26), kind=kLoop, calls=%fused_computation.253 | loop fusion | flops 18610048 | bytes 20980224 | tf_op jit(solution)/shard_map/reduce_sum | solution.py:179
  396.5 2.5 convolution_bitcast_fusion.7
  399.8 9.5 %fusion.2 = f32[16,128,6,128]{3,2,1,0:T(8,128)} fusion(f32[16,128,6,128]{3,2,1,0:T(8,128)S(1)} %get-tuple-element.123, s32[16,128,6]{2,1,0:T(8,128)S(1)} %copy-done.18, s32[6]{0:T(128)S(1)} %copy-done.86), kind=kOutput, calls=%fused_computation.2 | convolution fusion | flops 113319936 | bytes 12632088 | tf_op jit(solution)/shard_map/tnks,tnkd->tnsd/dot_general | solution.py:161
  409.3 24.8 %slice_reduce_fusion.1 = (f32[128]{0:T(128)}, f32[16,128,1,128]{3,2,1,0:T(1,128)}, f32[16,128,1,128]{3,2,1,0:T(1,128)}, f32[16,128,1,128]{3,2,1,0:T(1,128)}, f32...) fusion(f32[16,128,6,128]{3,2,1,0:T(8,128)} %fusion.2), kind=kLoop, calls=%fused_computation.251 | loop fusion | flops 262016 | bytes 12583424 | tf_op jit(solution)/shard_map/reduce_sum | solution.py:167
  434.1 2.4 reduce_sum.352
  437.3 2.1 reduce_sum.349
  439.4 2.1 reduce_sum.350
  441.5 2.1 reduce_sum.351
  443.7 3.5 pad_add_fusion.1
  450.5 2.3 fusion.37
  453.9 2.6 convolution_bitcast_fusion.6
  457.2 3.0 concatenate.33
  463.7 61.8 %all-reduce.14 = (f32[16,128]{1,0:T(8,128)S(1)}, f32[16,1,128]{2,0,1:T(8,128)S(1)}) all-reduce(f32[16,128]{1,0:T(8,128)S(1)} %get-tuple-element.99, f32[16,1,128]{2,0,1:T(8,128)S(1)} %bitcast.420), channel_id=1, replica_groups=mesh['graph'=2,'blk'=16] {'blk'}, use_global_device_ids=true, to_apply=%region_18.0 | all-reduce | flops 4096 | bytes 32768 | tf_op jit(solution)/shard_map/psum | solution.py:135
  525.5 2.9 fusion.138
  528.3 3.8 convolution_bitcast_fusion.1
  536.1 2.5 convolution_bitcast_fusion.4
  538.6 2.5 convolution_bitcast_fusion.5
  542.1 7.3 fusion.140
  549.5 7.3 fusion.43
  556.8 5.7 fusion.22
  562.6 11.5 %fusion.132 = (f32[128]{0:T(128)}, f32[16,128]{1,0:T(8,128)S(1)}, f32[16,128,128]{2,1,0:T(8,128)S(1)}, f32[16,128,6,128]{3,2,1,0:T(8,128)S(1)}) fusion(f32[16,128,6,128]{3,2,1,0:T(8,128)} %get-tuple-element.188, f32[16,128,128]{2,1,0:T(8,128)S(1)} %copy-done.34, f32[16,128,6,128]{3,1,2,0:T(8,128)S(1)} %fusion.22), kind=kLoop, calls=%fused_computation.252 | loop fusion | flops 18610048 | bytes 20980224 | tf_op jit(solution)/shard_map/reduce_sum | solution.py:179
  574.8 2.5 convolution_bitcast_fusion.9
  577.3 9.5 %fusion = f32[16,128,6,128]{3,2,1,0:T(8,128)} fusion(f32[16,128,6,128]{3,2,1,0:T(8,128)S(1)} %get-tuple-element.122, s32[16,128,6]{2,1,0:T(8,128)S(1)} %copy-done.19, s32[6]{0:T(128)S(1)} %copy-done.87), kind=kOutput, calls=%fused_computation | convolution fusion | flops 113319936 | bytes 12632088 | tf_op jit(solution)/shard_map/tnks,tnkd->tnsd/dot_general | solution.py:161
  586.8 24.6 %slice_reduce_fusion = (f32[128]{0:T(128)}, f32[16,128,1,128]{3,2,1,0:T(1,128)S(1)}, f32[16,128,1,128]{3,2,1,0:T(1,128)}, f32[16,128,1,128]{3,2,1,0:T(1,128)}, f...) fusion(f32[16,128,6,128]{3,2,1,0:T(8,128)} %fusion), kind=kLoop, calls=%fused_computation.250 | loop fusion | flops 262016 | bytes 12583424 | tf_op jit(solution)/shard_map/reduce_sum | solution.py:167
  612.5 3.8 pad_add_fusion
  616.3 2.8 convolution_bitcast_fusion.8
  619.1 2.1 fusion.159
  623.0 2.1 reduce_sum.340
  627.1 2.1 reduce_sum.342
  633.1 2.6 fusion.36
  642.4 38.7 %all-reduce.12 = (f32[2,128]{1,0:T(2,128)}, f32[2,128]{1,0:T(2,128)}, f32[2,128]{1,0:T(2,128)}, f32[2,128]{1,0:T(2,128)}) all-reduce(f32[2,128]{1,0:T(2,128)S(1)} %get-tuple-element.197, f32[2,128]{1,0:T(2,128)S(1)} %get-tuple-element.198, f32[2,128]{1,0:T(2,128)S(1)} %get-tuple-element.199, ...), channel_id=1, replica_groups=mesh['graph'=2,'blk'=16] {'graph','blk'}, use_global_device_ids=true, to_apply=%region_37.38 | all-reduce | flops 1024 | bytes 8192 | tf_op jit(solution)/shard_map/psum | solution.py:250
  681.5 91.5 %all-reduce.18.cloned.1.call-done = (f32[2,285,128]{2,1,0:T(8,128)}, f32[2,128,128]{2,1,0:T(8,128)}, f32[2,259,128]{2,1,0:T(8,128)}, f32[2,128,128]{2,1,0:T(8,128)}) async-done(((f32[2,285,128]{2,1,0:T(8,128)}, f32[2,128,128]{2,1,0:T(8,128)}, f32[2,259,128]{2,1,0:T(8,128)}, f32[2,128,128]{2,1,0:T(8,128)}), (f32[2,285,128]{2,1,0:T(8,128)}, f32[2,128,128]{2,1,0:T(8,128)}, f32[2,259,128]{2,1,0:T(8,128)}, ...) | async-done | bytes 819216 | tf_op jit(solution)/shard_map/psum | solution.py:250
  (377 shorter events, 76.4 us)
Async XLA Ops:
  7.2 20.4 %copy-start = (f32[8,3]{0,1:T(4,128)S(1)}, f32[8,3]{0,1:T(4,128)}, u32[]{:S(2)}) copy-start(f32[8,3]{0,1:T(4,128)} %param.27) | copy-start | bytes 292
  7.2 18.5 %copy-start.4 = (f32[16,128,128]{2,1,0:T(8,128)S(1)}, f32[16,128,128]{2,1,0:T(8,128)}, u32[]{:S(2)}) copy-start(f32[16,128,128]{2,1,0:T(8,128)} %param.23) | copy-start | bytes 3145732
  7.2 14.8 %copy-start.62 = (f32[2,285,128]{2,0,1:T(2,128)S(1)}, f32[2,285,128]{2,0,1:T(2,128)}, u32[]{:S(2)}) copy-start(f32[2,285,128]{2,0,1:T(2,128)} %param.29) | copy-start | bytes 875524
  7.2 16.1 %copy-start.63 = (f32[2,259,128]{2,0,1:T(2,128)S(1)}, f32[2,259,128]{2,0,1:T(2,128)}, u32[]{:S(2)}) copy-start(f32[2,259,128]{2,0,1:T(2,128)} %param.33) | copy-start | bytes 795652
  7.2 17.8 %copy-start.111 = (f32[2,128]{1,0:T(2,128)S(1)}, f32[2,128]{1,0:T(2,128)}, u32[]{:S(2)}) copy-start(f32[2,128]{1,0:T(2,128)} %param.30) | copy-start | bytes 3076
  7.2 17.8 %copy-start.112 = (f32[2,128]{1,0:T(2,128)S(1)}, f32[2,128]{1,0:T(2,128)}, u32[]{:S(2)}) copy-start(f32[2,128]{1,0:T(2,128)} %param.32) | copy-start | bytes 3076
  7.2 18.4 %copy-start.113 = (f32[2,128]{1,0:T(2,128)S(1)}, f32[2,128]{1,0:T(2,128)}, u32[]{:S(2)}) copy-start(f32[2,128]{1,0:T(2,128)} %param.34) | copy-start | bytes 3076
  7.3 18.4 %copy-start.72 = (s32[16,128,6]{1,0,2:T(8,128)S(1)}, s32[16,128,6]{1,0,2:T(8,128)}, u32[]{:S(2)}) copy-start(s32[16,128,6]{1,0,2:T(8,128)} %param.25) | copy-start | bytes 147460
  7.3 20.3 %copy-start.121 = (s32[16]{0:T(128)S(1)}, s32[16]{0:T(128)}, u32[]{:S(2)}) copy-start(s32[16]{0:T(128)} %param.26) | copy-start | bytes 196
  7.3 23.1 %copy-start.114 = (f32[2,128]{1,0:T(2,128)S(1)}, f32[2,128]{1,0:T(2,128)}, u32[]{:S(2)}) copy-start(f32[2,128]{1,0:T(2,128)} %param.36) | copy-start | bytes 3076
  7.3 765.7 %all-reduce.18.cloned.1.call-start = ((), (), s32[]{:S(2)}) async-start(), calls=%async_computation | async-start | bytes 1654784 | tf_op jit(solution)/shard_map/psum | solution.py:250
  8.4 23.8 %copy-start.30 = (f32[16,128,25]{1,2,0:T(8,128)}, f32[16,128,25]{1,2,0:T(8,128)S(1)}, u32[]{:S(2)}) copy-start(f32[16,128,25]{1,2,0:T(8,128)S(1)} %copy.138) | copy-start | bytes 614404
  10.1 36.9 %copy-start.5 = (f32[16,128,128]{1,2,0:T(8,128)}, f32[16,128,128]{1,2,0:T(8,128)S(1)}, u32[]{:S(2)}) copy-start(f32[16,128,128]{1,2,0:T(8,128)S(1)} %copy.137) | copy-start | bytes 3145732
  14.6 21.7 %collective-permute-start.1 = (f32[16,3,153]{2,0,1:T(8,128)}, f32[16,3,153]{2,0,1:T(8,128)}, u32[]{:S(2)}, u32[]{:S(2)}) collective-permute-start(f32[16,3,153]{2,0,1:T(8,128)} %copy.140), channel_id=1, source_target_pairs={{1,0},{2,1},{3,2},{4,3},{5,4},{6,5},{7,6},{8,7},{9,8},{10,9},{11,1... | collective-permute-start | bytes 88136 | tf_op jit(solution)/shard_map/ppermute | solution.py:27
  22.0 13.0 %collective-permute-start = (f32[16,3,153]{2,0,1:T(8,128)S(1)}, f32[16,3,153]{2,0,1:T(8,128)}, u32[]{:S(2)}, u32[]{:S(2)}) collective-permute-start(f32[16,3,153]{2,0,1:T(8,128)S(1)} %copy.139), channel_id=1, source_target_pairs={{0,1},{1,2},{2,3},{3,4},{4,5},{5,6},{6,7},{7,8},{8,9},{9,10},{10,1... | collective-permute-start | bytes 88136 | tf_op jit(solution)/shard_map/ppermute | solution.py:25
  24.2 10.8 %copy-start.50 = (f32[1,128,128]{2,0,1:T(1,128)}, f32[1,128,128]{2,0,1:T(1,128)S(1)}, u32[]{:S(2)}) copy-start(f32[1,128,128]{2,0,1:T(1,128)S(1)} %get-tuple-element.178) | copy-start | bytes 196612
  25.1 22.0 %copy-start.48 = (f32[1,128,128]{2,0,1:T(1,128)}, f32[1,128,128]{2,0,1:T(1,128)S(1)}, u32[]{:S(2)}) copy-start(f32[1,128,128]{2,0,1:T(1,128)S(1)} %get-tuple-element.156) | copy-start | bytes 196612
  25.1 26.3 %copy-start.46 = (f32[1,128,128]{2,0,1:T(1,128)}, f32[1,128,128]{2,0,1:T(1,128)S(1)}, u32[]{:S(2)}) copy-start(f32[1,128,128]{2,0,1:T(1,128)S(1)} %get-tuple-element.157) | copy-start | bytes 196612
  36.3 15.0 %copy-start.7 = (f32[16,3,153]{1,2,0:T(8,128)}, f32[16,3,153]{1,2,0:T(8,128)S(1)}, u32[]{:S(2)}) copy-start(f32[16,3,153]{1,2,0:T(8,128)S(1)} %copy.141) | copy-start | bytes 88132
  38.7 12.6 %copy-start.80 = (f32[16,128]{1,0:T(8,128)S(1)}, f32[16,128]{1,0:T(8,128)}, u32[]{:S(2)}) copy-start(f32[16,128]{1,0:T(8,128)} %convolution_add_fusion.11) | copy-start | bytes 24580
  40.2 12.2 %copy-start.109 = (f32[128]{0:T(128)S(1)}, f32[128]{0:T(128)}, u32[]{:S(2)}) copy-start(f32[128]{0:T(128)} %get-tuple-element.170) | copy-start | bytes 1540
  76.7 12.5 %copy-start.24 = (f32[16,128,6]{2,1,0:T(8,128)S(1)}, f32[16,128,6]{2,1,0:T(8,128)}, u32[]{:S(2)}) copy-start(f32[16,128,6]{2,1,0:T(8,128)} %copy.151) | copy-start | bytes 147460
  76.7 12.5 %copy-start.82 = (f32[128]{0:T(128)S(1)}, f32[128]{0:T(128)}, u32[]{:S(2)}) copy-start(f32[128]{0:T(128)} %get-tuple-element.184) | copy-start | bytes 1540
  89.1 10.7 %copy-start.2 = (f32[16,128,6,128]{3,1,2,0:T(8,128)}, f32[16,128,6,128]{3,1,2,0:T(8,128)S(1)}, u32[]{:S(2)}) copy-start(f32[16,128,6,128]{3,1,2,0:T(8,128)S(1)} %fusion.89) | copy-start | bytes 18874372
  97.4 71.8 %copy-start.52 = (f32[1,128,128]{2,0,1:T(1,128)S(1)}, f32[1,128,128]{2,0,1:T(1,128)}, u32[]{:S(2)}) copy-start(f32[1,128,128]{2,0,1:T(1,128)} %get-tuple-element.155) | copy-start | bytes 196612
  97.5 71.8 %copy-start.78 = (f32[16,128]{1,0:T(8,128)S(1)}, f32[16,128]{1,0:T(8,128)}, u32[]{:S(2)}) copy-start(f32[16,128]{1,0:T(8,128)} %convolution_add_fusion.9) | copy-start | bytes 24580
  97.5 74.0 %copy-start.53 = (f32[1,128,128]{2,0,1:T(1,128)S(1)}, f32[1,128,128]{2,0,1:T(1,128)}, u32[]{:S(2)}) copy-start(f32[1,128,128]{2,0,1:T(1,128)} %get-tuple-element.176) | copy-start | bytes 196612
  99.8 76.9 %copy-start.11 = (f32[16,128,128]{2,1,0:T(8,128)}, f32[16,128,128]{2,1,0:T(8,128)S(1)}, u32[]{:S(2)}) copy-start(f32[16,128,128]{2,1,0:T(8,128)S(1)} %get-tuple-element.130) | copy-start | bytes 3145732
  99.8 73.7 %copy-start.57 = (f32[1,128,128]{2,0,1:T(1,128)S(1)}, f32[1,128,128]{2,0,1:T(1,128)}, u32[]{:S(2)}) copy-start(f32[1,128,128]{2,0,1:T(1,128)} %get-tuple-element.158) | copy-start | bytes 196612
  134.4 42.3 %copy-start.71 = (f32[16,128]{1,0:T(8,128)}, f32[16,128]{1,0:T(8,128)S(1)}, u32[]{:S(2)}) copy-start(f32[16,128]{1,0:T(8,128)S(1)} %multiply_bitcast_fusion.3) | copy-start | bytes 24580
  164.6 12.1 %copy-start.69 = (f32[16,128]{1,0:T(8,128)}, f32[16,128]{1,0:T(8,128)S(1)}, u32[]{:S(2)}) copy-start(f32[16,128]{1,0:T(8,128)S(1)} %rsqrt_bitcast_fusion.1) | copy-start | bytes 24580
  164.6 12.1 %copy-start.103 = (f32[128]{0:T(128)S(1)}, f32[128]{0:T(128)}, u32[]{:S(2)}) copy-start(f32[128]{0:T(128)} %get-tuple-element.165) | copy-start | bytes 1540
  164.7 8.7 %collective-permute-start.2 = (f32[16,3,128]{2,1,0:T(4,128)S(1)}, f32[16,3,128]{2,1,0:T(4,128)S(1)}, u32[]{:S(2)}, u32[]{:S(2)}) collective-permute-start(f32[16,3,128]{2,1,0:T(4,128)S(1)} %get-tuple-element.151), channel_id=1, source_target_pairs={{0,1},{1,2},{2,3},{3,4},{4,5},{5,6},{6,7},{7,8},{8,9},{9,10},{10,1... | collective-permute-start | bytes 73736 | tf_op jit(solution)/shard_map/ppermute | solution.py:25
  164.8 8.6 %collective-permute-start.3 = (f32[16,3,128]{2,1,0:T(4,128)S(1)}, f32[16,3,128]{2,1,0:T(4,128)S(1)}, u32[]{:S(2)}, u32[]{:S(2)}) collective-permute-start(f32[16,3,128]{2,1,0:T(4,128)S(1)} %get-tuple-element.152), channel_id=1, source_target_pairs={{1,0},{2,1},{3,2},{4,3},{5,4},{6,5},{7,6},{8,7},{9,8},{10,9},{11,1... | collective-permute-start | bytes 73736 | tf_op jit(solution)/shard_map/ppermute | solution.py:27
  200.3 12.5 %copy-start.25 = (f32[16,128,6]{2,1,0:T(8,128)S(1)}, f32[16,128,6]{2,1,0:T(8,128)}, u32[]{:S(2)}) copy-start(f32[16,128,6]{2,1,0:T(8,128)} %copy.151) | copy-start | bytes 147460
  200.3 12.5 %copy-start.84 = (f32[128]{0:T(128)S(1)}, f32[128]{0:T(128)}, u32[]{:S(2)}) copy-start(f32[128]{0:T(128)} %get-tuple-element.183) | copy-start | bytes 1540
  212.8 10.5 %copy-start.3 = (f32[16,128,6,128]{3,1,2,0:T(8,128)}, f32[16,128,6,128]{3,1,2,0:T(8,128)S(1)}, u32[]{:S(2)}) copy-start(f32[16,128,6,128]{3,1,2,0:T(8,128)S(1)} %fusion.92) | copy-start | bytes 18874372
  383.6 11.6 %copy-start.40 = (f32[16,128,25]{1,0,2:T(8,128)S(1)}, f32[16,128,25]{1,0,2:T(8,128)}, u32[]{:S(2)}) copy-start(f32[16,128,25]{1,0,2:T(8,128)} %param.24) | copy-start | bytes 614404
  383.6 16.2 %copy-start.18 = (s32[16,128,6]{2,1,0:T(8,128)S(1)}, s32[16,128,6]{2,1,0:T(8,128)}, u32[]{:S(2)}) copy-start(s32[16,128,6]{2,1,0:T(8,128)} %copy.144) | copy-start | bytes 147460
  383.6 16.2 %copy-start.86 = (s32[6]{0:T(128)S(1)}, s32[6]{0:T(128)}, u32[]{:S(2)}) copy-start(s32[6]{0:T(128)} %constant.136.clone) | copy-start | bytes 76
  437.3 10.9 %copy-start.14 = (f32[16,134,25]{1,2,0:T(8,128)S(1)}, f32[16,134,25]{1,2,0:T(8,128)}, u32[]{:S(2)}) copy-start(f32[16,134,25]{1,2,0:T(8,128)} %copy-done.13) | copy-start | bytes 643204
  437.3 10.9 %copy-start.77 = (f32[25,128]{1,0:T(8,128)S(1)}, f32[25,128]{1,0:T(8,128)}, u32[]{:S(2)}) copy-start(f32[25,128]{1,0:T(8,128)} %convolution_bitcast_fusion.12) | copy-start | bytes 38404
  443.6 9.8 %copy-start.97 = (f32[128]{0:T(128)S(1)}, f32[128]{0:T(128)}, u32[]{:S(2)}) copy-start(f32[128]{0:T(128)} %reduce_sum.350) | copy-start | bytes 1540
  443.7 10.3 %copy-start.74 = (f32[16,3,128]{2,1,0:T(4,128)S(1)}, f32[16,3,128]{2,1,0:T(4,128)}, u32[]{:S(2)}) copy-start(f32[16,3,128]{2,1,0:T(4,128)} %copy-done.73) | copy-start | bytes 73732
  443.7 10.3 %copy-start.76 = (f32[16,3,128]{2,1,0:T(4,128)S(1)}, f32[16,3,128]{2,1,0:T(4,128)}, u32[]{:S(2)}) copy-start(f32[16,3,128]{2,1,0:T(4,128)} %copy-done.75) | copy-start | bytes 73732
  452.8 8.4 %collective-permute-start.5 = (f32[16,3,128]{2,1,0:T(4,128)}, f32[16,3,128]{2,1,0:T(4,128)}, u32[]{:S(2)}, u32[]{:S(2)}) collective-permute-start(f32[16,3,128]{2,1,0:T(4,128)} %get-tuple-element.149), channel_id=1, source_target_pairs={{1,0},{2,1},{3,2},{4,3},{5,4},{6,5},{7,6},{8,7},{9,8},{10,9},{11,1... | collective-permute-start | bytes 73736 | tf_op jit(solution)/shard_map/ppermute | solution.py:27
  452.9 7.4 collective-permute-start.4
  532.2 9.9 %slice-start.4 = ((s8[6291456]{0:T(1024)(128)(4,1)}), s8[4194304]{0:T(1024)(128)(4,1)S(1)}, s32[]{:S(2)}) async-start(s8[6291456]{0:T(1024)(128)(4,1)} %bitcast.375), calls=%async_computation.5 | async-start | bytes 8388608
  538.6 10.9 %slice-start = ((s8[6291456]{0:T(1024)(128)(4,1)}), s8[4194304]{0:T(1024)(128)(4,1)S(1)}, s32[]{:S(2)}) async-start(s8[6291456]{0:T(1024)(128)(4,1)} %bitcast.371), calls=%async_computation.1 | async-start | bytes 8388608
  562.5 14.7 %copy-start.19 = (s32[16,128,6]{2,1,0:T(8,128)S(1)}, s32[16,128,6]{2,1,0:T(8,128)}, u32[]{:S(2)}) copy-start(s32[16,128,6]{2,1,0:T(8,128)} %copy.144) | copy-start | bytes 147460
  562.6 14.7 %copy-start.87 = (s32[6]{0:T(128)S(1)}, s32[6]{0:T(128)}, u32[]{:S(2)}) copy-start(s32[6]{0:T(128)} %constant.136.clone) | copy-start | bytes 76
  616.3 14.9 %copy-start.15 = (f32[16,134,25]{1,2,0:T(8,128)S(1)}, f32[16,134,25]{1,2,0:T(8,128)}, u32[]{:S(2)}) copy-start(f32[16,134,25]{1,2,0:T(8,128)} %copy-done.13) | copy-start | bytes 643204
  616.3 16.8 %copy-start.47 = (f32[1,128,128]{2,0,1:T(1,128)S(1)}, f32[1,128,128]{2,0,1:T(1,128)}, u32[]{:S(2)}) copy-start(f32[1,128,128]{2,0,1:T(1,128)} %copy-done.46) | copy-start | bytes 196612
  619.1 17.2 %copy-start.67 = (f32[128,128]{1,0:T(8,128)S(1)}, f32[128,128]{1,0:T(8,128)}, u32[]{:S(2)}) copy-start(f32[128,128]{1,0:T(8,128)} %convolution_bitcast_fusion.4) | copy-start | bytes 196612
  619.1 17.2 %copy-start.68 = (f32[128,128]{1,0:T(8,128)S(1)}, f32[128,128]{1,0:T(8,128)}, u32[]{:S(2)}) copy-start(f32[128,128]{1,0:T(8,128)} %convolution_bitcast_fusion.5) | copy-start | bytes 196612
  621.2 15.1 %copy-start.58 = (f32[1,259,128]{2,1,0:T(8,128)S(1)}, f32[1,259,128]{2,1,0:T(8,128)}, u32[]{:S(2)}) copy-start(f32[1,259,128]{2,1,0:T(8,128)} %maximum_bitcast_fusion.1) | copy-start | bytes 397828
  621.4 18.6 %copy-start.64 = (f32[1,128,128]{2,1,0:T(8,128)S(1)}, f32[1,128,128]{2,1,0:T(8,128)}, u32[]{:S(2)}) copy-start(f32[1,128,128]{2,1,0:T(8,128)} %fusion.40) | copy-start | bytes 196612
  621.4 18.6 %copy-start.65 = (f32[1,128,128]{2,1,0:T(8,128)S(1)}, f32[1,128,128]{2,1,0:T(8,128)}, u32[]{:S(2)}) copy-start(f32[1,128,128]{2,1,0:T(8,128)} %fusion.43) | copy-start | bytes 196612
  623.0 18.7 %copy-start.88 = (f32[128]{0:T(128)S(1)}, f32[128]{0:T(128)}, u32[]{:S(2)}) copy-start(f32[128]{0:T(128)} %get-tuple-element.91) | copy-start | bytes 1540
  623.0 18.7 %copy-start.89 = (f32[128]{0:T(128)S(1)}, f32[128]{0:T(128)}, u32[]{:S(2)}) copy-start(f32[128]{0:T(128)} %get-tuple-element.88) | copy-start | bytes 1540
  627.1 152.8 %copy-start.1 = (f32[8,3]{0,1:T(4,128)S(1)}, f32[8,3]{0,1:T(4,128)}, u32[]{:S(2)}) copy-start(f32[8,3]{0,1:T(4,128)} %param.27) | copy-start | bytes 292
  635.7 45.5 %collective-permute-start.7 = (f32[16,3,128]{2,1,0:T(4,128)S(1)}, f32[16,3,128]{2,1,0:T(4,128)S(1)}, u32[]{:S(2)}, u32[]{:S(2)}) collective-permute-start(f32[16,3,128]{2,1,0:T(4,128)S(1)} %get-tuple-element.147), channel_id=1, source_target_pairs={{1,0},{2,1},{3,2},{4,3},{5,4},{6,5},{7,6},{8,7},{9,8},{10,9},{11,1... | collective-permute-start | bytes 73736 | tf_op jit(solution)/shard_map/ppermute | solution.py:27
  635.8 45.3 %collective-permute-start.6 = (f32[16,3,128]{2,1,0:T(4,128)S(1)}, f32[16,3,128]{2,1,0:T(4,128)S(1)}, u32[]{:S(2)}, u32[]{:S(2)}) collective-permute-start(f32[16,3,128]{2,1,0:T(4,128)S(1)} %get-tuple-element.148), channel_id=1, source_target_pairs={{0,1},{1,2},{2,3},{3,4},{4,5},{5,6},{6,7},{7,8},{8,9},{9,10},{10,1... | collective-permute-start | bytes 73736 | tf_op jit(solution)/shard_map/ppermute | solution.py:25
  681.5 98.4 %copy-start.41 = (f32[16,128,128]{2,1,0:T(8,128)}, f32[16,128,128]{2,1,0:T(8,128)S(1)}, u32[]{:S(2)}) copy-start(f32[16,128,128]{2,1,0:T(8,128)S(1)} %scatter-add.19) | copy-start | bytes 3145732
  (75 other events, 457.2 us)
Sparse Core Ops, SparseCore 0:
  642.5 130.4 all-reduce.17
where the time goes:
time: 799 us; the launch traced here: 787 us
  blocking collectives  285 us (36%)
  matrix products  180 us (23%)
  other arithmetic  154 us (19%)
  waiting for transfers between devices  91.6 us (11%)
  local copies, waits for them, and re-layouts  49.9 us (6%)
  between operations  16 us (2%)
  starting transfers between devices  11.1 us (1%)
    psum x2, blocking collectives, backward_layer(): lax.psum((jnp.sum(upstream, 1, keepdims=True), jnp.sum(upstream * normed,...  120 us
    psum x1, waiting for transfers between devices, on_device(): stacked = lax.psum(stacked, ('graph', 'blk'))  91.5 us
    dot_general x31, matrix products, project(): return jnp.dot(left, right, precision=PRECISE)  83.8 us
    reduce_sum x12, other arithmetic, backward_layer(): place_grad = place_grad - shift / HALO * jnp.sum(piece, (0, 1))  68.7 us
    psum x2, blocking collectives, norm_stats(): center = lax.psum(jnp.sum(update, 1, keepdims=True), 'blk') / node_total  66.4 us
    psum x2, blocking collectives, norm_stats(): lax.psum(jnp.sum(centred * centred, 1, keepdims=True), 'blk') / node_total  60 us
    dot_general x20, matrix products, outer_sum(): return jnp.dot(flat_left.T, flat_right, precision=PRECISE)  47.8 us
    psum x1, blocking collectives, on_device(): stacked = lax.psum(stacked, ('graph', 'blk'))  38.7 us
  transfers between devices with their start and end apart: 9, of which 1 were waited for; matrix products, arithmetic and copies ran while one was open for 4% of the time, Pallas kernels for 0%

commit v1 on v0

v1 whole, which is shorter than its diff:
```python
import functools

import jax
import jax.numpy as jnp
from jax import lax
from jax.experimental import pallas as pl
from jax.experimental.pallas import tpu as pltpu
from jax.sharding import PartitionSpec as P

D = 128
TW = 25
NPAR = 3
K = 6
HALO = 3
NPDE = 8
LAYERS = 2
EDGE_IN = 2 * D + TW + 1 + NPAR
NODE_IN = 2 * D + NPAR
OFFSETS = tuple(o for o in range(-HALO, HALO + 1) if o != 0)

EPSILON = 1e-05
RIM = 8
GROUPS = 2
AUX = 32
A_THETA = TW
A_ONE = TW + NPAR
A_PLACE = TW + NPAR + 1
UNIT_AUX = 3 * D
UNIT_BIAS = UNIT_AUX + AUX
UNIT_ROWS = UNIT_BIAS + 8

F32 = jnp.float32
BF16 = jnp.bfloat16
MESH = pl.DeviceIdType.MESH


def dot(left, right):
    return jnp.dot(left, right, preferred_element_type=F32)


def dot_t(left, right):
    return lax.dot_general(left, right, (((0,), (0,)), ((), ())), preferred_element_type=F32)


def split(value):
    head = value.astype(BF16)
    tail = (value - head.astype(F32)).astype(BF16)
    return head, tail


def pair(value):
    head, tail = split(value)
    return jnp.concatenate([head, tail], 1)


def halves(product):
    return product[:, :D] + product[:, D:]


def doubled(weight):
    both = pair(weight)
    return jnp.concatenate([both, both], 0)


def swish_parts(half):
    t = jnp.tanh(half)
    u = 1.0 + t
    act = half * u
    return act, u + act * (1.0 - t)


def digit_stages(count, sizes=(4,)):
    stages, stride, step = [], 1, 0
    while stride < count:
        size = sizes[min(step, len(sizes) - 1)]
        while count // stride % size:
            size -= 1
        stages.append((stride, size))
        stride *= size
        step += 1
    return stages


class Links:
    def __init__(self, blk, graph):
        self.blk, self.graph = blk, graph
        self.me = lax.axis_index("blk")
        self.mine = lax.axis_index("graph")
        self.stat_stages = digit_stages(blk)
        self.sum_stages = []
        for position, (stride, size) in enumerate(digit_stages(blk, (2, 2, 4))):
            digits = [("blk", stride, size)]
            if position == 1:
                digits.append(("graph", 1, graph))
            self.sum_stages.append(digits)

    def ring(self, shift):
        return (self.mine, lax.rem(self.me + shift + self.blk, self.blk))

    def stat_peer(self, stage, shift):
        stride, size = self.stat_stages[stage]
        digit = lax.rem(self.me // stride, size)
        other = lax.rem(digit + shift, size)
        return (self.mine, self.me + (other - digit) * stride)

    def sum_size(self, stage):
        size = 1
        for _, _, count in self.sum_stages[stage]:
            size *= count
        return size

    def sum_digit(self, stage):
        value = 0
        for axis, stride, size in self.sum_stages[stage]:
            place = self.me if axis == "blk" else self.mine
            value = value * size + lax.rem(place // stride, size)
        return value

    def sum_peer(self, stage, shift):
        size = self.sum_size(stage)
        other = lax.rem(self.sum_digit(stage) + shift, size)
        coords = {"blk": self.me, "graph": self.mine}
        rest = other
        for axis, stride, count in reversed(self.sum_stages[stage]):
            place = coords[axis]
            now = lax.rem(place // stride, count)
            coords[axis] = place + (lax.rem(rest, count) - now) * stride
            rest = rest // count
        return (coords["graph"], coords["blk"]), other

    def greeted(self):
        peers = [self.ring(1), self.ring(-1)]
        for stage, (_, size) in enumerate(self.stat_stages):
            peers += [self.stat_peer(stage, shift) for shift in range(1, size)]
        for stage in range(len(self.sum_stages)):
            peers += [self.sum_peer(stage, shift)[0] for shift in range(1, self.sum_size(stage))]
        return peers


def remote(src, dst, send_sem, recv_sem, device):
    return pltpu.make_async_remote_copy(
        src_ref=src,
        dst_ref=dst,
        send_sem=send_sem,
        recv_sem=recv_sem,
        device_id=device,
        device_id_type=MESH,
    )


def kernel_body(
    blk,
    graph,
    state_in,
    field_in,
    offset_in,
    id_in,
    table_in,
    cot_in,
    ew1,
    eb1,
    ew2,
    eb2,
    nw1,
    nb1,
    nw2,
    nb2,
    state_out,
    dst,
    unit_all,
    w_in,
    w_e2,
    w_e2t,
    w_agg,
    w_n2,
    w_n2t,
    w_np,
    w_ep,
    w_aux,
    spread,
    counts,
    weigh,
    aux_t,
    xs,
    xa,
    a_buf,
    r_buf,
    n_buf,
    slope,
    agg2,
    hid2,
    sn1,
    sn2,
    upd,
    y0,
    yh,
    dag,
    e1,
    dxh,
    dxl,
    acc_n2,
    acc_agg,
    acc_nx,
    acc_e2,
    acc_x,
    acc_b,
    stat,
    stat_recv,
    fin,
    h0s,
    h0r,
    hs,
    hr,
    rs,
    rr,
    unit,
    unit_recv,
    stat_ssem,
    stat_rsem,
    rim_ssem,
    rim_rsem,
    sum_ssem,
    sum_rsem,
):
    traj, nodes, _ = state_in.shape
    per = traj // GROUPS
    chunk = min(4, per)
    ext = nodes + 2 * RIM
    total = float(nodes * blk)
    links = Links(blk, graph)
    stages = links.stat_stages

    barrier = pltpu.get_barrier_semaphore()
    greeted = links.greeted()
    for peer in greeted:
        pl.semaphore_signal(barrier, inc=1, device_id=peer, device_id_type=MESH)

    offs = [offset_in[pl.ds(k * traj, traj), :] for k in range(K)]
    for i, o in enumerate(OFFSETS):
        many = jnp.zeros((traj, nodes), F32)
        for k in range(K):
            many = many + jnp.where(offs[k] == o, 1.0, 0.0)
        counts[pl.ds(i * traj, traj), :] = many
    counts[pl.ds(K * traj, 2 * traj), :] = jnp.zeros((2 * traj, nodes), F32)
    rows = lax.broadcasted_iota(jnp.int32, (D, K * D), 0)
    cols = lax.broadcasted_iota(jnp.int32, (D, K * D), 1)
    spread[...] = jnp.where(rows == 3 * AUX + cols // D, 1.0, 0.0).astype(BF16)
    aux_t[...] = jnp.zeros_like(aux_t)
    place = lax.broadcasted_iota(jnp.int32, (1, nodes), 1).astype(F32) - nodes / 2

    def prepare(t, slot):
        tile = aux_t.at[slot]
        tile[pl.ds(0, TW), :] = field_in[pl.ds(t, TW, stride=traj), :]
        row = id_in[t]
        for q in range(NPAR):
            tile[pl.ds(A_THETA + q, 1), :] = jnp.full((1, nodes), table_in[q, row], F32)
        tile[pl.ds(A_ONE, 1), :] = jnp.ones((1, nodes), F32)
        tile[pl.ds(A_PLACE, 1), :] = place
        head, tail = split(tile[pl.ds(0, AUX), :])
        head, tail = head.astype(F32), tail.astype(F32)
        full = jnp.concatenate(
            [
                head,
                tail,
                head,
                counts[pl.ds(t, 8, stride=traj), :],
                jnp.zeros((D - 3 * AUX - 8, nodes), F32),
            ],
            0,
        )
        back = full.T
        h0s[0, 1, t] = back[:RIM]
        h0s[1, 1, t] = back[nodes - RIM :]
        h0s[0, 0, t] = state_in[t, pl.ds(0, RIM), :]
        h0s[1, 0, t] = state_in[t, pl.ds(nodes - RIM, RIM), :]
        low = back.astype(BF16)
        xa[t, pl.ds(0, nodes), :] = low
        return low

    def prepare_chunk(j, _):
        lows = [prepare(j * chunk + c, c) for c in range(chunk)]
        many = dot(jnp.concatenate(lows, 0), spread[...])
        for c in range(chunk):
            for i in range(K):
                weigh[j * chunk + c, pl.ds(i * nodes, nodes), :] = many[
                    c * nodes : (c + 1) * nodes, i * D : (i + 1) * D
                ]
        return 0

    lax.fori_loop(0, traj // chunk, prepare_chunk, 0)

    pl.semaphore_wait(barrier, len(greeted))

    def halo0(way):
        return remote(
            h0s.at[way],
            h0r.at[way],
            rim_ssem.at[0, way],
            rim_rsem.at[0, way],
            links.ring(1 if way else -1),
        )

    for way in range(2):
        halo0(way).start()

    e1[...] = jnp.zeros_like(e1)
    for l in range(LAYERS):
        w_self = ew1[pl.ds(0, D), l, :]
        w_far = ew1[pl.ds(D, D), l, :]
        n_self = nw1[pl.ds(0, D), l, :]
        n_agg = nw1[pl.ds(D, D), l, :]
        for i, w in enumerate((w_self, w_far, n_self)):
            head, tail = split(0.5 * w)
            cut = pl.ds(i * D, D)
            w_in[l, pl.ds(0, D), cut] = head
            w_in[l, pl.ds(D, D), cut] = head
            w_in[l, pl.ds(2 * D, D), cut] = tail
        w_field = 0.5 * ew1[pl.ds(2 * D, TW), l, :]
        w_place = (0.5 / HALO) * ew1[pl.ds(2 * D + TW, 1), l, :]
        w_theta = 0.5 * ew1[pl.ds(2 * D + TW + 1, NPAR), l, :]
        n_theta = 0.5 * nw1[pl.ds(2 * D, NPAR), l, :]
        w_aux[...] = jnp.zeros_like(w_aux)
        w_aux[pl.ds(0, TW), pl.ds(0, D)] = w_field
        w_aux[pl.ds(0, TW), pl.ds(D, D)] = -w_field
        w_aux[pl.ds(A_THETA, NPAR), pl.ds(0, D)] = w_theta
        w_aux[pl.ds(A_THETA, NPAR), pl.ds(2 * D, D)] = n_theta
        w_aux[pl.ds(A_ONE, 1), pl.ds(0, D)] = 0.5 * eb1[pl.ds(l, 1), :]
        w_aux[pl.ds(A_ONE, 1), pl.ds(2 * D, D)] = 0.5 * nb1[pl.ds(l, 1), :]
        w_aux[pl.ds(A_PLACE, 1), pl.ds(0, D)] = w_place
        w_aux[pl.ds(A_PLACE, 1), pl.ds(D, D)] = -w_place
        head, tail = split(w_aux[...])
        w_in[l, pl.ds(3 * D, AUX), :] = head
        w_in[l, pl.ds(3 * D + AUX, AUX), :] = head
        w_in[l, pl.ds(3 * D + 2 * AUX, AUX), :] = tail
        w_in[l, pl.ds(3 * D + 3 * AUX, AUX), :] = jnp.zeros((AUX, 3 * D), BF16)
        second = 0.5 * ew2[l]
        w_e2[l] = doubled(second)
        w_e2t[l] = doubled(second.T)
        w_agg[l] = doubled(0.5 * n_agg)
        w_n2[l] = doubled(0.5 * nw2[l])
        w_n2t[l] = doubled(nw2[l].T)
        head, tail = split(jnp.concatenate([n_self.T, 0.5 * n_agg.T], 1))
        w_np[l, pl.ds(0, D), :] = head
        w_np[l, pl.ds(D, D), :] = head
        w_np[l, pl.ds(2 * D, D), :] = tail
        w_ep[l, pl.ds(0, D), :] = pair(w_self.T)
        w_ep[l, pl.ds(D, D), :] = pair(w_far.T)

    def stat_copy(event, stage, shift):
        size = stages[stage][1]
        return remote(
            stat.at[event, stage],
            stat_recv.at[event, stage, shift - 1],
            stat_ssem.at[event, stage, shift - 1],
            stat_rsem.at[event, stage, shift - 1],
            links.stat_peer(stage, shift),
        )

    def stat_send(event, stage):
        for shift in range(1, stages[stage][1]):
            stat_copy(event, stage, shift).start()

    def stat_merge(event, stage):
        stride, size = stages[stage]
        for shift in range(1, size):
            stat_copy(event, stage, shift).wait_recv()
        parts = [stat.at[event, stage]] + [
            stat_recv.at[event, stage, shift - 1] for shift in range(1, size)
        ]

        def row(q):
            return [part[pl.ds(q * per, per), :] for part in parts]

        u, c = row(2), row(3)
        if event >= 4:
            return None, None, sum(u[1:], u[0]), sum(c[1:], c[0])
        m, m2 = row(0), row(1)
        mean = sum(m[1:], m[0]) * (1.0 / size)
        gaps = [value - mean for value in m]
        spread2 = sum((gap * gap for gap in gaps[1:]), gaps[0] * gaps[0])
        m2_all = sum(m2[1:], m2[0]) + spread2 * float(nodes * stride)
        u_all = sum(u[1:], u[0])
        c_all = sum(c[1:], c[0])
        for gap, value in zip(gaps, u):
            c_all = c_all + gap * value
        return mean, m2_all, u_all, c_all

    def stat_forward(event):
        for stage in range(1, len(stages)):
            merged = stat_merge(event, stage - 1)
            for q, value in enumerate(merged):
                if value is not None:
                    stat[event, stage, pl.ds(q * per, per), :] = value
            stat_send(event, stage)

    def stat_finish(event):
        mean, m2, u, c = stat_merge(event, len(stages) - 1)
        if event < 4:
            scale = lax.rsqrt(m2 * (1.0 / total) + EPSILON)
            fin[event, 0] = mean
            fin[event, 1] = scale
            fin[event, 2] = u * (1.0 / total)
            fin[event, 3] = scale * c * (1.0 / total)
        else:
            fin[event, 2] = u * (1.0 / total)
            fin[event, 3] = c * (1.0 / total)

    def rim_copy(kind, send, recv, way):
        return remote(
            send.at[way],
            recv.at[way],
            rim_ssem.at[kind, way],
            rim_rsem.at[kind, way],
            links.ring(1 if way else -1),
        )

    def rows_of(buf, l, t, c, start, size):
        return buf[l, pl.ds(t, c), pl.ds(start, size), :].reshape(c * size, buf.shape[-1])

    def forward(l, g, hook):
        base = g * per
        event = 2 * l + g
        if l == 0:
            if g == 0:
                for way in range(2):
                    halo0(way).wait_recv()
        else:
            stat_finish(g)
            for way in range(2):
                rim_copy(1 + g, hs.at[g], hr.at[g], way).wait_recv()
        lane = lax.broadcasted_iota(jnp.int32, (RIM, D), 1)
        moved = jnp.where((lane == A_PLACE) | (lane == 2 * AUX + A_PLACE), float(nodes), 0.0)

        def enter(j, _):
            for c in range(chunk):
                s = j * chunk + c
                t = base + s
                if l == 0:
                    xs[0, t, pl.ds(0, nodes), :] = pair(state_in[t])
                    near = jnp.concatenate([h0r[1, 0, t], h0r[0, 0, t]], 0)
                    xs[0, t, pl.ds(nodes, 2 * RIM), :] = pair(near)
                    side = jnp.concatenate([h0r[1, 1, t] - moved, h0r[0, 1, t] + moved], 0)
                    xa[t, pl.ds(nodes, 2 * RIM), :] = side.astype(BF16)
                else:
                    mean = fin[g, 0, pl.ds(s, 1), :]
                    scale = fin[g, 1, pl.ds(s, 1), :]
                    y = (upd[t] - mean) * scale
                    y0[t] = y
                    xs[1, t, pl.ds(0, nodes), :] = pair(y)
                    near = jnp.concatenate([hr[g, 1, s], hr[g, 0, s]], 0)
                    near = (near - mean) * scale
                    yh[t] = near
                    xs[1, t, pl.ds(nodes, 2 * RIM), :] = pair(near)
            t = base + j * chunk
            x = rows_of(xs, l, t, chunk, 0, ext)
            side = xa[pl.ds(t, chunk)].reshape(chunk * ext, D)
            p = dot(x, w_in[l, pl.ds(0, 2 * D), :])
            p = p + dot(jnp.concatenate([x[:, :D], side], 1), w_in[l, pl.ds(2 * D, 2 * D), :])
            for c in range(chunk):
                at = c * ext
                a_buf[l, t + c] = p[at : at + nodes, :D]
                r_buf[l, t + c, pl.ds(RIM, nodes), :] = p[at : at + nodes, D : 2 * D]
                r_buf[l, t + c, pl.ds(0, RIM), :] = p[at + nodes : at + nodes + RIM, D : 2 * D]
                r_buf[l, t + c, pl.ds(RIM + nodes, RIM), :] = p[
                    at + nodes + RIM : at + ext, D : 2 * D
                ]
                n_buf[j * chunk + c] = p[at : at + nodes, 2 * D :]
            return 0

        lax.fori_loop(0, per // chunk, enter, 0)

        bias2 = 0.5 * eb2[pl.ds(l, 1), :]

        def edge(t, s):
            hidden = []
            for o in OFFSETS:
                half = a_buf[l, t] + r_buf[l, t, pl.ds(RIM + o, nodes), :]
                hidden.append(pair(half * (1.0 + jnp.tanh(half))))
            p = dot(jnp.concatenate(hidden, 0), w_e2[l])
            summed = None
            for i in range(K):
                half = halves(p[i * nodes : (i + 1) * nodes]) + bias2
                tanh = jnp.tanh(half)
                scaled = weigh[t, pl.ds(i * nodes, nodes), :] * (1.0 + tanh)
                message = scaled * half
                summed = message if summed is None else summed + message
                slope[l, t, pl.ds(i * nodes, nodes), :] = scaled + message * (1.0 - tanh)
            dag[s] = summed * (1.0 / K)

        half_way = per // 4

        def edge_pair(j, _):
            for c in range(2):
                edge(base + 2 * j + c, 2 * j + c)
            return 0

        lax.fori_loop(0, half_way, edge_pair, 0)
        hook()
        lax.fori_loop(half_way, per // 2, edge_pair, 0)

        node2 = 0.5 * nb2[pl.ds(l, 1), :]

        def node(j, _):
            s = j * chunk
            t = base + s
            both = pair(dag[pl.ds(s, chunk)].reshape(chunk * nodes, D))
            agg2[l, pl.ds(t, chunk)] = both.reshape(chunk, nodes, 2 * D)
            half = n_buf[pl.ds(s, chunk)].reshape(chunk * nodes, D) + halves(dot(both, w_agg[l]))
            act, rise = swish_parts(half)
            sn1[l, pl.ds(t, chunk)] = (0.5 * rise).reshape(chunk, nodes, D)
            both = pair(act)
            hid2[l, pl.ds(t, chunk)] = both.reshape(chunk, nodes, 2 * D)
            half = halves(dot(both, w_n2[l])) + node2
            act, rise = swish_parts(half)
            sn2[l, pl.ds(t, chunk)] = (0.5 * rise).reshape(chunk, nodes, D)
            for c in range(chunk):
                before = state_in[t + c] if l == 0 else y0[t + c]
                new = before + act[c * nodes : (c + 1) * nodes]
                (upd if l == 0 else state_out)[t + c] = new
                mean = jnp.sum(new, 0, keepdims=True) * (1.0 / nodes)
                gap = new - mean
                stat[event, 0, pl.ds(s + c, 1), :] = mean
                stat[event, 0, pl.ds(per + s + c, 1), :] = jnp.sum(gap * gap, 0, keepdims=True)
                if l == LAYERS - 1:
                    up = cot_in[t + c]
                    stat[event, 0, pl.ds(2 * per + s + c, 1), :] = jnp.sum(up, 0, keepdims=True)
                    stat[event, 0, pl.ds(3 * per + s + c, 1), :] = jnp.sum(
                        up * gap, 0, keepdims=True
                    )
                else:
                    hs[g, 0, s + c] = new[:RIM]
                    hs[g, 1, s + c] = new[nodes - RIM :]
            return 0

        if l < LAYERS - 1:
            stat[event, 0, pl.ds(2 * per, 2 * per), :] = jnp.zeros((2 * per, D), F32)
        lax.fori_loop(0, per // chunk, node, 0)
        stat_send(event, 0)
        if l < LAYERS - 1:
            for way in range(2):
                rim_copy(1 + g, hs.at[g], hr.at[g], way).start()

    def backward(l, g, hook):
        base = g * per
        event = 4 + g
        source = 2 + g if l == LAYERS - 1 else 4 + g
        if l == LAYERS - 1:
            stat_finish(2 + g)
        else:
            stat_finish(4 + g)
            for way in range(2):
                rim_copy(3 + g, rs.at[1, g], rr.at[1, g], way).wait_recv()
        own = 2 * l + g

        def node(j, _):
            s0 = j * chunk
            t0 = base + s0
            deltas, firsts = [], []
            for c in range(chunk):
                s, t = s0 + c, t0 + c
                scale = fin[own, 1, pl.ds(s, 1), :]
                mu = fin[source, 2, pl.ds(s, 1), :]
                cross = fin[source, 3, pl.ds(s, 1), :]
                if l == LAYERS - 1:
                    up = cot_in[t]
                    y = (state_out[t] - fin[own, 0, pl.ds(s, 1), :]) * scale
                    state_out[t] = y
                else:
                    dst[t, pl.ds(0, RIM), :] += rr[1, g, 1, s]
                    dst[t, pl.ds(nodes - RIM, RIM), :] += rr[1, g, 0, s]
                    up = dst[t]
                    y = y0[t]
                delta = scale * (up - mu - y * cross)
                first = delta * sn2[l, t]
                acc_b[l, 0] += jnp.sum(first.reshape(nodes // 8, 8, D), 0)
                deltas.append(delta)
                firsts.append(first)
            d2 = pair(jnp.concatenate(firsts, 0))
            x = rows_of(xs, l, t0, chunk, 0, nodes)
            side = xa[pl.ds(t0, chunk), pl.ds(0, nodes), :].reshape(chunk * nodes, D)
            size = chunk * nodes
            acc_n2[l] += dot_t(hid2[l, pl.ds(t0, chunk)].reshape(size, 2 * D), d2)
            d1 = halves(dot(d2, w_n2t[l])) * sn1[l, pl.ds(t0, chunk)].reshape(size, D)
            d1 = pair(d1)
            p = dot(jnp.concatenate([d1, d1[:, :D]], 1), w_np[l])
            for c in range(chunk):
                at = c * nodes
                dst[t0 + c] = deltas[c] + p[at : at + nodes, :D]
                dag[s0 + c] = p[at : at + nodes, D:] * (1.0 / K)
            acc_agg[l] += dot_t(agg2[l, pl.ds(t0, chunk)].reshape(size, 2 * D), d1)
            acc_nx[l] += dot_t(jnp.concatenate([x, side], 1), d1)
            return 0

        lax.fori_loop(0, per // chunk, node, 0)

        def edge(t, s, slot):
            hidden, deltas, rises = [], [], []
            coming = dag[s]
            bias = None
            for i, o in enumerate(OFFSETS):
                half = a_buf[l, t] + r_buf[l, t, pl.ds(RIM + o, nodes), :]
                act, rise = swish_parts(half)
                rises.append(rise)
                hidden.append(pair(act))
                delta = coming * slope[l, t, pl.ds(i * nodes, nodes), :]
                bias = delta if bias is None else bias + delta
                deltas.append(pair(delta))
            d2 = jnp.concatenate(deltas, 0)
            acc_e2[l] += dot_t(jnp.concatenate(hidden, 0), d2)
            acc_b[l, 1] += jnp.sum(bias.reshape(nodes // 8, 8, D), 0)
            p = dot(d2, w_e2t[l])
            near = None
            for i in range(K):
                d1 = halves(p[i * nodes : (i + 1) * nodes]) * rises[i]
                near = d1 if near is None else near + d1
                e1[slot, i, pl.ds(RIM, nodes), :] = d1
            far = None
            left = None
            right = None
            for i, o in enumerate(OFFSETS):
                part = e1[slot, i, pl.ds(RIM - o, nodes), :]
                far = part if far is None else far + part
                if o < 0:
                    part = e1[slot, i, pl.ds(-o, RIM), :]
                    left = part if left is None else left + part
                else:
                    part = e1[slot, i, pl.ds(RIM + nodes - o, RIM), :]
                    right = part if right is None else right + part
            rims = jnp.concatenate([left, right], 0)
            head, tail = split(near)
            head_f, tail_f = split(far)
            head_r, tail_r = split(rims)
            nothing = jnp.zeros((2 * RIM, D), BF16)
            dxh[s, pl.ds(0, nodes), :] = jnp.concatenate([head, head_f], 1)
            dxl[s, pl.ds(0, nodes), :] = jnp.concatenate([tail, tail_f], 1)
            dxh[s, pl.ds(nodes, 2 * RIM), :] = jnp.concatenate([nothing, head_r], 1)
            dxl[s, pl.ds(nodes, 2 * RIM), :] = jnp.concatenate([nothing, tail_r], 1)

        half_way = per // 4

        def edge_pair(j, _):
            for c in range(2):
                edge(base + 2 * j + c, 2 * j + c, c)
            return 0

        lax.fori_loop(0, half_way, edge_pair, 0)
        hook()
        lax.fori_loop(half_way, per // 2, edge_pair, 0)

        def leave(j, _):
            s0 = j * chunk
            t0 = base + s0
            size = chunk * ext
            x = rows_of(xs, l, t0, chunk, 0, ext)
            side = xa[pl.ds(t0, chunk)].reshape(size, D)
            high = dxh[pl.ds(s0, chunk)].reshape(size, 2 * D)
            low = dxl[pl.ds(s0, chunk)].reshape(size, 2 * D)
            p = halves(dot(high, w_ep[l]) + dot(low, w_ep[l]))
            for c in range(chunk):
                s, t, at = s0 + c, t0 + c, c * ext
                new = dst[t] + p[at : at + nodes]
                dst[t] = new
                rims = p[at + nodes : at + ext]
                rs[l, g, 0, s] = rims[:RIM]
                rs[l, g, 1, s] = rims[RIM:]
                if l > 0:
                    stat[event, 0, pl.ds(2 * per + s, 1), :] = jnp.sum(
                        new, 0, keepdims=True
                    ) + jnp.sum(rims, 0, keepdims=True)
                    stat[event, 0, pl.ds(3 * per + s, 1), :] = jnp.sum(
                        new * y0[t], 0, keepdims=True
                    ) + jnp.sum(rims * yh[t], 0, keepdims=True)
            inputs = jnp.concatenate([x, side], 1)
            acc_x[l] += dot_t(inputs, high) + dot_t(inputs, low)
            return 0

        if l > 0:
            stat[event, 0, pl.ds(0, 2 * per), :] = jnp.zeros((2 * per, D), F32)
        lax.fori_loop(0, per // chunk, leave, 0)
        if l > 0:
            stat_send(event, 0)
        for way in range(2):
            rim_copy(3 + 2 * (1 - l) + g, rs.at[l, g], rr.at[l, g], way).start()

    sums = links.sum_stages

    def quarter(acc, rows):
        return (
            acc[pl.ds(0, rows), pl.ds(0, D)]
            + acc[pl.ds(D, rows), pl.ds(0, D)]
            + acc[pl.ds(0, rows), pl.ds(D, D)]
            + acc[pl.ds(D, rows), pl.ds(D, D)]
        )

    def fold8(value):
        return jnp.sum(value, 0, keepdims=True)

    def node_unit(l, out):
        out[pl.ds(0, D), :] = quarter(acc_nx.at[l], D)
        out[pl.ds(D, D), :] = quarter(acc_agg.at[l], D)
        out[pl.ds(2 * D, D), :] = quarter(acc_n2.at[l], D)
        side = acc_nx[l, pl.ds(2 * D, AUX), :] + acc_nx[l, pl.ds(2 * D + AUX, AUX), :]
        out[pl.ds(UNIT_AUX, AUX), :] = halves(side)
        out[pl.ds(UNIT_BIAS, 1), :] = fold8(acc_b[l, 0])

    def edge_unit(l, out):
        both = acc_x[l, pl.ds(0, D), :] + acc_x[l, pl.ds(D, D), :]
        out[pl.ds(0, D), :] = both[:, :D]
        out[pl.ds(D, D), :] = both[:, D:]
        out[pl.ds(2 * D, D), :] = quarter(acc_e2.at[l], D)
        side = acc_x[l, pl.ds(2 * D, AUX), :] + acc_x[l, pl.ds(2 * D + AUX, AUX), :]
        row = lax.broadcasted_iota(jnp.int32, (AUX, D), 0)
        both = side[:, :D] - side[:, D:]
        out[pl.ds(UNIT_AUX, AUX), :] = jnp.where(
            row < TW, both, jnp.where(row == A_PLACE, both * (1.0 / HALO), side[:, :D])
        )
        out[pl.ds(UNIT_BIAS, 1), :] = fold8(acc_b[l, 1])

    unit_rows = unit_sizes(blk, graph)
    unit_at = [0, unit_rows[0], unit_rows[0] + unit_rows[1]]
    share = [1]
    for stage in range(len(sums)):
        share.append(share[-1] * links.sum_size(stage))

    def seg_rows(n, stage):
        return unit_rows[n] // share[stage + 1]

    def seg_start(n, stage):
        start = unit_at[n]
        for s in range(stage):
            start = start + links.sum_digit(s) * seg_rows(n, s)
        return start

    def recv_start(n, stage):
        at = sum(unit_rows[:n])
        for s in range(stage):
            at += (links.sum_size(s) - 1) * seg_rows(n, s)
        return at

    sem_start = []
    at = 0
    for stage in range(len(sums)):
        sem_start.append(at)
        at += links.sum_size(stage) - 1
    sem_count = at

    def rows_at(start, rows):
        return pl.ds(pl.multiple_of(start, 8), rows)

    def scatter_copy(n, stage, shift):
        peer, digit = links.sum_peer(stage, shift)
        rows = seg_rows(n, stage)
        sem = sem_start[stage] + shift - 1
        return remote(
            unit.at[rows_at(seg_start(n, stage) + digit * rows, rows), :],
            unit_recv.at[pl.ds(recv_start(n, stage) + (shift - 1) * rows, rows), :],
            sum_ssem.at[n, sem],
            sum_rsem.at[n, sem],
            peer,
        )

    def gather_copy(n, stage, shift):
        peer, _ = links.sum_peer(stage, shift)
        rows = seg_rows(n, stage)
        sem = sem_count + sem_start[stage] + shift - 1
        cut = rows_at(seg_start(n, stage + 1), rows)
        return remote(
            unit_all.at[cut, :],
            unit_all.at[cut, :],
            sum_ssem.at[n, sem],
            sum_rsem.at[n, sem],
            peer,
        )

    def gathered(n, stage, shift):
        peer, digit = links.sum_peer(stage, links.sum_size(stage) - shift)
        rows = seg_rows(n, stage)
        sem = sem_count + sem_start[stage] + shift - 1
        cut = rows_at(seg_start(n, stage) + digit * rows, rows)
        return remote(
            unit_all.at[cut, :],
            unit_all.at[cut, :],
            sum_ssem.at[n, sem],
            sum_rsem.at[n, sem],
            peer,
        )

    def shifts(stage):
        return range(1, links.sum_size(stage))

    def sum_step(n, step):
        count = len(sums)
        if 0 < step <= count:
            stage = step - 1
            rows = seg_rows(n, stage)
            for shift in shifts(stage):
                scatter_copy(n, stage, shift).wait_recv()
            cut = rows_at(seg_start(n, step), rows)
            value = unit[cut, :]
            for shift in shifts(stage):
                value = value + unit_recv[
                    pl.ds(recv_start(n, stage) + (shift - 1) * rows, rows), :
                ]
            if step < count:
                unit[cut, :] = value
            else:
                unit_all[cut, :] = value
        if step < count:
            for shift in shifts(step):
                scatter_copy(n, step, shift).start()
            return
        if step > count:
            stage = 2 * count - step
            for shift in shifts(stage):
                gathered(n, stage, shift).wait_recv()
        if step < 2 * count:
            for shift in shifts(2 * count - 1 - step):
                gather_copy(n, 2 * count - 1 - step, shift).start()

    steps = 2 * len(sums)

    def sum_drain(n):
        for stage in range(len(sums)):
            for shift in shifts(stage):
                scatter_copy(n, stage, shift).wait_send()
                gather_copy(n, stage, shift).wait_send()

    for acc in (acc_n2, acc_agg, acc_nx, acc_e2, acc_x, acc_b):
        acc[...] = jnp.zeros_like(acc)

    def nothing():
        pass

    forward(0, 0, nothing)
    forward(0, 1, lambda: stat_forward(0))
    forward(1, 0, lambda: stat_forward(1))
    forward(1, 1, lambda: stat_forward(2))
    backward(1, 0, lambda: stat_forward(3))
    backward(1, 1, lambda: stat_forward(4))
    def unit_part(at):
        return unit.at[pl.ds(at, UNIT_ROWS), :]

    filled = unit_at[0] + 2 * UNIT_ROWS, unit_at[1] + UNIT_ROWS, unit_at[2] + UNIT_ROWS
    for n in range(3):
        left = unit_at[n] + unit_rows[n] - filled[n]
        if left:
            unit[pl.ds(filled[n], left), :] = jnp.zeros((left, D), F32)
    for at in (0, UNIT_ROWS, unit_at[1], unit_at[2]):
        unit[pl.ds(at + UNIT_ROWS - 8, 8), :] = jnp.zeros((8, D), F32)
    node_unit(1, unit_part(0))
    edge_unit(1, unit_part(UNIT_ROWS))
    sum_step(0, 0)

    def hook_a():
        stat_forward(5)
        sum_step(0, 1)

    backward(0, 0, hook_a)
    sum_step(0, 2)
    backward(0, 1, lambda: sum_step(0, 3))
    node_unit(0, unit_part(unit_at[1]))
    edge_unit(0, unit_part(unit_at[2]))
    sum_step(1, 0)
    sum_step(2, 0)
    sum_step(0, 4)
    for step in range(1, steps + 1):
        sum_step(1, step)
        sum_step(2, step)
        if step == 1:
            for g in range(GROUPS):
                for way in range(2):
                    rim_copy(5 + g, rs.at[0, g], rr.at[0, g], way).wait_recv()
                for s in range(per):
                    t = g * per + s
                    dst[t, pl.ds(0, RIM), :] += rr[0, g, 1, s]
                    dst[t, pl.ds(nodes - RIM, RIM), :] += rr[0, g, 0, s]
    for step in range(5, steps + 1):
        sum_step(0, step)

    for way in range(2):
        halo0(way).wait_send()
    for g in range(GROUPS):
        for way in range(2):
            rim_copy(1 + g, hs.at[g], hr.at[g], way).wait_send()
            rim_copy(3 + g, rs.at[1, g], rr.at[1, g], way).wait_send()
            rim_copy(5 + g, rs.at[0, g], rr.at[0, g], way).wait_send()
    for event in range(6):
        for stage in range(len(stages)):
            for shift in range(1, stages[stage][1]):
                stat_copy(event, stage, shift).wait_send()
    for n in range(3):
        sum_drain(n)


def unit_sizes(blk, graph):
    share = 8 * blk * graph
    return [-(-rows // share) * share for rows in (2 * UNIT_ROWS, UNIT_ROWS, UNIT_ROWS)]


def assemble(
    traj,
    unit_at,
    state_mid,
    grad_mid,
    units,
    state_out,
    grad_out,
    g_ew1,
    g_eb1,
    g_ew2,
    g_eb2,
    g_nw1,
    g_nb1,
    g_nw2,
    g_nb2,
    sems,
):
    parts = 4
    rows = traj // parts
    copies = []
    for i, (src, dst) in enumerate(((state_mid, state_out), (grad_mid, grad_out))):
        for part in range(parts):
            cut = pl.ds(part * rows, rows)
            copies.append(pltpu.make_async_copy(src.at[cut], dst.at[cut], sems.at[i, part]))
            copies[-1].start()
    for l in range(LAYERS):
        node_at = 0 if l else unit_at[1]
        edge_at = UNIT_ROWS if l else unit_at[2]

        def rows_of(at, start, count):
            return units[pl.ds(at + start, count), :]

        g_nw1[pl.ds(0, 2 * D), l, :] = rows_of(node_at, 0, 2 * D)
        g_nw1[pl.ds(2 * D, NPAR), l, :] = rows_of(node_at, UNIT_AUX + A_THETA, NPAR)
        g_nb1[pl.ds(l, 1), :] = rows_of(node_at, UNIT_AUX + A_ONE, 1)
        g_nw2[l] = rows_of(node_at, 2 * D, D)
        g_nb2[pl.ds(l, 1), :] = rows_of(node_at, UNIT_BIAS, 1)
        g_ew1[pl.ds(0, 2 * D), l, :] = rows_of(edge_at, 0, 2 * D)
        g_ew1[pl.ds(2 * D, TW), l, :] = rows_of(edge_at, UNIT_AUX, TW)
        g_ew1[pl.ds(2 * D + TW, 1), l, :] = rows_of(edge_at, UNIT_AUX + A_PLACE, 1)
        g_ew1[pl.ds(2 * D + TW + 1, NPAR), l, :] = rows_of(edge_at, UNIT_AUX + A_THETA, NPAR)
        g_eb1[pl.ds(l, 1), :] = rows_of(edge_at, UNIT_AUX + A_ONE, 1)
        g_ew2[l] = rows_of(edge_at, 2 * D, D)
        g_eb2[pl.ds(l, 1), :] = rows_of(edge_at, UNIT_BIAS, 1)
    for copy in copies:
        copy.wait()


def on_device(
    blk,
    graph,
    node_state,
    field_window,
    edge_offset,
    pde_id,
    pde_table,
    cotangent,
    edge_w1,
    edge_b1,
    edge_w2,
    edge_b2,
    node_w1,
    node_b1,
    node_w2,
    node_b2,
):
    traj, nodes, _ = node_state.shape
    per = traj // GROUPS
    ext = nodes + 2 * RIM
    field = jnp.transpose(field_window, (2, 0, 1)).reshape(TW * traj, nodes)
    offset = jnp.transpose(edge_offset, (2, 0, 1)).reshape(K * traj, nodes)
    table = jnp.transpose(pde_table, (1, 0))
    ew1 = jnp.transpose(edge_w1, (1, 0, 2))
    nw1 = jnp.transpose(node_w1, (1, 0, 2))
    vmem = pl.BlockSpec(memory_space=pltpu.VMEM)
    smem = pl.BlockSpec(memory_space=pltpu.SMEM)
    stages = digit_stages(blk)
    peers = max([size - 1 for _, size in stages] + [1])
    rows = unit_sizes(blk, graph)
    unit_at = [0, rows[0], rows[0] + rows[1]]
    rows = sum(rows)
    sum_peers = 0
    for position, (_, size) in enumerate(digit_stages(blk, (2, 2, 4))):
        sum_peers += (size * graph if position == 1 else size) - 1

    def f(*shape):
        return pltpu.VMEM(shape, F32)

    def b(*shape):
        return pltpu.VMEM(shape, BF16)

    L = LAYERS
    scratch = [
        b(L, 4 * D, 3 * D),
        b(L, 2 * D, 2 * D),
        b(L, 2 * D, 2 * D),
        b(L, 2 * D, 2 * D),
        b(L, 2 * D, 2 * D),
        b(L, 2 * D, 2 * D),
        b(L, 3 * D, 2 * D),
        b(L, 2 * D, 2 * D),
        f(AUX, 3 * D),
        b(D, K * D),
        f(8 * traj, nodes),
        f(traj, K * nodes, D),
        f(4, AUX, nodes),
        b(L, traj, ext, 2 * D),
        b(traj, ext, D),
        f(L, traj, nodes, D),
        f(L, traj, ext, D),
        f(per, nodes, D),
        f(L, traj, K * nodes, D),
        b(L, traj, nodes, 2 * D),
        b(L, traj, nodes, 2 * D),
        f(L, traj, nodes, D),
        f(L, traj, nodes, D),
        f(traj, nodes, D),
        f(traj, nodes, D),
        f(traj, 2 * RIM, D),
        f(per, nodes, D),
        f(2, K, ext, D),
        b(per, ext, 2 * D),
        b(per, ext, 2 * D),
        f(L, 2 * D, 2 * D),
        f(L, 2 * D, 2 * D),
        f(L, 3 * D, 2 * D),
        f(L, 2 * D, 2 * D),
        f(L, 3 * D, 2 * D),
        f(L, 2, 8, D),
        f(6, len(stages), 4 * per, D),
        f(6, len(stages), peers, 4 * per, D),
        f(6, 4, per, D),
        f(2, 2, traj, RIM, D),
        f(2, 2, traj, RIM, D),
        f(GROUPS, 2, per, RIM, D),
        f(GROUPS, 2, per, RIM, D),
        f(L, GROUPS, 2, per, RIM, D),
        f(L, GROUPS, 2, per, RIM, D),
        f(rows, D),
        f(rows, D),
        pltpu.SemaphoreType.DMA((6, len(stages), peers)),
        pltpu.SemaphoreType.DMA((6, len(stages), peers)),
        pltpu.SemaphoreType.DMA((7, 2)),
        pltpu.SemaphoreType.DMA((7, 2)),
        pltpu.SemaphoreType.DMA((3, 2 * sum_peers)),
        pltpu.SemaphoreType.DMA((3, 2 * sum_peers)),
    ]
    any_space = pl.BlockSpec(memory_space=pl.ANY)
    mid = pl.pallas_call(
        functools.partial(kernel_body, blk, graph),
        out_shape=[
            jax.ShapeDtypeStruct((traj, nodes, D), F32),
            jax.ShapeDtypeStruct((traj, nodes, D), F32),
            jax.ShapeDtypeStruct((rows, D), F32),
        ],
        in_specs=[vmem, vmem, vmem, smem, smem] + [vmem] * 9,
        out_specs=[vmem] * 3,
        scratch_shapes=scratch,
        compiler_params=pltpu.CompilerParams(
            collective_id=0, has_side_effects=True, vmem_limit_bytes=62 * 2**20
        ),
        name="processor",
    )(
        node_state,
        field,
        offset,
        pde_id,
        table,
        cotangent,
        ew1,
        edge_b1,
        edge_w2,
        edge_b2,
        nw1,
        node_b1,
        node_w2,
        node_b2,
    )
    shapes = [
        (traj, nodes, D),
        (traj, nodes, D),
        (EDGE_IN, L, D),
        (L, D),
        (L, D, D),
        (L, D),
        (NODE_IN, L, D),
        (L, D),
        (L, D, D),
        (L, D),
    ]
    out = pl.pallas_call(
        functools.partial(assemble, traj, unit_at),
        out_shape=[jax.ShapeDtypeStruct(shape, F32) for shape in shapes],
        in_specs=[vmem] * 3,
        out_specs=[any_space, any_space] + [vmem] * 8,
        scratch_shapes=[pltpu.SemaphoreType.DMA((2, 4))],
        name="assemble",
    )(*mid)
    out = list(out)
    out[2] = jnp.transpose(out[2], (1, 0, 2))
    out[6] = jnp.transpose(out[6], (1, 0, 2))
    return tuple(out)


def solution(mesh):
    rows = P("graph", "blk", None)
    return jax.shard_map(
        functools.partial(on_device, mesh.shape["blk"], mesh.shape["graph"]),
        mesh=mesh,
        in_specs=(rows, rows, rows, P("graph"), P(), rows) + (P(),) * 8,
        out_specs=(rows, rows) + (P(),) * 8,
        check_vma=False,
    )
```

time: 799 us -> 92.2 us (0.12); the launches traced: 787 us -> 92.1 us
  blocking collectives: 285 us -> 0 us
  matrix products: 180 us -> 0 us
  other arithmetic: 154 us -> 0 us
  waiting for transfers between devices: 91.6 us -> 0 us
  Pallas kernels: 0 us -> 91.3 us
  local copies, waits for them, and re-layouts: 49.9 us -> 0 us
  between operations: 16 us -> 0.82 us
  starting transfers between devices: 11.1 us -> 0 us
    psum x7 -> x0, blocking collectives: 285 us -> none  [the longest x2 120 us: backward_layer(): lax.psum((jnp.sum(upstream, 1, keepdims=True), jnp.sum(upstream * normed,...]
    dot_general x55 -> x0, matrix products: 180 us -> none  [the longest x31 83.8 us: project(): return jnp.dot(left, right, precision=PRECISE)]
    reduce_sum x24 -> x0, other arithmetic: 132 us -> none  [the longest x12 68.7 us: backward_layer(): place_grad = place_grad - shift / HALO * jnp.sum(piece, (0, 1))]
    psum x1 -> x0, waiting for transfers between devices: 91.5 us -> none  [on_device(): stacked = lax.psum(stacked, ('graph', 'blk'))]
    pallas_call x0 -> x2, Pallas kernels: none -> 91.3 us  [the longest x1 87.1 us: on_device(): pl.pallas_call(functools.partial(kernel_body, blk, graph), out_shape=[jax...]
    mul x2 -> x0, local copies, waits for them, and re-layouts: 16.5 us -> none  [swish_act(): return value * jax.nn.sigmoid(value)]
    unnamed x267 -> x0, local copies, waits for them, and re-layouts: 12.9 us -> none
    ppermute x8 -> x0, starting transfers between devices: 11.1 us -> none  [the longest x4 9.99 us: padded(): lax.ppermute(head, axis, [((i + 1) % count, i) for i in range(count)])]
  transfers between devices with their start and end apart: 9 -> 0, of which waited for: 1 -> 0; matrix products, arithmetic and copies ran while one was open for 4% -> 0% of each run, Pallas kernels for 0% -> 0%
where the time goes in v1:
time: 92.2 us; the launch traced here: 92.1 us
  Pallas kernels  91.3 us (99%)
    pallas_call x1, Pallas kernels, on_device(): pl.pallas_call(functools.partial(kernel_body, blk, graph), out_shape=[jax...  87.1 us
    pallas_call x1, Pallas kernels, on_device(): pl.pallas_call(functools.partial(assemble, traj, unit_at), out_shape=[jax...  4.13 us

profile of v1, /device:TPU:0, one launch (start us, length us, event | category | flops | bytes accessed | tf_op | source)
XLA Modules:
  0.0 92.1 jit_solution(14895569253908781533)
XLA Ops:
  0.6 87.1 %processor.1 = (f32[16,128,128]{2,1,0:T(8,128)}, f32[16,128,128]{2,1,0:T(8,128)}, f32[2048,128]{1,0:T(8,128)}) custom-call(f32[16,128,128]{2,1,0:T(8,128)} %state_in.1, f32[400,128]{1,0:T(8,128)} %bitcast.13, s32[96,128]{1,0:T(8,128)} %bitcast.14, s32[16]{0:T(128)} %id_in.1, f32[3,8]{1,0:T(4,128)} %bitcast.15, f32[16,128,128]{2,1,0:T(8,128)} %cot_in.1, ...), custom_call_target="tpu_custom_call" | custom-call | tf_op jit(solution)/shard_map/processor/pallas_call | solution.py:1049
  87.8 4.1 %assemble.1 = (f32[16,128,128]{2,1,0:T(8,128)}, f32[16,128,128]{2,1,0:T(8,128)}, f32[285,2,128]{2,1,0:T(2,128)}, f32[2,128]{1,0:T(2,128)}, f32[2,128,128]{2,1,0:...) custom-call(f32[16,128,128]{2,1,0:T(8,128)} %get-tuple-element.23.st, ...), custom_call_target="tpu_custom_call" | custom-call | tf_op jit(solution)/shard_map/assemble/pallas_call | solution.py:1091

commit v2 on v1

v2 whole, which is shorter than its diff:
```python
import functools

import jax
import jax.numpy as jnp
from jax import lax
from jax.experimental import pallas as pl
from jax.experimental.pallas import tpu as pltpu
from jax.sharding import PartitionSpec as P

D = 128
TW = 25
NPAR = 3
K = 6
HALO = 3
NPDE = 8
LAYERS = 2
EDGE_IN = 2 * D + TW + 1 + NPAR
NODE_IN = 2 * D + NPAR
OFFSETS = tuple(o for o in range(-HALO, HALO + 1) if o != 0)

EPSILON = 1e-05
RIM = 8
GROUPS = 4
AUX = 32
A_THETA = TW
A_ONE = TW + NPAR
A_PLACE = TW + NPAR + 1
UNIT_AUX = 3 * D
UNIT_BIAS = UNIT_AUX + AUX
UNIT_ROWS = UNIT_BIAS + 8

F32 = jnp.float32
BF16 = jnp.bfloat16
MESH = pl.DeviceIdType.MESH


def dot(left, right):
    return jnp.dot(left, right, preferred_element_type=F32)


def dot_t(left, right):
    return lax.dot_general(left, right, (((0,), (0,)), ((), ())), preferred_element_type=F32)


def split(value):
    head = value.astype(BF16)
    tail = (value - head.astype(F32)).astype(BF16)
    return head, tail


def pair(value):
    head, tail = split(value)
    return jnp.concatenate([head, tail], 1)


def halves(product):
    return product[:, :D] + product[:, D:]


def doubled(weight):
    both = pair(weight)
    return jnp.concatenate([both, both], 0)


def swish_parts(half):
    t = jnp.tanh(half)
    u = 1.0 + t
    act = half * u
    return act, u + act * (1.0 - t)


def digit_stages(count, sizes=(4,)):
    stages, stride, step = [], 1, 0
    while stride < count:
        size = sizes[min(step, len(sizes) - 1)]
        while count // stride % size:
            size -= 1
        stages.append((stride, size))
        stride *= size
        step += 1
    return stages


class Links:
    def __init__(self, blk, graph):
        self.blk, self.graph = blk, graph
        self.me = lax.axis_index("blk")
        self.mine = lax.axis_index("graph")
        self.stat_stages = digit_stages(blk)
        self.share_stages = [[("blk", 1, 2)], [("blk", 2, 2), ("graph", 1, graph)]]
        self.swap_stages = digit_stages(blk // 4)
        self.swap_stages = [(stride * 4, size) for stride, size in self.swap_stages]

    def ring(self, shift):
        return (self.mine, lax.rem(self.me + shift + self.blk, self.blk))

    def digit_peer(self, stride, size, shift):
        digit = lax.rem(self.me // stride, size)
        other = lax.rem(digit + shift, size)
        return (self.mine, self.me + (other - digit) * stride)

    def share_size(self, stage):
        size = 1
        for _, _, count in self.share_stages[stage]:
            size *= count
        return size

    def share_digit(self, stage):
        value = 0
        for axis, stride, size in self.share_stages[stage]:
            place = self.me if axis == "blk" else self.mine
            value = value * size + lax.rem(place // stride, size)
        return value

    def share_peer(self, stage, shift):
        other = lax.rem(self.share_digit(stage) + shift, self.share_size(stage))
        coords = {"blk": self.me, "graph": self.mine}
        rest = other
        for axis, stride, count in reversed(self.share_stages[stage]):
            place = coords[axis]
            now = lax.rem(place // stride, count)
            coords[axis] = place + (lax.rem(rest, count) - now) * stride
            rest = rest // count
        return (coords["graph"], coords["blk"]), other

    def greeted(self):
        peers = [self.ring(1), self.ring(-1)]
        for stride, size in self.stat_stages + self.swap_stages:
            peers += [self.digit_peer(stride, size, shift) for shift in range(1, size)]
        for stage in range(len(self.share_stages)):
            peers += [self.share_peer(stage, shift)[0] for shift in range(1, self.share_size(stage))]
        return peers


def remote(src, dst, send_sem, recv_sem, device):
    return pltpu.make_async_remote_copy(
        src_ref=src,
        dst_ref=dst,
        send_sem=send_sem,
        recv_sem=recv_sem,
        device_id=device,
        device_id_type=MESH,
    )


def kernel_body(
    blk,
    graph,
    state_hbm,
    field_hbm,
    offset_hbm,
    id_in,
    table_in,
    cot_hbm,
    ew1_hbm,
    eb1,
    ew2_hbm,
    eb2,
    nw1_hbm,
    nb1,
    nw2_hbm,
    nb2,
    state_out,
    grad_out,
    unit_out,
    state_in,
    field_in,
    offset_in,
    ew1,
    ew2,
    nw1,
    nw2,
    w_in,
    w_e2,
    w_e2t,
    w_agg,
    w_n2,
    w_n2t,
    w_np,
    w_ep,
    w_aux,
    spread,
    counts,
    weigh,
    aux_t,
    xs,
    xa,
    a_buf,
    r_buf,
    n_buf,
    slope,
    agg2,
    hid2,
    sn1,
    sn2,
    upd,
    y0,
    yh,
    y1,
    dst,
    dag,
    e1,
    dxh,
    dxl,
    acc_n2,
    acc_agg,
    acc_nx,
    acc_e2,
    acc_x,
    acc_b,
    stat,
    stat_recv,
    fin,
    h0s,
    h0r,
    hs,
    hr,
    rs,
    rr,
    unit,
    unit_recv,
    swap,
    swap_recv,
    unit_all,
    load_sem,
    store_sem,
    stat_ssem,
    stat_rsem,
    rim_ssem,
    rim_rsem,
    sum_ssem,
    sum_rsem,
):
    traj, nodes, _ = state_in.shape
    per = traj // GROUPS
    ext = nodes + 2 * RIM
    total = float(nodes * blk)
    links = Links(blk, graph)
    stages = links.stat_stages

    barrier = pltpu.get_barrier_semaphore()
    greeted = links.greeted()
    for peer in greeted:
        pl.semaphore_signal(barrier, inc=1, device_id=peer, device_id_type=MESH)

    loads = [
        pltpu.make_async_copy(src, to, load_sem.at[i])
        for i, (src, to) in enumerate(
            (
                (offset_hbm, offset_in),
                (field_hbm, field_in),
                (state_hbm, state_in),
                (ew1_hbm, ew1),
                (nw1_hbm, nw1),
                (ew2_hbm, ew2),
                (nw2_hbm, nw2),
                (cot_hbm, dst),
            )
        )
    ]
    for load in loads:
        load.start()

    rows = lax.broadcasted_iota(jnp.int32, (D, K * D), 0)
    cols = lax.broadcasted_iota(jnp.int32, (D, K * D), 1)
    spread[...] = jnp.where(rows == 3 * AUX + cols // D, 1.0, 0.0).astype(BF16)
    aux_t[...] = jnp.zeros_like(aux_t)
    place = lax.broadcasted_iota(jnp.int32, (1, nodes), 1).astype(F32) - nodes / 2
    loads[0].wait()
    offs = [offset_in[pl.ds(k * traj, traj), :] for k in range(K)]
    for i, o in enumerate(OFFSETS):
        many = jnp.zeros((traj, nodes), F32)
        for k in range(K):
            many = many + jnp.where(offs[k] == o, 1.0, 0.0)
        counts[pl.ds(i * traj, traj), :] = many
    counts[pl.ds(K * traj, 2 * traj), :] = jnp.zeros((2 * traj, nodes), F32)
    loads[1].wait()
    loads[2].wait()

    def prepare(j, _):
        for c in range(per):
            t = j * per + c
            tile = aux_t.at[c]
            tile[pl.ds(0, TW), :] = field_in[pl.ds(t, TW, stride=traj), :]
            row = id_in[t]
            for q in range(NPAR):
                tile[pl.ds(A_THETA + q, 1), :] = jnp.full((1, nodes), table_in[q, row], F32)
            tile[pl.ds(A_ONE, 1), :] = jnp.ones((1, nodes), F32)
            tile[pl.ds(A_PLACE, 1), :] = place
            head, tail = split(tile[pl.ds(0, AUX), :])
            head, tail = head.astype(F32), tail.astype(F32)
            full = jnp.concatenate(
                [
                    head,
                    tail,
                    head,
                    counts[pl.ds(t, 8, stride=traj), :],
                    jnp.zeros((D - 3 * AUX - 8, nodes), F32),
                ],
                0,
            )
            back = full.T
            h0s[0, 1, t] = back[:RIM]
            h0s[1, 1, t] = back[nodes - RIM :]
            h0s[0, 0, t] = state_in[t, pl.ds(0, RIM), :]
            h0s[1, 0, t] = state_in[t, pl.ds(nodes - RIM, RIM), :]
            xa[t, pl.ds(0, nodes), :] = back.astype(BF16)
        return 0

    lax.fori_loop(0, GROUPS, prepare, 0)

    pl.semaphore_wait(barrier, len(greeted))

    def rim_copy(kind, send, recv, way):
        return remote(
            send.at[way],
            recv.at[way],
            rim_ssem.at[kind, way],
            rim_rsem.at[kind, way],
            links.ring(1 if way else -1),
        )

    for way in range(2):
        rim_copy(0, h0s, h0r, way).start()

    e1[...] = jnp.zeros_like(e1)
    for acc in (acc_n2, acc_agg, acc_nx, acc_e2, acc_x, acc_b):
        acc[...] = jnp.zeros_like(acc)

    def multiply(j, _):
        for c in range(per):
            t = j * per + c
            many = dot(xa[t, pl.ds(0, nodes), :], spread[...])
            for i in range(K):
                weigh[t, pl.ds(i * nodes, nodes), :] = many[:, i * D : (i + 1) * D]
        return 0

    lax.fori_loop(0, GROUPS, multiply, 0)
    for load in loads[3:]:
        load.wait()
    for l in range(LAYERS):
        w_self = ew1[pl.ds(0, D), l, :]
        w_far = ew1[pl.ds(D, D), l, :]
        n_self = nw1[pl.ds(0, D), l, :]
        n_agg = nw1[pl.ds(D, D), l, :]
        for i, w in enumerate((w_self, w_far, n_self)):
            head, tail = split(0.5 * w)
            cut = pl.ds(i * D, D)
            w_in[l, pl.ds(0, D), cut] = head
            w_in[l, pl.ds(D, D), cut] = head
            w_in[l, pl.ds(2 * D, D), cut] = tail
        w_field = 0.5 * ew1[pl.ds(2 * D, TW), l, :]
        w_place = (0.5 / HALO) * ew1[pl.ds(2 * D + TW, 1), l, :]
        w_theta = 0.5 * ew1[pl.ds(2 * D + TW + 1, NPAR), l, :]
        n_theta = 0.5 * nw1[pl.ds(2 * D, NPAR), l, :]
        w_aux[...] = jnp.zeros_like(w_aux)
        w_aux[pl.ds(0, TW), pl.ds(0, D)] = w_field
        w_aux[pl.ds(0, TW), pl.ds(D, D)] = -w_field
        w_aux[pl.ds(A_THETA, NPAR), pl.ds(0, D)] = w_theta
        w_aux[pl.ds(A_THETA, NPAR), pl.ds(2 * D, D)] = n_theta
        w_aux[pl.ds(A_ONE, 1), pl.ds(0, D)] = 0.5 * eb1[pl.ds(l, 1), :]
        w_aux[pl.ds(A_ONE, 1), pl.ds(2 * D, D)] = 0.5 * nb1[pl.ds(l, 1), :]
        w_aux[pl.ds(A_PLACE, 1), pl.ds(0, D)] = w_place
        w_aux[pl.ds(A_PLACE, 1), pl.ds(D, D)] = -w_place
        head, tail = split(w_aux[...])
        w_in[l, pl.ds(3 * D, AUX), :] = head
        w_in[l, pl.ds(3 * D + AUX, AUX), :] = head
        w_in[l, pl.ds(3 * D + 2 * AUX, AUX), :] = tail
        w_in[l, pl.ds(3 * D + 3 * AUX, AUX), :] = jnp.zeros((AUX, 3 * D), BF16)
        second = 0.5 * ew2[l]
        w_e2[l] = doubled(second)
        w_e2t[l] = doubled(second.T)
        w_agg[l] = doubled(0.5 * n_agg)
        w_n2[l] = doubled(0.5 * nw2[l])
        w_n2t[l] = doubled(nw2[l].T)
        head, tail = split(jnp.concatenate([n_self.T, 0.5 * n_agg.T], 1))
        w_np[l, pl.ds(0, D), :] = head
        w_np[l, pl.ds(D, D), :] = head
        w_np[l, pl.ds(2 * D, D), :] = tail
        w_ep[l, pl.ds(0, D), :] = pair(w_self.T)
        w_ep[l, pl.ds(D, D), :] = pair(w_far.T)

    def stat_copy(event, stage, shift):
        stride, size = stages[stage]
        return remote(
            stat.at[event, stage],
            stat_recv.at[event, stage, shift - 1],
            stat_ssem.at[event, stage, shift - 1],
            stat_rsem.at[event, stage, shift - 1],
            links.digit_peer(stride, size, shift),
        )

    def stat_send(event, stage):
        for shift in range(1, stages[stage][1]):
            stat_copy(event, stage, shift).start()

    def stat_merge(event, stage):
        stride, size = stages[stage]
        for shift in range(1, size):
            stat_copy(event, stage, shift).wait_recv()
        parts = [stat.at[event, stage]] + [
            stat_recv.at[event, stage, shift - 1] for shift in range(1, size)
        ]
        m, m2, u, c = [
            [part[pl.ds(q * per, per), :] for part in parts] for q in range(4)
        ]
        mean = sum(m[1:], m[0]) * (1.0 / size)
        gaps = [value - mean for value in m]
        spread2 = sum((gap * gap for gap in gaps[1:]), gaps[0] * gaps[0])
        m2_all = sum(m2[1:], m2[0]) + spread2 * float(nodes * stride)
        u_all = sum(u[1:], u[0])
        c_all = sum(c[1:], c[0])
        for gap, value in zip(gaps, u):
            c_all = c_all + gap * value
        return mean, m2_all, u_all, c_all

    def stat_forward(event):
        for stage in range(1, len(stages)):
            merged = stat_merge(event, stage - 1)
            for q, value in enumerate(merged):
                stat[event, stage, pl.ds(q * per, per), :] = value
            stat_send(event, stage)

    def stat_finish(event, forward):
        mean, m2, u, c = stat_merge(event, len(stages) - 1)
        fin[event, 2] = u * (1.0 / total)
        if forward:
            scale = lax.rsqrt(m2 * (1.0 / total) + EPSILON)
            fin[event, 0] = mean
            fin[event, 1] = scale
            fin[event, 3] = scale * c * (1.0 / total)
        else:
            fin[event, 3] = c * (1.0 / total)

    def rows_of(buf, l, t, start, size):
        return buf[l, pl.ds(t, per), pl.ds(start, size), :].reshape(per * size, buf.shape[-1])

    lane = lax.broadcasted_iota(jnp.int32, (RIM, D), 1)
    moved = jnp.where((lane == A_PLACE) | (lane == 2 * AUX + A_PLACE), float(nodes), 0.0)

    def forward(l, g):
        base = g * per
        event = GROUPS * l + g
        if l > 0:
            before = GROUPS * (l - 1) + g
            stat_finish(before, True)
            for way in range(2):
                rim_copy(1 + g, hs.at[g], hr.at[g], way).wait_recv()
        for c in range(per):
            t = base + c
            if l == 0:
                xs[0, t, pl.ds(0, nodes), :] = pair(state_in[t])
                near = jnp.concatenate([h0r[1, 0, t], h0r[0, 0, t]], 0)
                xs[0, t, pl.ds(nodes, 2 * RIM), :] = pair(near)
                side = jnp.concatenate([h0r[1, 1, t] - moved, h0r[0, 1, t] + moved], 0)
                xa[t, pl.ds(nodes, 2 * RIM), :] = side.astype(BF16)
            else:
                mean = fin[before, 0, pl.ds(c, 1), :]
                scale = fin[before, 1, pl.ds(c, 1), :]
                y = (upd[t] - mean) * scale
                y0[t] = y
                xs[1, t, pl.ds(0, nodes), :] = pair(y)
                near = jnp.concatenate([hr[g, 1, c], hr[g, 0, c]], 0)
                near = (near - mean) * scale
                yh[t] = near
                xs[1, t, pl.ds(nodes, 2 * RIM), :] = pair(near)
        x = rows_of(xs, l, base, 0, ext)
        side = xa[pl.ds(base, per)].reshape(per * ext, D)
        p = dot(x, w_in[l, pl.ds(0, 2 * D), :])
        p = p + dot(jnp.concatenate([x[:, :D], side], 1), w_in[l, pl.ds(2 * D, 2 * D), :])
        for c in range(per):
            at = c * ext
            a_buf[l, base + c] = p[at : at + nodes, :D]
            r_buf[l, base + c, pl.ds(RIM, nodes), :] = p[at : at + nodes, D : 2 * D]
            r_buf[l, base + c, pl.ds(0, RIM), :] = p[at + nodes : at + nodes + RIM, D : 2 * D]
            r_buf[l, base + c, pl.ds(RIM + nodes, RIM), :] = p[
                at + nodes + RIM : at + ext, D : 2 * D
            ]
            n_buf[c] = p[at : at + nodes, 2 * D :]

        bias2 = 0.5 * eb2[pl.ds(l, 1), :]

        def edge(t, s):
            hidden = []
            for o in OFFSETS:
                half = a_buf[l, t] + r_buf[l, t, pl.ds(RIM + o, nodes), :]
                hidden.append(pair(half * (1.0 + jnp.tanh(half))))
            p = dot(jnp.concatenate(hidden, 0), w_e2[l])
            summed = None
            for i in range(K):
                half = halves(p[i * nodes : (i + 1) * nodes]) + bias2
                tanh = jnp.tanh(half)
                scaled = weigh[t, pl.ds(i * nodes, nodes), :] * (1.0 + tanh)
                message = scaled * half
                summed = message if summed is None else summed + message
                slope[l, t, pl.ds(i * nodes, nodes), :] = scaled + message * (1.0 - tanh)
            dag[s] = summed * (1.0 / K)

        def edge_pair(j, _):
            if l == 0:

                @pl.when((j == 1) & (g >= 2))
                def _():
                    stat_forward(event - 2)

            else:

                @pl.when(j == 1)
                def _():
                    stat_forward(event - 2)

            for c in range(2):
                edge(base + 2 * j + c, 2 * j + c)
            return 0

        lax.fori_loop(0, per // 2, edge_pair, 0)

        node2 = 0.5 * nb2[pl.ds(l, 1), :]
        both = pair(dag[...].reshape(per * nodes, D))
        agg2[l, pl.ds(base, per)] = both.reshape(per, nodes, 2 * D)
        half = n_buf[...].reshape(per * nodes, D) + halves(dot(both, w_agg[l]))
        act, rise = swish_parts(half)
        sn1[l, pl.ds(base, per)] = (0.5 * rise).reshape(per, nodes, D)
        both = pair(act)
        hid2[l, pl.ds(base, per)] = both.reshape(per, nodes, 2 * D)
        half = halves(dot(both, w_n2[l])) + node2
        act, rise = swish_parts(half)
        sn2[l, pl.ds(base, per)] = (0.5 * rise).reshape(per, nodes, D)
        last = l == LAYERS - 1
        for c in range(per):
            new = (y0 if l else state_in)[base + c] + act[c * nodes : (c + 1) * nodes]
            (y1 if last else upd)[base + c] = new
            mean = jnp.sum(new, 0, keepdims=True) * (1.0 / nodes)
            gap = new - mean
            stat[event, 0, pl.ds(c, 1), :] = mean
            stat[event, 0, pl.ds(per + c, 1), :] = jnp.sum(gap * gap, 0, keepdims=True)
            if last:
                up = dst[base + c]
                stat[event, 0, pl.ds(2 * per + c, 1), :] = jnp.sum(up, 0, keepdims=True)
                stat[event, 0, pl.ds(3 * per + c, 1), :] = jnp.sum(up * gap, 0, keepdims=True)
            else:
                hs[g, 0, c] = new[:RIM]
                hs[g, 1, c] = new[nodes - RIM :]
        if not last:
            stat[event, 0, pl.ds(2 * per, 2 * per), :] = jnp.zeros((2 * per, D), F32)
        stat_send(event, 0)
        if not last:
            for way in range(2):
                rim_copy(1 + g, hs.at[g], hr.at[g], way).start()
        return 0

    def backward(l, g):
        base = g * per
        last = l == LAYERS - 1
        order = LAYERS if last else LAYERS + 1
        event = GROUPS * order + g
        source = event - GROUPS
        own = GROUPS * l + g
        stat_finish(source, last)
        if not last:
            for way in range(2):
                rim_copy(1 + GROUPS + g, rs.at[1, g], rr.at[1, g], way).wait_recv()
        deltas, firsts = [], []
        for c in range(per):
            t = base + c
            scale = fin[own, 1, pl.ds(c, 1), :]
            mu = fin[source, 2, pl.ds(c, 1), :]
            cross = fin[source, 3, pl.ds(c, 1), :]
            if last:
                up = dst[t]
                y = (y1[t] - fin[own, 0, pl.ds(c, 1), :]) * scale
                y1[t] = y
            else:
                dst[t, pl.ds(0, RIM), :] += rr[1, g, 1, c]
                dst[t, pl.ds(nodes - RIM, RIM), :] += rr[1, g, 0, c]
                up = dst[t]
                y = y0[t]
            delta = scale * (up - mu - y * cross)
            first = delta * sn2[l, t]
            acc_b[l, 0] += jnp.sum(first.reshape(nodes // 8, 8, D), 0)
            deltas.append(delta)
            firsts.append(first)
        if last:
            pltpu.make_async_copy(
                y1.at[pl.ds(base, per)], state_out.at[pl.ds(base, per)], store_sem.at[0, g]
            ).start()
        d2 = pair(jnp.concatenate(firsts, 0))
        x = rows_of(xs, l, base, 0, nodes)
        side = xa[pl.ds(base, per), pl.ds(0, nodes), :].reshape(per * nodes, D)
        size = per * nodes
        acc_n2[l] += dot_t(hid2[l, pl.ds(base, per)].reshape(size, 2 * D), d2)
        d1 = halves(dot(d2, w_n2t[l])) * sn1[l, pl.ds(base, per)].reshape(size, D)
        d1 = pair(d1)
        p = dot(jnp.concatenate([d1, d1[:, :D]], 1), w_np[l])
        for c in range(per):
            at = c * nodes
            dst[base + c] = deltas[c] + p[at : at + nodes, :D]
            dag[c] = p[at : at + nodes, D:] * (1.0 / K)
        acc_agg[l] += dot_t(agg2[l, pl.ds(base, per)].reshape(size, 2 * D), d1)
        acc_nx[l] += dot_t(jnp.concatenate([x, side], 1), d1)

        if not last:
            @pl.when(g == GROUPS - 1)
            def _():
                node_unit(0, unit_part(unit_at[1]))
                sum_step(1, 0)

            @pl.when(g == 2)
            def _():
                sum_step(0, 2)

        def edge(t, s, slot):
            hidden, deltas, rises = [], [], []
            coming = dag[s]
            bias = None
            for i, o in enumerate(OFFSETS):
                half = a_buf[l, t] + r_buf[l, t, pl.ds(RIM + o, nodes), :]
                act, rise = swish_parts(half)
                rises.append(rise)
                hidden.append(pair(act))
                delta = coming * slope[l, t, pl.ds(i * nodes, nodes), :]
                bias = delta if bias is None else bias + delta
                deltas.append(pair(delta))
            d2 = jnp.concatenate(deltas, 0)
            acc_e2[l] += dot_t(jnp.concatenate(hidden, 0), d2)
            acc_b[l, 1] += jnp.sum(bias.reshape(nodes // 8, 8, D), 0)
            p = dot(d2, w_e2t[l])
            near = None
            for i in range(K):
                d1 = halves(p[i * nodes : (i + 1) * nodes]) * rises[i]
                near = d1 if near is None else near + d1
                e1[slot, i, pl.ds(RIM, nodes), :] = d1
            far = None
            left = None
            right = None
            for i, o in enumerate(OFFSETS):
                part = e1[slot, i, pl.ds(RIM - o, nodes), :]
                far = part if far is None else far + part
                if o < 0:
                    part = e1[slot, i, pl.ds(-o, RIM), :]
                    left = part if left is None else left + part
                else:
                    part = e1[slot, i, pl.ds(RIM + nodes - o, RIM), :]
                    right = part if right is None else right + part
            rims = jnp.concatenate([left, right], 0)
            head, tail = split(near)
            head_f, tail_f = split(far)
            head_r, tail_r = split(rims)
            nothing = jnp.zeros((2 * RIM, D), BF16)
            dxh[s, pl.ds(0, nodes), :] = jnp.concatenate([head, head_f], 1)
            dxl[s, pl.ds(0, nodes), :] = jnp.concatenate([tail, tail_f], 1)
            dxh[s, pl.ds(nodes, 2 * RIM), :] = jnp.concatenate([nothing, head_r], 1)
            dxl[s, pl.ds(nodes, 2 * RIM), :] = jnp.concatenate([nothing, tail_r], 1)

        def edge_pair(j, _):
            if last:

                @pl.when(j == 1)
                def _():
                    stat_forward(event - 2)

            else:

                @pl.when((j == 1) & (g < 2))
                def _():
                    stat_forward(event - 2)

                @pl.when((j == 1) & (g == 0))
                def _():
                    sum_step(0, 1)

                @pl.when((j == 1) & (g == GROUPS - 1))
                def _():
                    sum_step(1, 1)

            for c in range(2):
                edge(base + 2 * j + c, 2 * j + c, c)
            return 0

        lax.fori_loop(0, per // 2, edge_pair, 0)

        size = per * ext
        x = rows_of(xs, l, base, 0, ext)
        side = xa[pl.ds(base, per)].reshape(size, D)
        high = dxh[...].reshape(size, 2 * D)
        low = dxl[...].reshape(size, 2 * D)
        p = halves(dot(high, w_ep[l]) + dot(low, w_ep[l]))
        for c in range(per):
            t, at = base + c, c * ext
            new = dst[t] + p[at : at + nodes]
            dst[t] = new
            rims = p[at + nodes : at + ext]
            rs[l, g, 0, c] = rims[:RIM]
            rs[l, g, 1, c] = rims[RIM:]
            if last:
                stat[event, 0, pl.ds(2 * per + c, 1), :] = jnp.sum(
                    new, 0, keepdims=True
                ) + jnp.sum(rims, 0, keepdims=True)
                stat[event, 0, pl.ds(3 * per + c, 1), :] = jnp.sum(
                    new * y0[t], 0, keepdims=True
                ) + jnp.sum(rims * yh[t], 0, keepdims=True)
        inputs = jnp.concatenate([x, side], 1)
        acc_x[l] += dot_t(inputs, high) + dot_t(inputs, low)
        if last:
            stat[event, 0, pl.ds(0, 2 * per), :] = jnp.zeros((2 * per, D), F32)
            stat_send(event, 0)
        for way in range(2):
            rim_copy(
                1 + GROUPS * (2 if not last else 1) + g, rs.at[l, g], rr.at[l, g], way
            ).start()
        return 0

    def quarter(acc, rows):
        return (
            acc[pl.ds(0, rows), pl.ds(0, D)]
            + acc[pl.ds(D, rows), pl.ds(0, D)]
            + acc[pl.ds(0, rows), pl.ds(D, D)]
            + acc[pl.ds(D, rows), pl.ds(D, D)]
        )

    def fold8(value):
        return jnp.sum(value, 0, keepdims=True)

    def node_unit(l, out):
        out[pl.ds(0, D), :] = quarter(acc_nx.at[l], D)
        out[pl.ds(D, D), :] = quarter(acc_agg.at[l], D)
        out[pl.ds(2 * D, D), :] = quarter(acc_n2.at[l], D)
        side = acc_nx[l, pl.ds(2 * D, AUX), :] + acc_nx[l, pl.ds(2 * D + AUX, AUX), :]
        out[pl.ds(UNIT_AUX, AUX), :] = halves(side)
        out[pl.ds(UNIT_BIAS, 1), :] = fold8(acc_b[l, 0])

    def edge_unit(l, out):
        both = acc_x[l, pl.ds(0, D), :] + acc_x[l, pl.ds(D, D), :]
        out[pl.ds(0, D), :] = both[:, :D]
        out[pl.ds(D, D), :] = both[:, D:]
        out[pl.ds(2 * D, D), :] = quarter(acc_e2.at[l], D)
        side = acc_x[l, pl.ds(2 * D, AUX), :] + acc_x[l, pl.ds(2 * D + AUX, AUX), :]
        row = lax.broadcasted_iota(jnp.int32, (AUX, D), 0)
        both = side[:, :D] - side[:, D:]
        out[pl.ds(UNIT_AUX, AUX), :] = jnp.where(
            row < TW, both, jnp.where(row == A_PLACE, both * (1.0 / HALO), side[:, :D])
        )
        out[pl.ds(UNIT_BIAS, 1), :] = fold8(acc_b[l, 1])

    unit_rows = unit_sizes(graph)
    unit_at = unit_starts(graph)
    shares = len(links.share_stages)
    swaps = links.swap_stages
    pieces = [1]
    for stage in range(shares):
        pieces.append(pieces[-1] * links.share_size(stage))

    def unit_part(at):
        return unit.at[pl.ds(at, UNIT_ROWS), :]

    def seg_rows(n, stage):
        return unit_rows[n] // pieces[stage]

    def seg(n, stage):
        start = unit_at[n]
        for s in range(stage):
            start = start + links.share_digit(s) * seg_rows(n, s + 1)
        return pl.ds(pl.multiple_of(start, 8), seg_rows(n, stage))

    def peer_seg(n, stage, digit):
        start = unit_at[n]
        for s in range(stage):
            start = start + links.share_digit(s) * seg_rows(n, s + 1)
        rows = seg_rows(n, stage + 1)
        return pl.ds(pl.multiple_of(start + digit * rows, 8), rows)

    def recv_seg(n, stage, shift):
        at = unit_at[n]
        for s in range(stage):
            at += (links.share_size(s) - 1) * seg_rows(n, s + 1)
        rows = seg_rows(n, stage + 1)
        return pl.ds(at + (shift - 1) * rows, rows)

    def share_sem(stage, shift):
        return sum(links.share_size(s) - 1 for s in range(stage)) + shift - 1

    share_sems = share_sem(shares, 1)

    def swap_sem(stage, shift):
        return 2 * share_sems + sum(size - 1 for _, size in swaps[:stage]) + shift - 1

    def swap_seg(n):
        return pl.ds(unit_at[n] // pieces[-1], seg_rows(n, shares))

    def share_copy(n, stage, shift):
        peer, digit = links.share_peer(stage, shift)
        sem = share_sem(stage, shift)
        return remote(
            unit.at[peer_seg(n, stage, digit), :],
            unit_recv.at[recv_seg(n, stage, shift), :],
            sum_ssem.at[n, sem],
            sum_rsem.at[n, sem],
            peer,
        )

    def swap_copy(n, stage, shift):
        stride, size = swaps[stage]
        sem = swap_sem(stage, shift)
        return remote(
            swap.at[stage, swap_seg(n), :],
            swap_recv.at[stage, shift - 1, swap_seg(n), :],
            sum_ssem.at[n, sem],
            sum_rsem.at[n, sem],
            links.digit_peer(stride, size, shift),
        )

    def gather_copy(n, stage, shift, arriving):
        size = links.share_size(stage)
        peer, digit = links.share_peer(stage, size - shift if arriving else shift)
        sem = share_sems + share_sem(stage, shift)
        cut = peer_seg(n, stage, digit) if arriving else seg(n, stage + 1)
        return remote(
            unit_all.at[cut, :],
            unit_all.at[cut, :],
            sum_ssem.at[n, sem],
            sum_rsem.at[n, sem],
            peer,
        )

    steps = 2 * shares + len(swaps)

    def shifts(size):
        return range(1, size)

    def sum_step(n, step):
        done = step - 1
        value = None
        if 0 <= done < shares:
            for shift in shifts(links.share_size(done)):
                share_copy(n, done, shift).wait_recv()
            value = unit[seg(n, done + 1), :]
            for shift in shifts(links.share_size(done)):
                value = value + unit_recv[recv_seg(n, done, shift), :]
        elif 0 <= done < shares + len(swaps):
            stage = done - shares
            size = swaps[stage][1]
            for shift in shifts(size):
                swap_copy(n, stage, shift).wait_recv()
            value = swap[stage, swap_seg(n), :]
            for shift in shifts(size):
                value = value + swap_recv[stage, shift - 1, swap_seg(n), :]
        elif done >= 0:
            stage = steps - 1 - done
            for shift in shifts(links.share_size(stage)):
                gather_copy(n, stage, shift, True).wait_recv()
        if step < shares:
            if value is not None:
                unit[seg(n, step), :] = value
            for shift in shifts(links.share_size(step)):
                share_copy(n, step, shift).start()
        elif step < shares + len(swaps):
            stage = step - shares
            swap[stage, swap_seg(n), :] = value
            for shift in shifts(swaps[stage][1]):
                swap_copy(n, stage, shift).start()
        elif step < steps:
            if value is not None:
                unit_all[seg(n, shares), :] = value
            stage = steps - 1 - step
            for shift in shifts(links.share_size(stage)):
                gather_copy(n, stage, shift, False).start()

    def sum_drain(n):
        for stage in range(shares):
            for shift in shifts(links.share_size(stage)):
                share_copy(n, stage, shift).wait_send()
                gather_copy(n, stage, shift, False).wait_send()
        for stage, (_, size) in enumerate(swaps):
            for shift in shifts(size):
                swap_copy(n, stage, shift).wait_send()

    for way in range(2):
        rim_copy(0, h0s, h0r, way).wait_recv()
    lax.fori_loop(0, GROUPS, lambda g, _: forward(0, g), 0)
    lax.fori_loop(0, GROUPS, lambda g, _: forward(1, g), 0)
    lax.fori_loop(0, GROUPS, lambda g, _: backward(1, g), 0)
    for n, filled in enumerate((2 * UNIT_ROWS, UNIT_ROWS, UNIT_ROWS)):
        left = unit_rows[n] - filled
        if left:
            unit[pl.ds(unit_at[n] + filled, left), :] = jnp.zeros((left, D), F32)
    for at in (0, UNIT_ROWS, unit_at[1], unit_at[2]):
        unit[pl.ds(at + UNIT_ROWS - 8, 8), :] = jnp.zeros((8, D), F32)
    node_unit(1, unit_part(0))
    edge_unit(1, unit_part(UNIT_ROWS))
    sum_step(0, 0)
    lax.fori_loop(0, GROUPS, lambda g, _: backward(0, g), 0)
    edge_unit(0, unit_part(unit_at[2]))
    sum_step(2, 0)
    sum_step(0, 3)
    stores = []
    for g in range(GROUPS):
        for way in range(2):
            rim_copy(1 + 2 * GROUPS + g, rs.at[0, g], rr.at[0, g], way).wait_recv()
        for c in range(per):
            t = g * per + c
            dst[t, pl.ds(0, RIM), :] += rr[0, g, 1, c]
            dst[t, pl.ds(nodes - RIM, RIM), :] += rr[0, g, 0, c]
        cut = pl.ds(g * per, per)
        stores.append(pltpu.make_async_copy(dst.at[cut], grad_out.at[cut], store_sem.at[1, g]))
        stores[-1].start()
    for step in range(1, steps + 1):
        sum_step(2, step)
        if step + 1 <= steps:
            sum_step(1, step + 1)
        if step + 3 <= steps:
            sum_step(0, step + 3)
    stores.append(pltpu.make_async_copy(unit_all, unit_out, store_sem.at[2, 0]))
    stores[-1].start()

    for way in range(2):
        rim_copy(0, h0s, h0r, way).wait_send()
    for g in range(GROUPS):
        for way in range(2):
            rim_copy(1 + g, hs.at[g], hr.at[g], way).wait_send()
            rim_copy(1 + GROUPS + g, rs.at[1, g], rr.at[1, g], way).wait_send()
            rim_copy(1 + 2 * GROUPS + g, rs.at[0, g], rr.at[0, g], way).wait_send()
        cut = pl.ds(g * per, per)
        pltpu.make_async_copy(y1.at[cut], state_out.at[cut], store_sem.at[0, g]).wait()

    def drain(event, _):
        for stage in range(len(stages)):
            for shift in range(1, stages[stage][1]):
                stat_copy(event, stage, shift).wait_send()
        return 0

    lax.fori_loop(0, 3 * GROUPS, drain, 0)
    for n in range(3):
        sum_drain(n)
    for store in stores:
        store.wait()


def unit_sizes(graph):
    share = 8 * 4 * graph
    return [-(-rows // share) * share for rows in (2 * UNIT_ROWS, UNIT_ROWS, UNIT_ROWS)]


def unit_starts(graph):
    sizes = unit_sizes(graph)
    return [0, sizes[0], sizes[0] + sizes[1]]


def assemble(
    traj,
    unit_at,
    state_mid,
    grad_mid,
    units,
    state_out,
    grad_out,
    g_ew1,
    g_eb1,
    g_ew2,
    g_eb2,
    g_nw1,
    g_nb1,
    g_nw2,
    g_nb2,
    sems,
):
    parts = 4
    rows = traj // parts
    copies = []
    for i, (src, dst) in enumerate(((state_mid, state_out), (grad_mid, grad_out))):
        for part in range(parts):
            cut = pl.ds(part * rows, rows)
            copies.append(pltpu.make_async_copy(src.at[cut], dst.at[cut], sems.at[i, part]))
            copies[-1].start()
    for l in range(LAYERS):
        node_at = 0 if l else unit_at[1]
        edge_at = UNIT_ROWS if l else unit_at[2]

        def rows_of(at, start, count):
            return units[pl.ds(at + start, count), :]

        g_nw1[pl.ds(0, 2 * D), l, :] = rows_of(node_at, 0, 2 * D)
        g_nw1[pl.ds(2 * D, NPAR), l, :] = rows_of(node_at, UNIT_AUX + A_THETA, NPAR)
        g_nb1[pl.ds(l, 1), :] = rows_of(node_at, UNIT_AUX + A_ONE, 1)
        g_nw2[l] = rows_of(node_at, 2 * D, D)
        g_nb2[pl.ds(l, 1), :] = rows_of(node_at, UNIT_BIAS, 1)
        g_ew1[pl.ds(0, 2 * D), l, :] = rows_of(edge_at, 0, 2 * D)
        g_ew1[pl.ds(2 * D, TW), l, :] = rows_of(edge_at, UNIT_AUX, TW)
        g_ew1[pl.ds(2 * D + TW, 1), l, :] = rows_of(edge_at, UNIT_AUX + A_PLACE, 1)
        g_ew1[pl.ds(2 * D + TW + 1, NPAR), l, :] = rows_of(edge_at, UNIT_AUX + A_THETA, NPAR)
        g_eb1[pl.ds(l, 1), :] = rows_of(edge_at, UNIT_AUX + A_ONE, 1)
        g_ew2[l] = rows_of(edge_at, 2 * D, D)
        g_eb2[pl.ds(l, 1), :] = rows_of(edge_at, UNIT_BIAS, 1)
    for copy in copies:
        copy.wait()


def on_device(
    blk,
    graph,
    node_state,
    field_window,
    edge_offset,
    pde_id,
    pde_table,
    cotangent,
    edge_w1,
    edge_b1,
    edge_w2,
    edge_b2,
    node_w1,
    node_b1,
    node_w2,
    node_b2,
):
    traj, nodes, _ = node_state.shape
    per = traj // GROUPS
    ext = nodes + 2 * RIM
    field = jnp.transpose(field_window, (2, 0, 1)).reshape(TW * traj, nodes)
    offset = jnp.transpose(edge_offset, (2, 0, 1)).reshape(K * traj, nodes)
    table = jnp.transpose(pde_table, (1, 0))
    ew1 = jnp.transpose(edge_w1, (1, 0, 2))
    nw1 = jnp.transpose(node_w1, (1, 0, 2))
    vmem = pl.BlockSpec(memory_space=pltpu.VMEM)
    smem = pl.BlockSpec(memory_space=pltpu.SMEM)
    any_space = pl.BlockSpec(memory_space=pl.ANY)
    stages = digit_stages(blk)
    peers = max(size - 1 for _, size in stages)
    swaps = digit_stages(blk // 4)
    swap_peers = max([size - 1 for _, size in swaps] + [1])
    sum_sems = 2 * (1 + 2 * graph - 1) + sum(size - 1 for _, size in swaps)
    unit_at = unit_starts(graph)
    rows = sum(unit_sizes(graph))
    pieces = 4 * graph
    events = 3 * GROUPS

    def f(*shape):
        return pltpu.VMEM(shape, F32)

    def b(*shape):
        return pltpu.VMEM(shape, BF16)

    L = LAYERS
    scratch = [
        f(traj, nodes, D),
        f(TW * traj, nodes),
        pltpu.VMEM((K * traj, nodes), jnp.int32),
        f(EDGE_IN, L, D),
        f(L, D, D),
        f(NODE_IN, L, D),
        f(L, D, D),
        b(L, 4 * D, 3 * D),
        b(L, 2 * D, 2 * D),
        b(L, 2 * D, 2 * D),
        b(L, 2 * D, 2 * D),
        b(L, 2 * D, 2 * D),
        b(L, 2 * D, 2 * D),
        b(L, 3 * D, 2 * D),
        b(L, 2 * D, 2 * D),
        f(AUX, 3 * D),
        b(D, K * D),
        f(8 * traj, nodes),
        f(traj, K * nodes, D),
        f(per, AUX, nodes),
        b(L, traj, ext, 2 * D),
        b(traj, ext, D),
        f(L, traj, nodes, D),
        f(L, traj, ext, D),
        f(per, nodes, D),
        f(L, traj, K * nodes, D),
        b(L, traj, nodes, 2 * D),
        b(L, traj, nodes, 2 * D),
        f(L, traj, nodes, D),
        f(L, traj, nodes, D),
        f(traj, nodes, D),
        f(traj, nodes, D),
        f(traj, 2 * RIM, D),
        f(traj, nodes, D),
        f(traj, nodes, D),
        f(per, nodes, D),
        f(2, K, ext, D),
        b(per, ext, 2 * D),
        b(per, ext, 2 * D),
        f(L, 2 * D, 2 * D),
        f(L, 2 * D, 2 * D),
        f(L, 3 * D, 2 * D),
        f(L, 2 * D, 2 * D),
        f(L, 3 * D, 2 * D),
        f(L, 2, 8, D),
        f(events, len(stages), 4 * per, D),
        f(events, len(stages), peers, 4 * per, D),
        f(events, 4, per, D),
        f(2, 2, traj, RIM, D),
        f(2, 2, traj, RIM, D),
        f(GROUPS, 2, per, RIM, D),
        f(GROUPS, 2, per, RIM, D),
        f(L, GROUPS, 2, per, RIM, D),
        f(L, GROUPS, 2, per, RIM, D),
        f(rows, D),
        f(rows, D),
        f(len(swaps), rows // pieces, D),
        f(len(swaps), swap_peers, rows // pieces, D),
        f(rows, D),
        pltpu.SemaphoreType.DMA((8,)),
        pltpu.SemaphoreType.DMA((3, GROUPS)),
        pltpu.SemaphoreType.DMA((events, len(stages), peers)),
        pltpu.SemaphoreType.DMA((events, len(stages), peers)),
        pltpu.SemaphoreType.DMA((1 + 3 * GROUPS, 2)),
        pltpu.SemaphoreType.DMA((1 + 3 * GROUPS, 2)),
        pltpu.SemaphoreType.DMA((3, sum_sems)),
        pltpu.SemaphoreType.DMA((3, sum_sems)),
    ]
    hbm = any_space
    mid = pl.pallas_call(
        functools.partial(kernel_body, blk, graph),
        out_shape=[
            jax.ShapeDtypeStruct((traj, nodes, D), F32),
            jax.ShapeDtypeStruct((traj, nodes, D), F32),
            jax.ShapeDtypeStruct((rows, D), F32),
        ],
        in_specs=[hbm, hbm, hbm, smem, smem, hbm, hbm, vmem, hbm, vmem, hbm, vmem, hbm, vmem],
        out_specs=[hbm] * 3,
        scratch_shapes=scratch,
        compiler_params=pltpu.CompilerParams(
            collective_id=0, has_side_effects=True, vmem_limit_bytes=62 * 2**20
        ),
        name="processor",
    )(
        node_state,
        field,
        offset,
        pde_id,
        table,
        cotangent,
        ew1,
        edge_b1,
        edge_w2,
        edge_b2,
        nw1,
        node_b1,
        node_w2,
        node_b2,
    )
    shapes = [
        (traj, nodes, D),
        (traj, nodes, D),
        (EDGE_IN, L, D),
        (L, D),
        (L, D, D),
        (L, D),
        (NODE_IN, L, D),
        (L, D),
        (L, D, D),
        (L, D),
    ]
    out = pl.pallas_call(
        functools.partial(assemble, traj, unit_at),
        out_shape=[jax.ShapeDtypeStruct(shape, F32) for shape in shapes],
        in_specs=[vmem] * 3,
        out_specs=[any_space, any_space] + [vmem] * 8,
        scratch_shapes=[pltpu.SemaphoreType.DMA((2, 4))],
        name="assemble",
    )(*mid)
    out = list(out)
    out[2] = jnp.transpose(out[2], (1, 0, 2))
    out[6] = jnp.transpose(out[6], (1, 0, 2))
    return tuple(out)


def solution(mesh):
    rows = P("graph", "blk", None)
    return jax.shard_map(
        functools.partial(on_device, mesh.shape["blk"], mesh.shape["graph"]),
        mesh=mesh,
        in_specs=(rows, rows, rows, P("graph"), P(), rows) + (P(),) * 8,
        out_specs=(rows, rows) + (P(),) * 8,
        check_vma=False,
    )
```

time: 92.2 us -> 77.8 us (0.84)
  Pallas kernels: 91.3 us -> 76.1 us
    pallas_call x1, Pallas kernels: 87.1 us -> 72.1 us  [on_device(): pl.pallas_call(functools.partial(kernel_body, blk, graph), out_shape=[jax...]
where the time goes in v2:
time: 77.8 us; the launch traced here: 76.8 us
  Pallas kernels  76.1 us (98%)
    pallas_call x1, Pallas kernels, on_device(): pl.pallas_call(functools.partial(kernel_body, blk, graph), out_shape=[jax...  72.1 us
    pallas_call x1, Pallas kernels, on_device(): pl.pallas_call(functools.partial(assemble, traj, unit_at), out_shape=[jax...  4.08 us

profile of v2, /device:TPU:0, one launch (start us, length us, event | category | flops | bytes accessed | tf_op | source)
XLA Modules:
  0.0 76.8 jit_solution(17696235838970151418)
XLA Ops:
  0.6 72.1 %processor.1 = (f32[16,128,128]{2,1,0:T(8,128)}, f32[16,128,128]{2,1,0:T(8,128)}, f32[1792,128]{1,0:T(8,128)}) custom-call(f32[16,128,128]{2,1,0:T(8,128)} %state_hbm.1, f32[400,128]{1,0:T(8,128)} %bitcast.13, s32[96,128]{1,0:T(8,128)} %bitcast.14, s32[16]{0:T(128)} %id_in.1, f32[3,8]{1,0:T(4,128)} %bitcast.15, f32[16,128,128]{2,1,0:T(8,128)} %cot_hbm.1, ...), custom_call_target="tpu_custom_call" | custom-call | tf_op jit(solution)/shard_map/processor/pallas_call | solution.py:1113
  72.7 4.1 %assemble.1 = (f32[16,128,128]{2,1,0:T(8,128)}, f32[16,128,128]{2,1,0:T(8,128)}, f32[285,2,128]{2,1,0:T(2,128)}, f32[2,128]{1,0:T(2,128)}, f32[2,128,128]{2,1,0:...) custom-call(f32[16,128,128]{2,1,0:T(8,128)} %get-tuple-element.23.st, ...), custom_call_target="tpu_custom_call" | custom-call | tf_op jit(solution)/shard_map/assemble/pallas_call | solution.py:1155

commit v3 on v2

v3 whole, which is shorter than its diff:
```python
import functools

import jax
import jax.numpy as jnp
from jax import lax
from jax.experimental import pallas as pl
from jax.experimental.pallas import tpu as pltpu
from jax.sharding import PartitionSpec as P

D = 128
TW = 25
NPAR = 3
K = 6
HALO = 3
NPDE = 8
LAYERS = 2
EDGE_IN = 2 * D + TW + 1 + NPAR
NODE_IN = 2 * D + NPAR
OFFSETS = tuple(o for o in range(-HALO, HALO + 1) if o != 0)

EPSILON = 1e-05
RIM = 8
GROUPS = 4
AUX = 32
A_THETA = TW
A_ONE = TW + NPAR
A_PLACE = TW + NPAR + 1
UNIT_AUX = 3 * D
UNIT_BIAS = UNIT_AUX + AUX
UNIT_ROWS = UNIT_BIAS + 8
STAT_SIZES = (2, 8)
ORDER_NODE = "1012112001020020"
ORDER_EDGES = ""
ORDER_ENTER = "002011220001111"
ORDER_LEAVE = "1020101130001133"
ORDER_BACK = ""
ORDER_BACK_NODE = "2020101222002211011"

F32 = jnp.float32
BF16 = jnp.bfloat16
MESH = pl.DeviceIdType.MESH


def dot(left, right):
    return jnp.dot(left, right, preferred_element_type=F32)


def dot_t(left, right):
    return lax.dot_general(left, right, (((0,), (0,)), ((), ())), preferred_element_type=F32)


def split(value):
    head = value.astype(BF16)
    tail = (value - head.astype(F32)).astype(BF16)
    return head, tail


def pair(value):
    head, tail = split(value)
    return jnp.concatenate([head, tail], 1)


def halves(product):
    return product[:, :D] + product[:, D:]


def doubled(weight):
    both = pair(weight)
    return jnp.concatenate([both, both], 0)


def swish_parts(half):
    t = jnp.tanh(half)
    u = 1.0 + t
    act = half * u
    return act, u + act * (1.0 - t)


def digit_stages(count, sizes):
    stages, stride, step = [], 1, 0
    while stride < count:
        size = sizes[min(step, len(sizes) - 1)]
        while count // stride % size:
            size -= 1
        stages.append((stride, size))
        stride *= size
        step += 1
    return stages


class Links:
    def __init__(self, blk, graph):
        self.blk, self.graph = blk, graph
        self.me = lax.axis_index("blk")
        self.mine = lax.axis_index("graph")
        self.stat_stages = digit_stages(blk, STAT_SIZES)
        self.share_digits = [("blk", 1, 2), ("blk", 2, 2), ("graph", 1, graph)]
        self.shares = 4 * graph
        self.swap_stages = [(stride * 4, size) for stride, size in digit_stages(blk // 4, (4,))]

    def ring(self, shift):
        return (self.mine, lax.rem(self.me + shift + self.blk, self.blk))

    def digit_peer(self, stride, size, shift):
        digit = lax.rem(self.me // stride, size)
        other = lax.rem(digit + shift, size)
        return (self.mine, self.me + (other - digit) * stride)

    def share_digit(self):
        value = 0
        for axis, stride, size in self.share_digits:
            place = self.me if axis == "blk" else self.mine
            value = value * size + lax.rem(place // stride, size)
        return value

    def share_peer(self, shift):
        other = lax.rem(self.share_digit() + shift, self.shares)
        coords = {"blk": self.me, "graph": self.mine}
        rest = other
        for axis, stride, count in reversed(self.share_digits):
            place = coords[axis]
            now = lax.rem(place // stride, count)
            coords[axis] = place + (lax.rem(rest, count) - now) * stride
            rest = rest // count
        return (coords["graph"], coords["blk"]), other

    def greeted(self):
        peers = [self.ring(1), self.ring(-1)]
        for stride, size in self.stat_stages + self.swap_stages:
            peers += [self.digit_peer(stride, size, shift) for shift in range(1, size)]
        peers += [self.share_peer(shift)[0] for shift in range(1, self.shares)]
        return peers


def div(value, by):
    return value // by if isinstance(value, int) else lax.div(value, jnp.int32(by))


def rem(value, by):
    return value % by if isinstance(value, int) else lax.rem(value, jnp.int32(by))


def weave(order, *parts):
    for name in order:
        next(parts[int(name)], None)
    for part in parts:
        for _ in part:
            pass


def remote(src, dst, send_sem, recv_sem, device):
    return pltpu.make_async_remote_copy(
        src_ref=src,
        dst_ref=dst,
        send_sem=send_sem,
        recv_sem=recv_sem,
        device_id=device,
        device_id_type=MESH,
    )


def kernel_body(
    blk,
    graph,
    state_hbm,
    field_hbm,
    offset_hbm,
    id_hbm,
    table_hbm,
    cot_hbm,
    ew1_hbm,
    eb1_hbm,
    ew2_hbm,
    eb2_hbm,
    nw1_hbm,
    nb1_hbm,
    nw2_hbm,
    nb2_hbm,
    raw,
    dst,
    unit_all,
    field_in,
    offset_in,
    id_in,
    table_in,
    ew1,
    eb1,
    ew2,
    eb2,
    nw1,
    nb1,
    nw2,
    nb2,
    w_in,
    w_e2,
    w_e2t,
    w_agg,
    w_n2,
    w_n2t,
    w_np,
    w_ep,
    w_aux,
    spread,
    counts,
    weigh,
    aux_t,
    xs,
    xa,
    a_buf,
    r_buf,
    n_buf,
    slope,
    agg2,
    hid2,
    sn1,
    sn2,
    yh,
    dag,
    e1,
    dxh,
    dxl,
    acc_n2,
    acc_agg,
    acc_nx,
    acc_e2,
    acc_x,
    acc_bn,
    acc_be,
    fin,
    hs,
    hr,
    rs,
    rr,
    unit,
    unit_recv,
    load_sem,
    rim_ssem,
    rim_rsem,
    share_ssem,
    share_rsem,
    *staged,
):
    _, traj, nodes, _ = raw.shape
    state_in = raw.at[0]
    per = traj // GROUPS
    ext = nodes + 2 * RIM
    total = float(nodes * blk)
    links = Links(blk, graph)
    stages = links.stat_stages
    swaps = links.swap_stages
    staged = list(staged)
    stat, stat_recv, stat_ssem, stat_rsem = [
        [staged.pop(0) for _ in stages] for _ in range(4)
    ]
    swap, swap_recv, swap_ssem, swap_rsem = [
        [staged.pop(0) for _ in swaps] for _ in range(4)
    ]

    barrier = pltpu.get_barrier_semaphore()
    greeted = links.greeted()
    for peer in greeted:
        pl.semaphore_signal(barrier, inc=1, device_id=peer, device_id_type=MESH)

    parts = [
        (offset_hbm, offset_in),
        (field_hbm, field_in),
        (id_hbm, id_in),
        (table_hbm, table_in),
        (state_hbm, raw.at[0]),
        (eb1_hbm, eb1),
        (eb2_hbm, eb2),
        (nb1_hbm, nb1),
        (nb2_hbm, nb2),
        (ew2_hbm, ew2),
        (nw2_hbm, nw2),
        (cot_hbm, dst),
    ]
    for l in range(LAYERS):
        parts.append((ew1_hbm.at[:, l, :], ew1.at[l, pl.ds(0, EDGE_IN), :]))
        parts.append((nw1_hbm.at[:, l, :], nw1.at[l, pl.ds(0, NODE_IN), :]))
    loads = [pltpu.make_async_copy(src, to, load_sem.at[i]) for i, (src, to) in enumerate(parts)]
    for load in loads:
        load.start()

    rows = lax.broadcasted_iota(jnp.int32, (D, K * D), 0)
    cols = lax.broadcasted_iota(jnp.int32, (D, K * D), 1)
    spread[...] = jnp.where(rows == 3 * AUX + cols // D, 1.0, 0.0).astype(BF16)
    aux_t[...] = jnp.zeros_like(aux_t)
    place = lax.broadcasted_iota(jnp.int32, (1, nodes), 1).astype(F32) - nodes / 2
    loads[0].wait()
    offs = [offset_in[pl.ds(k * traj, traj), :] for k in range(K)]
    for i, o in enumerate(OFFSETS):
        many = jnp.zeros((traj, nodes), F32)
        for k in range(K):
            many = many + jnp.where(offs[k] == o, 1.0, 0.0)
        counts[pl.ds(i * traj, traj), :] = many
    counts[pl.ds(K * traj, 2 * traj), :] = jnp.zeros((2 * traj, nodes), F32)
    for load in loads[1:5]:
        load.wait()

    near_row = lax.broadcasted_iota(jnp.int32, (RIM, D), 0)

    def prepare(j, _):
        for c in range(per):
            t = j * per + c
            tile = aux_t.at[c]
            tile[pl.ds(0, TW), :] = field_in[pl.ds(t, TW, stride=traj), :]
            row = id_in[t]
            for q in range(NPAR):
                tile[pl.ds(A_THETA + q, 1), :] = jnp.full((1, nodes), table_in[q, row], F32)
            tile[pl.ds(A_ONE, 1), :] = jnp.ones((1, nodes), F32)
            tile[pl.ds(A_PLACE, 1), :] = place
            head, tail = split(tile[pl.ds(0, AUX), :])
            head, tail = head.astype(F32), tail.astype(F32)
            full = jnp.concatenate(
                [
                    head,
                    tail,
                    head,
                    counts[pl.ds(t, 8, stride=traj), :],
                    jnp.zeros((D - 3 * AUX - 8, nodes), F32),
                ],
                0,
            )
            back = full.T
            ahead, behind = raw[0, t, pl.ds(0, RIM), :], raw[0, t, pl.ds(nodes - RIM, RIM), :]
            hs[0, 0, t] = jnp.where(near_row < HALO, ahead, pltpu.roll(back[:RIM], HALO, 0))
            hs[1, 0, t] = jnp.where(
                near_row >= RIM - HALO, behind, pltpu.roll(back[nodes - RIM :], RIM - HALO, 0)
            )
            xa[t, pl.ds(0, nodes), :] = back.astype(BF16)
        return 0

    lax.fori_loop(0, GROUPS, prepare, 0)

    pl.semaphore_wait(barrier, len(greeted))

    def ring_send(src, dst, kind, back=0):
        for way in range(2):
            remote(
                src.at[way],
                dst.at[way],
                rim_ssem.at[back],
                rim_rsem.at[kind],
                links.ring(1 if way else -1),
            ).start()

    def arrived(dst, sem):
        pltpu.make_async_copy(dst, dst, sem).wait()

    first = hs.at[:, 0], hr.at[:, 0]
    ring_send(*first, 0)

    def layer_rims(g):
        cut = pl.ds(g * per, per)
        return hs.at[:, 1, cut], hr.at[:, 1, cut]

    def grad_rims(p):
        cut = pl.ds(rem(p, GROUPS) * per, per)
        back = div(p, GROUPS)
        return rs.at[back, :, cut], rr.at[back + 1, :, cut]

    e1[...] = jnp.zeros_like(e1)
    for acc in (acc_n2, acc_agg, acc_nx, acc_e2, acc_x, acc_bn, acc_be):
        acc[...] = jnp.zeros_like(acc)

    def multiply(j, _):
        for c in range(per):
            t = j * per + c
            many = dot(xa[t, pl.ds(0, nodes), :], spread[...])
            for i in range(K):
                weigh[t, pl.ds(i * nodes, nodes), :] = many[:, i * D : (i + 1) * D]
        return 0

    lax.fori_loop(0, GROUPS, multiply, 0)
    for load in loads[5:]:
        load.wait()
    for l in range(LAYERS):
        w_self = ew1[l, pl.ds(0, D), :]
        w_far = ew1[l, pl.ds(D, D), :]
        n_self = nw1[l, pl.ds(0, D), :]
        n_agg = nw1[l, pl.ds(D, D), :]
        for i, w in enumerate((w_self, w_far, n_self)):
            head, tail = split(0.5 * w)
            cut = pl.ds(i * D, D)
            w_in[l, pl.ds(0, D), cut] = head
            w_in[l, pl.ds(D, D), cut] = head
            w_in[l, pl.ds(2 * D, D), cut] = tail
        w_field = 0.5 * ew1[l, pl.ds(2 * D, TW), :]
        w_place = (0.5 / HALO) * ew1[l, pl.ds(2 * D + TW, 1), :]
        w_theta = 0.5 * ew1[l, pl.ds(2 * D + TW + 1, NPAR), :]
        n_theta = 0.5 * nw1[l, pl.ds(2 * D, NPAR), :]
        w_aux[...] = jnp.zeros_like(w_aux)
        w_aux[pl.ds(0, TW), pl.ds(0, D)] = w_field
        w_aux[pl.ds(0, TW), pl.ds(D, D)] = -w_field
        w_aux[pl.ds(A_THETA, NPAR), pl.ds(0, D)] = w_theta
        w_aux[pl.ds(A_THETA, NPAR), pl.ds(2 * D, D)] = n_theta
        w_aux[pl.ds(A_ONE, 1), pl.ds(0, D)] = 0.5 * eb1[pl.ds(l, 1), :]
        w_aux[pl.ds(A_ONE, 1), pl.ds(2 * D, D)] = 0.5 * nb1[pl.ds(l, 1), :]
        w_aux[pl.ds(A_PLACE, 1), pl.ds(0, D)] = w_place
        w_aux[pl.ds(A_PLACE, 1), pl.ds(D, D)] = -w_place
        head, tail = split(w_aux[...])
        w_in[l, pl.ds(3 * D, AUX), :] = head
        w_in[l, pl.ds(3 * D + AUX, AUX), :] = head
        w_in[l, pl.ds(3 * D + 2 * AUX, AUX), :] = tail
        w_in[l, pl.ds(3 * D + 3 * AUX, AUX), :] = jnp.zeros((AUX, 3 * D), BF16)
        second = 0.5 * ew2[l]
        w_e2[l] = doubled(second)
        w_e2t[l] = doubled(second.T)
        w_agg[l] = doubled(0.5 * n_agg)
        w_n2[l] = doubled(0.5 * nw2[l])
        w_n2t[l] = doubled(nw2[l].T)
        head, tail = split(jnp.concatenate([n_self.T, 0.5 * n_agg.T], 1))
        w_np[l, pl.ds(0, D), :] = head
        w_np[l, pl.ds(D, D), :] = head
        w_np[l, pl.ds(2 * D, D), :] = tail
        w_ep[l, pl.ds(0, D), :] = pair(w_self.T)
        w_ep[l, pl.ds(D, D), :] = pair(w_far.T)

    phases = LAYERS * GROUPS
    kinds = (
        (0, GROUPS, pl.ds(0, 2 * per)),
        (GROUPS, phases, pl.ds(0, 4 * per)),
        (phases, phases + GROUPS, pl.ds(2 * per, 2 * per)),
    )

    def by_kind(event, action):
        for low, high, cut in kinds:
            if isinstance(event, int):
                if low <= event < high:
                    action(cut)
            else:
                pl.when((event >= low) & (event < high))(functools.partial(action, cut))

    def stat_send(event, stage):
        stride, size = stages[stage]

        def send(cut):
            for shift in range(1, size):
                remote(
                    stat[stage].at[event, cut],
                    stat_recv[stage].at[event, shift - 1, cut],
                    stat_ssem[stage].at[0],
                    stat_rsem[stage].at[event],
                    links.digit_peer(stride, size, shift),
                ).start()

        by_kind(event, send)

    def stat_merge(event, stage):
        stride, size = stages[stage]
        by_kind(
            event,
            lambda cut: arrived(stat_recv[stage].at[event, :, cut], stat_rsem[stage].at[event]),
        )
        parts = [stat[stage].at[event]] + [
            stat_recv[stage].at[event, shift - 1] for shift in range(1, size)
        ]
        m, m2, u, c = [[part[pl.ds(q * per, per), :] for part in parts] for q in range(4)]
        mean = sum(m[1:], m[0]) * (1.0 / size)
        gaps = [value - mean for value in m]
        spread2 = sum((gap * gap for gap in gaps[1:]), gaps[0] * gaps[0])
        m2_all = sum(m2[1:], m2[0]) + spread2 * float(nodes * stride)
        u_all = sum(u[1:], u[0])
        c_all = sum(c[1:], c[0])
        for gap, value in zip(gaps, u):
            c_all = c_all + gap * value
        return mean, m2_all, u_all, c_all

    def stat_forward(event):
        for stage in range(1, len(stages)):
            merged = stat_merge(event, stage - 1)
            for q, value in enumerate(merged):
                stat[stage][event, pl.ds(q * per, per), :] = value
            stat_send(event, stage)

    def stat_finish(event):
        mean, m2, u, c = stat_merge(event, len(stages) - 1)
        scale = lax.rsqrt(m2 * (1.0 / total) + EPSILON)
        at = event + GROUPS
        fin[at, 0] = mean
        fin[at, 1] = scale
        fin[at, 2] = u * (1.0 / total)
        fin[at, 3] = jnp.where(event < phases, scale, 1.0) * c * (1.0 / total)

    fin[pl.ds(0, GROUPS), 0] = jnp.zeros((GROUPS, per, D), F32)
    fin[pl.ds(0, GROUPS), 1] = jnp.ones((GROUPS, per, D), F32)
    rr[0] = jnp.zeros(rr.shape[1:], F32)
    for stage in range(len(stages)):
        for low, high, unused in (
            (0, GROUPS, pl.ds(2 * per, 2 * per)),
            (phases, phases + GROUPS, pl.ds(0, 2 * per)),
        ):
            cut = pl.ds(low, high - low)
            stat[stage][cut, unused, :] = jnp.zeros((GROUPS, 2 * per, D), F32)
            arrive = stat_recv[stage]
            arrive[cut, :, unused, :] = jnp.zeros((GROUPS, arrive.shape[1], 2 * per, D), F32)

    def rows_of(buf, l, t, start, size):
        return buf[l, pl.ds(t, per), pl.ds(start, size), :].reshape(per * size, buf.shape[-1])

    def enter(p):
        l, g = div(p, GROUPS), rem(p, GROUPS)
        base = g * per
        slot = rem(p, 2)
        for c in range(per):
            t = base + c
            mean = fin[p, 0, pl.ds(c, 1), :]
            scale = fin[p, 1, pl.ds(c, 1), :]
            xs[l, t, pl.ds(0, nodes), :] = pair((raw[l, t] - mean) * scale)
            near = jnp.concatenate([hr[1, l, t], hr[0, l, t]], 0)
            near = (near - mean) * scale
            yh[t] = near
            xs[l, t, pl.ds(nodes, 2 * RIM), :] = pair(near)
        x = rows_of(xs, l, base, 0, ext)
        side = xa[pl.ds(base, per)].reshape(per * ext, D)
        yield
        p4 = dot(x, w_in[l, pl.ds(0, 2 * D), :])
        p4 = p4 + dot(jnp.concatenate([x[:, :D], side], 1), w_in[l, pl.ds(2 * D, 2 * D), :])
        yield
        for c in range(per):
            at = c * ext
            a_buf[l, base + c] = p4[at : at + nodes, :D]
            r_buf[l, base + c, pl.ds(RIM, nodes), :] = p4[at : at + nodes, D : 2 * D]
            r_buf[l, base + c, pl.ds(0, RIM), :] = p4[at + nodes : at + nodes + RIM, D : 2 * D]
            r_buf[l, base + c, pl.ds(RIM + nodes, RIM), :] = p4[
                at + nodes + RIM : at + ext, D : 2 * D
            ]
            n_buf[slot, c] = p4[at : at + nodes, 2 * D :]
        yield

    def edges(p, s):
        l, g = div(p, GROUPS), rem(p, GROUPS)
        bias2 = 0.5 * eb2[pl.ds(l, 1), :]
        t = g * per + s
        hidden = []
        for i, o in enumerate(OFFSETS):
            half = a_buf[l, t] + r_buf[l, t, pl.ds(RIM + o, nodes), :]
            hidden.append(pair(half * (1.0 + jnp.tanh(half))))
            if i == K // 2 - 1:
                yield
        yield
        product = dot(jnp.concatenate(hidden, 0), w_e2[l])
        yield
        summed = None
        for i in range(K):
            half = halves(product[i * nodes : (i + 1) * nodes]) + bias2
            tanh = jnp.tanh(half)
            scaled = weigh[t, pl.ds(i * nodes, nodes), :] * (1.0 + tanh)
            message = scaled * half
            summed = message if summed is None else summed + message
            slope[l, t, pl.ds(i * nodes, nodes), :] = scaled + message * (1.0 - tanh)
            if i == K // 2 - 1:
                yield
        dag[rem(p, 2), s] = summed * (1.0 / K)
        yield

    def node(p):
        l, g = div(p, GROUPS), rem(p, GROUPS)
        base = g * per
        slot = rem(p, 2)
        node2 = 0.5 * nb2[pl.ds(l, 1), :]
        both = pair(dag[slot].reshape(per * nodes, D))
        agg2[l, pl.ds(base, per)] = both.reshape(per, nodes, 2 * D)
        product = dot(both, w_agg[l])
        yield
        half = n_buf[slot].reshape(per * nodes, D) + halves(product)
        act, rise = swish_parts(half)
        sn1[l, pl.ds(base, per)] = (0.5 * rise).reshape(per, nodes, D)
        both = pair(act)
        hid2[l, pl.ds(base, per)] = both.reshape(per, nodes, 2 * D)
        product = dot(both, w_n2[l])
        yield
        half = halves(product) + node2
        act, rise = swish_parts(half)
        sn2[l, pl.ds(base, per)] = (0.5 * rise).reshape(per, nodes, D)
        for c in range(per):
            t = base + c
            before = (raw[l, t] - fin[p, 0, pl.ds(c, 1), :]) * fin[p, 1, pl.ds(c, 1), :]
            new = before + act[c * nodes : (c + 1) * nodes]
            raw[l + 1, t] = new
            hs[0, 1 + l, t] = new[:RIM]
            hs[1, 1 + l, t] = new[nodes - RIM :]
            mean = jnp.sum(new, 0, keepdims=True) * (1.0 / nodes)
            gap = new - mean
            up = dst[t]
            stat[0][p, pl.ds(c, 1), :] = mean
            stat[0][p, pl.ds(per + c, 1), :] = jnp.sum(gap * gap, 0, keepdims=True)
            stat[0][p, pl.ds(2 * per + c, 1), :] = jnp.sum(up, 0, keepdims=True)
            stat[0][p, pl.ds(3 * per + c, 1), :] = jnp.sum(up * gap, 0, keepdims=True)
            if c % 2:
                yield

    def forward(p, _):
        @pl.when(p > 0)
        def _():
            weave(ORDER_NODE, edges(p, 0), edges(p, 1), node(p - 1))

        @pl.when(p == 0)
        def _():
            weave(ORDER_EDGES, edges(p, 0), edges(p, 1))

        @pl.when(p > 0)
        def _():
            stat_send(p - 1, 0)

        @pl.when((p > 0) & (p <= GROUPS))
        def _():
            ring_send(*layer_rims(p - 1), p)

        def ready():
            stat_finish(p + 1 - GROUPS)
            arrived(layer_rims(p + 1 - GROUPS)[1], rim_rsem.at[p + 2 - GROUPS])

        pl.when((p + 1 > GROUPS) & (p + 1 < phases))(ready)
        alone = (p + 1 == GROUPS) | (p + 1 == phases)

        @pl.when(jnp.logical_not(alone))
        def _():
            weave(ORDER_ENTER, edges(p, 2), edges(p, 3), enter(p + 1))

        @pl.when(alone)
        def _():
            weave(ORDER_EDGES, edges(p, 2), edges(p, 3))

        @pl.when(p + 1 == GROUPS)
        def _():
            ready()
            weave("", enter(p + 1))

        @pl.when(p > 0)
        def _():
            stat_forward(p - 1)

        return 0

    def back_node(p):
        l, g = LAYERS - 1 - div(p, GROUPS), rem(p, GROUPS)
        base = g * per
        source = phases + p
        own = GROUPS * (l + 1) + g
        back = div(p, GROUPS)
        deltas, firsts = [], []
        for c in range(per):
            t = base + c
            scale = fin[own, 1, pl.ds(c, 1), :]
            mu = fin[source, 2, pl.ds(c, 1), :]
            cross = fin[source, 3, pl.ds(c, 1), :]
            y = (raw[l + 1, t] - fin[own, 0, pl.ds(c, 1), :]) * scale
            raw[l + 1, t] = y
            up = dst[t]
            up = jnp.concatenate(
                [
                    up[:RIM] + rr[back, 1, t],
                    up[RIM : nodes - RIM],
                    up[nodes - RIM :] + rr[back, 0, t],
                ],
                0,
            )
            delta = scale * (up - mu - y * cross)
            first = delta * sn2[l, t]
            acc_bn[l] += jnp.sum(first.reshape(nodes // 8, 8, D), 0)
            deltas.append(delta)
            firsts.append(first)
        d2 = pair(jnp.concatenate(firsts, 0))
        yield
        x = rows_of(xs, l, base, 0, nodes)
        side = xa[pl.ds(base, per), pl.ds(0, nodes), :].reshape(per * nodes, D)
        size = per * nodes
        product = dot(d2, w_n2t[l])
        yield
        d1 = halves(product) * sn1[l, pl.ds(base, per)].reshape(size, D)
        d1 = pair(d1)
        product = dot(jnp.concatenate([d1, d1[:, :D]], 1), w_np[l])
        yield
        acc_n2[l] += dot_t(hid2[l, pl.ds(base, per)].reshape(size, 2 * D), d2)
        yield
        for c in range(per):
            at = c * nodes
            dst[base + c] = deltas[c] + product[at : at + nodes, :D]
            dag[rem(p, 2), c] = product[at : at + nodes, D:] * (1.0 / K)
        acc_agg[l] += dot_t(agg2[l, pl.ds(base, per)].reshape(size, 2 * D), d1)
        yield
        acc_nx[l] += dot_t(jnp.concatenate([x, side], 1), d1)
        yield

    def back_edges(p, s):
        l, g = LAYERS - 1 - div(p, GROUPS), rem(p, GROUPS)
        slot = rem(p, 2)
        t = g * per + s
        mine = e1.at[s % 2]
        hidden, deltas, rises = [], [], []
        coming = dag[slot, s]
        bias = None
        for i, o in enumerate(OFFSETS):
            half = a_buf[l, t] + r_buf[l, t, pl.ds(RIM + o, nodes), :]
            act, rise = swish_parts(half)
            rises.append(rise)
            hidden.append(pair(act))
            delta = coming * slope[l, t, pl.ds(i * nodes, nodes), :]
            bias = delta if bias is None else bias + delta
            deltas.append(pair(delta))
            if i == K // 2 - 1:
                yield
        d2 = jnp.concatenate(deltas, 0)
        acc_be[l] += jnp.sum(bias.reshape(nodes // 8, 8, D), 0)
        yield
        product = dot(d2, w_e2t[l])
        yield
        acc_e2[l] += dot_t(jnp.concatenate(hidden, 0), d2)
        yield
        near = None
        for i in range(K):
            d1 = halves(product[i * nodes : (i + 1) * nodes]) * rises[i]
            near = d1 if near is None else near + d1
            mine[i, pl.ds(RIM, nodes), :] = d1
        yield
        far = None
        left = None
        right = None
        for i, o in enumerate(OFFSETS):
            part = mine[i, pl.ds(RIM - o, nodes), :]
            far = part if far is None else far + part
            if o < 0:
                part = mine[i, pl.ds(-o, RIM), :]
                left = part if left is None else left + part
            else:
                part = mine[i, pl.ds(RIM + nodes - o, RIM), :]
                right = part if right is None else right + part
        rims = jnp.concatenate([left, right], 0)
        head, tail = split(near)
        head_f, tail_f = split(far)
        head_r, tail_r = split(rims)
        nothing = jnp.zeros((2 * RIM, D), BF16)
        dxh[slot, s, pl.ds(0, nodes), :] = jnp.concatenate([head, head_f], 1)
        dxl[slot, s, pl.ds(0, nodes), :] = jnp.concatenate([tail, tail_f], 1)
        dxh[slot, s, pl.ds(nodes, 2 * RIM), :] = jnp.concatenate([nothing, head_r], 1)
        dxl[slot, s, pl.ds(nodes, 2 * RIM), :] = jnp.concatenate([nothing, tail_r], 1)
        yield

    def leave_weights(p):
        l, g = LAYERS - 1 - div(p, GROUPS), rem(p, GROUPS)
        base = g * per
        size = per * ext
        slot = rem(p, 2)
        x = rows_of(xs, l, base, 0, ext)
        side = xa[pl.ds(base, per)].reshape(size, D)
        inputs = jnp.concatenate([x, side], 1)
        high = dxh[slot].reshape(size, 2 * D)
        low = dxl[slot].reshape(size, 2 * D)
        acc_x[l] += dot_t(
            jnp.concatenate([inputs, inputs], 0), jnp.concatenate([high, low], 0)
        )
        yield

    def leave_state(p):
        l, g = LAYERS - 1 - div(p, GROUPS), rem(p, GROUPS)
        base = g * per
        size = per * ext
        slot = rem(p, 2)
        event = phases + p
        back = div(p, GROUPS)
        own = GROUPS * l + g
        high = dxh[slot].reshape(size, 2 * D)
        low = dxl[slot].reshape(size, 2 * D)
        product = dot(high, w_ep[l]) + dot(low, w_ep[l])
        yield
        product = halves(product)
        for c in range(per):
            t, at = base + c, c * ext
            new = dst[t] + product[at : at + nodes]
            dst[t] = new
            rims = product[at + nodes : at + ext]
            rs[back, 0, t] = rims[:RIM]
            rs[back, 1, t] = rims[RIM:]
            y = (raw[l, t] - fin[own, 0, pl.ds(c, 1), :]) * fin[own, 1, pl.ds(c, 1), :]
            stat[0][event, pl.ds(2 * per + c, 1), :] = jnp.sum(new, 0, keepdims=True) + jnp.sum(
                rims, 0, keepdims=True
            )
            stat[0][event, pl.ds(3 * per + c, 1), :] = jnp.sum(
                new * y, 0, keepdims=True
            ) + jnp.sum(rims * yh[t], 0, keepdims=True)
            if c % 2:
                yield

    def backward(p, _):
        @pl.when(p > 0)
        def _():
            weave(
                ORDER_LEAVE,
                back_edges(p, 0),
                back_edges(p, 1),
                leave_weights(p - 1),
                leave_state(p - 1),
            )

        @pl.when(p == 0)
        def _():
            weave(ORDER_BACK, back_edges(p, 0), back_edges(p, 1))
            stat_forward(phases - 1)

        @pl.when(p > 0)
        def _():
            ring_send(*grad_rims(p - 1), GROUPS + p, 1)

        @pl.when((p > 0) & (p <= GROUPS))
        def _():
            stat_send(phases + p - 1, 0)

        @pl.when(p == GROUPS)
        def _():
            edge_unit(1, unit.at[1])
            sum_step(1, 0)
            sum_step(0, 1)

        @pl.when(p == phases - 1)
        def _():
            sum_step(0, 3)
            sum_step(1, 2)

        @pl.when(p + 1 < phases)
        def _():
            stat_finish(GROUPS + p + 1)

        @pl.when((p + 1 >= GROUPS) & (p + 1 < phases))
        def _():
            arrived(grad_rims(p + 1 - GROUPS)[1], rim_rsem.at[p + 2])

        @pl.when(p + 1 < phases)
        def _():
            weave(ORDER_BACK_NODE, back_edges(p, 2), back_edges(p, 3), back_node(p + 1))

        @pl.when(p + 1 == phases)
        def _():
            weave(ORDER_BACK, back_edges(p, 2), back_edges(p, 3))

        @pl.when((p > 0) & (p <= GROUPS))
        def _():
            stat_forward(phases + p - 1)

        @pl.when(p == GROUPS - 2)
        def _():
            node_unit(1, unit.at[0])
            sum_step(0, 0)

        @pl.when(p == phases - 3)
        def _():
            sum_step(0, 2)
            sum_step(1, 1)

        @pl.when(p == phases - 2)
        def _():
            node_unit(0, unit.at[2])
            sum_step(2, 0)

        return 0

    def quarter(acc, rows):
        return (
            acc[pl.ds(0, rows), pl.ds(0, D)]
            + acc[pl.ds(D, rows), pl.ds(0, D)]
            + acc[pl.ds(0, rows), pl.ds(D, D)]
            + acc[pl.ds(D, rows), pl.ds(D, D)]
        )

    def fold8(value):
        return jnp.sum(value, 0, keepdims=True)

    def node_unit(l, out):
        out[pl.ds(0, D), :] = quarter(acc_nx.at[l], D)
        out[pl.ds(D, D), :] = quarter(acc_agg.at[l], D)
        out[pl.ds(2 * D, D), :] = quarter(acc_n2.at[l], D)
        side = acc_nx[l, pl.ds(2 * D, AUX), :] + acc_nx[l, pl.ds(2 * D + AUX, AUX), :]
        out[pl.ds(UNIT_AUX, AUX), :] = halves(side)
        out[pl.ds(UNIT_BIAS, 1), :] = fold8(acc_bn[l])

    def edge_unit(l, out):
        both = acc_x[l, pl.ds(0, D), :] + acc_x[l, pl.ds(D, D), :]
        out[pl.ds(0, D), :] = both[:, :D]
        out[pl.ds(D, D), :] = both[:, D:]
        out[pl.ds(2 * D, D), :] = quarter(acc_e2.at[l], D)
        side = acc_x[l, pl.ds(2 * D, AUX), :] + acc_x[l, pl.ds(2 * D + AUX, AUX), :]
        row = lax.broadcasted_iota(jnp.int32, (AUX, D), 0)
        both = side[:, :D] - side[:, D:]
        out[pl.ds(UNIT_AUX, AUX), :] = jnp.where(
            row < TW, both, jnp.where(row == A_PLACE, both * (1.0 / HALO), side[:, :D])
        )
        out[pl.ds(UNIT_BIAS, 1), :] = fold8(acc_be[l])

    shares = links.shares
    seg_rows = unit.shape[1] // shares
    mine = pl.multiple_of(links.share_digit() * seg_rows, 8)
    mine = pl.ds(mine, seg_rows)
    steps = 2 + len(swaps)

    def sum_step(n, step):
        value = None
        if step == 1:
            arrived(unit_recv.at[n], share_rsem.at[n])
            value = unit[n, mine, :]
            for shift in range(1, shares):
                value = value + unit_recv[n, shift - 1]
        elif 1 < step < steps:
            stage = step - 2
            arrived(swap_recv[stage].at[n], swap_rsem[stage].at[n])
            value = swap[stage][n]
            for shift in range(1, swaps[stage][1]):
                value = value + swap_recv[stage][n, shift - 1]
        elif step == steps:
            arrived(unit_recv.at[n], share_rsem.at[4 + n])
        if step == 0:
            for shift in range(1, shares):
                peer, digit = links.share_peer(shift)
                cut = pl.ds(pl.multiple_of(digit * seg_rows, 8), seg_rows)
                remote(
                    unit.at[n, cut],
                    unit_recv.at[n, shift - 1],
                    share_ssem.at[0],
                    share_rsem.at[n],
                    peer,
                ).start()
        elif step < steps - 1:
            stage = step - 1
            swap[stage][n] = value
            stride, size = swaps[stage]
            for shift in range(1, size):
                remote(
                    swap[stage].at[n],
                    swap_recv[stage].at[n, shift - 1],
                    swap_ssem[stage].at[0],
                    swap_rsem[stage].at[n],
                    links.digit_peer(stride, size, shift),
                ).start()
        elif step == steps - 1:
            unit_all[n, mine, :] = value
            for shift in range(1, shares):
                remote(
                    unit_all.at[n, mine],
                    unit_all.at[n, mine],
                    share_ssem.at[1],
                    share_rsem.at[4 + n],
                    links.share_peer(shift)[0],
                ).start()

    rest = unit.shape[1] - UNIT_ROWS + 8
    for n in range(4):
        unit[n, pl.ds(UNIT_ROWS - 8, rest), :] = jnp.zeros((rest, D), F32)
    lane = lax.broadcasted_iota(jnp.int32, (RIM, D), 1)
    moved = jnp.where((lane == A_PLACE) | (lane == 2 * AUX + A_PLACE), float(nodes), 0.0)
    arrived(first[1], rim_rsem.at[0])
    for t in range(traj):
        side = jnp.concatenate(
            [
                pltpu.roll(hr[1, 0, t], HALO, 0) - moved,
                pltpu.roll(hr[0, 0, t], RIM - HALO, 0) + moved,
            ],
            0,
        )
        xa[t, pl.ds(nodes, 2 * RIM), :] = side.astype(BF16)
    weave("", enter(0))
    lax.fori_loop(0, phases, forward, 0)
    weave("", node(phases - 1))
    stat_send(phases - 1, 0)
    stat_finish(GROUPS)
    weave("", back_node(0))
    lax.fori_loop(0, phases, backward, 0)
    weave("", leave_weights(phases - 1))
    edge_unit(0, unit.at[3])
    sum_step(3, 0)
    weave("", leave_state(phases - 1))
    ring_send(*grad_rims(phases - 1), GROUPS + phases, 1)
    sum_step(2, 1)
    sum_step(1, 3)
    sum_step(3, 1)
    for g in range(GROUPS):
        arrived(grad_rims(phases - GROUPS + g)[1], rim_rsem.at[phases + 1 + g])
        for c in range(per):
            t = g * per + c
            dst[t, pl.ds(0, RIM), :] += rr[LAYERS, 1, t]
            dst[t, pl.ds(nodes - RIM, RIM), :] += rr[LAYERS, 0, t]
    for step in range(2, steps + 1):
        sum_step(2, step)
        sum_step(3, step)
    for step in range(4, steps + 1):
        sum_step(0, step)
        sum_step(1, step)

    arrived(hr, rim_ssem.at[0])
    arrived(rs, rim_ssem.at[1])
    for stage in range(len(stages)):
        arrived(stat_recv[stage].at[pl.ds(0, phases)], stat_ssem[stage].at[0])
    for stage in range(len(swaps)):
        arrived(swap_recv[stage], swap_ssem[stage].at[0])
    for way in range(2):
        arrived(unit_recv, share_ssem.at[way])


def unit_size(graph):
    share = 8 * 4 * graph
    return -(-UNIT_ROWS // share) * share


def assemble(
    raw,
    grad_mid,
    units,
    state_out,
    grad_out,
    g_ew1,
    g_eb1,
    g_ew2,
    g_eb2,
    g_nw1,
    g_nb1,
    g_nw2,
    g_nb2,
    sems,
):
    parts = sems.shape[1]
    rows = state_out.shape[0] // parts
    copies = []
    for i, (src, dst) in enumerate(((raw.at[LAYERS], state_out), (grad_mid, grad_out))):
        for part in range(parts):
            cut = pl.ds(part * rows, rows)
            copies.append(pltpu.make_async_copy(src.at[cut], dst.at[cut], sems.at[i, part]))
    for copy in copies:
        copy.start()
    for l in range(LAYERS):
        node, edge = units.at[2 * (LAYERS - 1 - l)], units.at[2 * (LAYERS - 1 - l) + 1]
        g_nw1[pl.ds(0, 2 * D), l, :] = node[pl.ds(0, 2 * D), :]
        g_nw1[pl.ds(2 * D, NPAR), l, :] = node[pl.ds(UNIT_AUX + A_THETA, NPAR), :]
        g_nb1[pl.ds(l, 1), :] = node[pl.ds(UNIT_AUX + A_ONE, 1), :]
        g_nw2[l] = node[pl.ds(2 * D, D), :]
        g_nb2[pl.ds(l, 1), :] = node[pl.ds(UNIT_BIAS, 1), :]
        g_ew1[pl.ds(0, 2 * D), l, :] = edge[pl.ds(0, 2 * D), :]
        g_ew1[pl.ds(2 * D, TW), l, :] = edge[pl.ds(UNIT_AUX, TW), :]
        g_ew1[pl.ds(2 * D + TW, 1), l, :] = edge[pl.ds(UNIT_AUX + A_PLACE, 1), :]
        g_ew1[pl.ds(2 * D + TW + 1, NPAR), l, :] = edge[pl.ds(UNIT_AUX + A_THETA, NPAR), :]
        g_eb1[pl.ds(l, 1), :] = edge[pl.ds(UNIT_AUX + A_ONE, 1), :]
        g_ew2[l] = edge[pl.ds(2 * D, D), :]
        g_eb2[pl.ds(l, 1), :] = edge[pl.ds(UNIT_BIAS, 1), :]
    for copy in copies:
        copy.wait()


def on_device(
    blk,
    graph,
    node_state,
    field_window,
    edge_offset,
    pde_id,
    pde_table,
    cotangent,
    edge_w1,
    edge_b1,
    edge_w2,
    edge_b2,
    node_w1,
    node_b1,
    node_w2,
    node_b2,
):
    traj, nodes, _ = node_state.shape
    per = traj // GROUPS
    ext = nodes + 2 * RIM
    field = jnp.transpose(field_window, (2, 0, 1)).reshape(TW * traj, nodes)
    offset = jnp.transpose(edge_offset, (2, 0, 1)).reshape(K * traj, nodes)
    table = jnp.transpose(pde_table, (1, 0))
    ew1 = jnp.transpose(edge_w1, (1, 0, 2))
    nw1 = jnp.transpose(node_w1, (1, 0, 2))
    vmem = pl.BlockSpec(memory_space=pltpu.VMEM)
    any_space = pl.BlockSpec(memory_space=pl.ANY)
    stages = digit_stages(blk, STAT_SIZES)
    swaps = digit_stages(blk // 4, (4,))
    shares = 4 * graph
    rows = unit_size(graph)
    seg = rows // shares
    events = 3 * GROUPS

    def f(*shape):
        return pltpu.VMEM(shape, F32)

    def b(*shape):
        return pltpu.VMEM(shape, BF16)

    L = LAYERS
    scratch = [
        f(TW * traj, nodes),
        pltpu.VMEM((K * traj, nodes), jnp.int32),
        pltpu.SMEM((traj,), jnp.int32),
        pltpu.SMEM((NPAR, NPDE), F32),
        f(L, -(-EDGE_IN // 8) * 8, D),
        f(L, D),
        f(L, D, D),
        f(L, D),
        f(L, -(-NODE_IN // 8) * 8, D),
        f(L, D),
        f(L, D, D),
        f(L, D),
        b(L, 4 * D, 3 * D),
        b(L, 2 * D, 2 * D),
        b(L, 2 * D, 2 * D),
        b(L, 2 * D, 2 * D),
        b(L, 2 * D, 2 * D),
        b(L, 2 * D, 2 * D),
        b(L, 3 * D, 2 * D),
        b(L, 2 * D, 2 * D),
        f(AUX, 3 * D),
        b(D, K * D),
        f(8 * traj, nodes),
        f(traj, K * nodes, D),
        f(per, AUX, nodes),
        b(L, traj, ext, 2 * D),
        b(traj, ext, D),
        f(L, traj, nodes, D),
        f(L, traj, ext, D),
        f(2, per, nodes, D),
        f(L, traj, K * nodes, D),
        b(L, traj, nodes, 2 * D),
        b(L, traj, nodes, 2 * D),
        f(L, traj, nodes, D),
        f(L, traj, nodes, D),
        f(traj, 2 * RIM, D),
        f(2, per, nodes, D),
        f(2, K, ext, D),
        b(2, per, ext, 2 * D),
        b(2, per, ext, 2 * D),
        f(L, 2 * D, 2 * D),
        f(L, 2 * D, 2 * D),
        f(L, 3 * D, 2 * D),
        f(L, 2 * D, 2 * D),
        f(L, 3 * D, 2 * D),
        f(L, 8, D),
        f(L, 8, D),
        f(events + GROUPS, 4, per, D),
        f(2, 1 + L, traj, RIM, D),
        f(2, 2, traj, RIM, D),
        f(L, 2, traj, RIM, D),
        f(L + 1, 2, traj, RIM, D),
        f(4, rows, D),
        f(4, shares - 1, seg, D),
        pltpu.SemaphoreType.DMA((16,)),
        pltpu.SemaphoreType.DMA((2,)),
        pltpu.SemaphoreType.DMA((1 + 3 * GROUPS,)),
        pltpu.SemaphoreType.DMA((2,)),
        pltpu.SemaphoreType.DMA((8,)),
    ]
    scratch += [f(events + GROUPS, 4 * per, D) for _ in stages]
    scratch += [f(events, size - 1, 4 * per, D) for _, size in stages]
    scratch += [pltpu.SemaphoreType.DMA((1,)) for _ in stages]
    scratch += [pltpu.SemaphoreType.DMA((events,)) for _ in stages]
    scratch += [f(4, seg, D) for _ in swaps]
    scratch += [f(4, size - 1, seg, D) for _, size in swaps]
    scratch += [pltpu.SemaphoreType.DMA((1,)) for _ in swaps]
    scratch += [pltpu.SemaphoreType.DMA((4,)) for _ in swaps]
    hbm = any_space
    mid = pl.pallas_call(
        functools.partial(kernel_body, blk, graph),
        out_shape=[f(L + 1, traj, nodes, D), f(traj, nodes, D), f(4, rows, D)],
        in_specs=[hbm] * 14,
        out_specs=[vmem] * 3,
        scratch_shapes=scratch,
        compiler_params=pltpu.CompilerParams(
            collective_id=0, has_side_effects=True, vmem_limit_bytes=54 * 2**20
        ),
        name="processor",
    )(
        node_state,
        field,
        offset,
        pde_id,
        table,
        cotangent,
        ew1,
        edge_b1,
        edge_w2,
        edge_b2,
        nw1,
        node_b1,
        node_w2,
        node_b2,
    )
    mid = [pltpu.with_memory_space_constraint(part, pltpu.VMEM) for part in mid]
    shapes = [
        (traj, nodes, D),
        (traj, nodes, D),
        (EDGE_IN, L, D),
        (L, D),
        (L, D, D),
        (L, D),
        (NODE_IN, L, D),
        (L, D),
        (L, D, D),
        (L, D),
    ]
    out = pl.pallas_call(
        assemble,
        out_shape=[jax.ShapeDtypeStruct(shape, F32) for shape in shapes],
        in_specs=[vmem] * 3,
        out_specs=[any_space, any_space] + [vmem] * 8,
        scratch_shapes=[pltpu.SemaphoreType.DMA((2, 8))],
        compiler_params=pltpu.CompilerParams(vmem_limit_bytes=8 * 2**20),
        name="assemble",
    )(*mid)
    out = list(out)
    out[2] = jnp.transpose(out[2], (1, 0, 2))
    out[6] = jnp.transpose(out[6], (1, 0, 2))
    return tuple(out)


def solution(mesh):
    rows = P("graph", "blk", None)
    return jax.shard_map(
        functools.partial(on_device, mesh.shape["blk"], mesh.shape["graph"]),
        mesh=mesh,
        in_specs=(rows, rows, rows, P("graph"), P(), rows) + (P(),) * 8,
        out_specs=(rows, rows) + (P(),) * 8,
        check_vma=False,
    )
```

time: 77.8 us -> 70.5 us (0.906); the launches traced: 76.8 us -> 70.3 us
  Pallas kernels: 76.1 us -> 69.7 us
    pallas_call x2, Pallas kernels: 76.1 us -> 69.7 us  [the longest x1 67.3 us: on_device(): pl.pallas_call(functools.partial(kernel_body, blk, graph), out_shape=[f(L...]
where the time goes in v3:
time: 70.5 us; the launch traced here: 70.3 us
  Pallas kernels  69.7 us (99%)
    pallas_call x1, Pallas kernels, on_device(): pl.pallas_call(functools.partial(kernel_body, blk, graph), out_shape=[f(L...  67.3 us
    pallas_call x1, Pallas kernels, on_device(): pl.pallas_call(assemble, out_shape=[jax.ShapeDtypeStruct(shape, F32) for...  2.34 us

profile of v3, /device:TPU:0, one launch (start us, length us, event | category | flops | bytes accessed | tf_op | source)
XLA Modules:
  0.0 70.3 jit_solution(13480873069635222385)
XLA Ops:
  0.6 67.3 %processor.1 = (f32[3,16,128,128]{3,2,1,0:T(8,128)S(1)}, f32[16,128,128]{2,1,0:T(8,128)S(1)}, f32[4,448,128]{2,1,0:T(8,128)S(1)}) custom-call(f32[16,128,128]{2,1,0:T(8,128)} %state_hbm.1, f32[400,128]{1,0:T(8,128)} %bitcast.13, s32[96,128]{1,0:T(8,128)} %bitcast.14, s32[16]{0:T(128)} %id_hbm.1, f32[3,8]{1,0:T(4,128)} %bitcast.15, f32[16,128,128]{2,1,0:T(8,128)} %cot_hbm.1, ...), custom_call_target="tpu_custom_call" | custom-call | tf_op jit(solution)/shard_map/processor/pallas_call | solution.py:1158
  68.0 2.3 %assemble.1 = (f32[16,128,128]{2,1,0:T(8,128)}, f32[16,128,128]{2,1,0:T(8,128)}, f32[285,2,128]{2,1,0:T(2,128)}, f32[2,128]{1,0:T(2,128)}, f32[2,128,128]{2,1,0:...) custom-call(f32[3,16,128,128]{3,2,1,0:T(8,128)S(1)} %get-tuple-eleme, ...), custom_call_target="tpu_custom_call" | custom-call | tf_op jit(solution)/shard_map/assemble/pallas_call | solution.py:1197

commit v4 on v3

--- a/solution.py
+++ b/solution.py
@@ -25,10 +25,14 @@
 A_THETA = TW
 A_ONE = TW + NPAR
 A_PLACE = TW + NPAR + 1
+A_SECOND = TW + NPAR + 2
+UNIT_FIRST = D
 UNIT_AUX = 3 * D
-UNIT_BIAS = UNIT_AUX + AUX
-UNIT_ROWS = UNIT_BIAS + 8
+UNIT_ROWS = UNIT_AUX + AUX
 STAT_SIZES = (2, 8)
+SUMS_MID = ((3, 0, 1), (4, 1, 0), (5, 1, 1), (5, 0, 2), (7, 2, 1), (7, 1, 2))
+SUMS_END = ((2, 0, 0), (6, 0, 3), (6, 2, 0))
+SUMS_TURNS = ((3, 4, 2, 0), (3, 4, 1), (2, 3, 4, 1, 0))
 ORDER_NODE = "1012112001020020"
 ORDER_EDGES = ""
 ORDER_ENTER = "002011220001111"
@@ -94,8 +98,7 @@
         self.me = lax.axis_index("blk")
         self.mine = lax.axis_index("graph")
         self.stat_stages = digit_stages(blk, STAT_SIZES)
-        self.share_digits = [("blk", 1, 2), ("blk", 2, 2), ("graph", 1, graph)]
-        self.shares = 4 * graph
+        self.share_stages = [[("blk", 1, 2)], [("blk", 2, 2), ("graph", 1, graph)]]
         self.swap_stages = [(stride * 4, size) for stride, size in digit_stages(blk // 4, (4,))]
 
     def ring(self, shift):
@@ -106,18 +109,24 @@
         other = lax.rem(digit + shift, size)
         return (self.mine, self.me + (other - digit) * stride)
 
-    def share_digit(self):
+    def share_size(self, stage):
+        size = 1
+        for _, _, count in self.share_stages[stage]:
+            size *= count
+        return size
+
+    def share_digit(self, stage):
         value = 0
-        for axis, stride, size in self.share_digits:
+        for axis, stride, size in self.share_stages[stage]:
             place = self.me if axis == "blk" else self.mine
             value = value * size + lax.rem(place // stride, size)
         return value
 
-    def share_peer(self, shift):
-        other = lax.rem(self.share_digit() + shift, self.shares)
+    def share_peer(self, stage, shift):
+        other = lax.rem(self.share_digit(stage) + shift, self.share_size(stage))
         coords = {"blk": self.me, "graph": self.mine}
         rest = other
-        for axis, stride, count in reversed(self.share_digits):
+        for axis, stride, count in reversed(self.share_stages[stage]):
             place = coords[axis]
             now = lax.rem(place // stride, count)
             coords[axis] = place + (lax.rem(rest, count) - now) * stride
@@ -128,7 +137,8 @@
         peers = [self.ring(1), self.ring(-1)]
         for stride, size in self.stat_stages + self.swap_stages:
             peers += [self.digit_peer(stride, size, shift) for shift in range(1, size)]
-        peers += [self.share_peer(shift)[0] for shift in range(1, self.shares)]
+        for stage in range(len(self.share_stages)):
+            peers += [self.share_peer(stage, shift)[0] for shift in range(1, self.share_size(stage))]
         return peers
 
 
@@ -232,7 +242,6 @@
     rs,
     rr,
     unit,
-    unit_recv,
     load_sem,
     rim_ssem,
     rim_rsem,
@@ -247,6 +256,7 @@
     total = float(nodes * blk)
     links = Links(blk, graph)
     stages = links.stat_stages
+    phases = LAYERS * GROUPS
     swaps = links.swap_stages
     staged = list(staged)
     stat, stat_recv, stat_ssem, stat_rsem = [
@@ -255,6 +265,7 @@
     swap, swap_recv, swap_ssem, swap_rsem = [
         [staged.pop(0) for _ in swaps] for _ in range(4)
     ]
+    unit_recv = staged
 
     barrier = pltpu.get_barrier_semaphore()
     greeted = links.greeted()
@@ -286,6 +297,24 @@
     cols = lax.broadcasted_iota(jnp.int32, (D, K * D), 1)
     spread[...] = jnp.where(rows == 3 * AUX + cols // D, 1.0, 0.0).astype(BF16)
     aux_t[...] = jnp.zeros_like(aux_t)
+    e1[...] = jnp.zeros_like(e1)
+    for acc in (acc_n2, acc_agg, acc_nx, acc_e2, acc_x, acc_bn, acc_be):
+        acc[...] = jnp.zeros_like(acc)
+    for u in range(4):
+        rest = unit.shape[1] - UNIT_ROWS
+        unit[u, pl.ds(UNIT_ROWS, rest), :] = jnp.zeros((rest, D), F32)
+    fin[pl.ds(0, GROUPS), 0] = jnp.zeros((GROUPS, per, D), F32)
+    fin[pl.ds(0, GROUPS), 1] = jnp.ones((GROUPS, per, D), F32)
+    rr[0] = jnp.zeros(rr.shape[1:], F32)
+    for stage in range(len(stages)):
+        for low, high, unused in (
+            (0, GROUPS, pl.ds(2 * per, 2 * per)),
+            (phases, phases + GROUPS, pl.ds(0, 2 * per)),
+        ):
+            cut = pl.ds(low, high - low)
+            stat[stage][cut, unused, :] = jnp.zeros((GROUPS, 2 * per, D), F32)
+            arrive = stat_recv[stage]
+            arrive[cut, :, unused, :] = jnp.zeros((GROUPS, arrive.shape[1], 2 * per, D), F32)
     place = lax.broadcasted_iota(jnp.int32, (1, nodes), 1).astype(F32) - nodes / 2
     loads[0].wait()
     offs = [offset_in[pl.ds(k * traj, traj), :] for k in range(K)]
@@ -300,38 +329,34 @@
 
     near_row = lax.broadcasted_iota(jnp.int32, (RIM, D), 0)
 
-    def prepare(j, _):
-        for c in range(per):
-            t = j * per + c
-            tile = aux_t.at[c]
-            tile[pl.ds(0, TW), :] = field_in[pl.ds(t, TW, stride=traj), :]
-            row = id_in[t]
-            for q in range(NPAR):
-                tile[pl.ds(A_THETA + q, 1), :] = jnp.full((1, nodes), table_in[q, row], F32)
-            tile[pl.ds(A_ONE, 1), :] = jnp.ones((1, nodes), F32)
-            tile[pl.ds(A_PLACE, 1), :] = place
-            head, tail = split(tile[pl.ds(0, AUX), :])
-            head, tail = head.astype(F32), tail.astype(F32)
-            full = jnp.concatenate(
-                [
-                    head,
-                    tail,
-                    head,
-                    counts[pl.ds(t, 8, stride=traj), :],
-                    jnp.zeros((D - 3 * AUX - 8, nodes), F32),
-                ],
-                0,
-            )
-            back = full.T
-            ahead, behind = raw[0, t, pl.ds(0, RIM), :], raw[0, t, pl.ds(nodes - RIM, RIM), :]
-            hs[0, 0, t] = jnp.where(near_row < HALO, ahead, pltpu.roll(back[:RIM], HALO, 0))
-            hs[1, 0, t] = jnp.where(
-                near_row >= RIM - HALO, behind, pltpu.roll(back[nodes - RIM :], RIM - HALO, 0)
-            )
-            xa[t, pl.ds(0, nodes), :] = back.astype(BF16)
-        return 0
-
-    lax.fori_loop(0, GROUPS, prepare, 0)
+    for t in range(traj):
+        tile = aux_t.at[t]
+        tile[pl.ds(0, TW), :] = field_in[pl.ds(t, TW, stride=traj), :]
+        row = id_in[t]
+        for q in range(NPAR):
+            tile[pl.ds(A_THETA + q, 1), :] = jnp.full((1, nodes), table_in[q, row], F32)
+        tile[pl.ds(A_ONE, 1), :] = jnp.ones((1, nodes), F32)
+        tile[pl.ds(A_PLACE, 1), :] = place
+    for t in range(traj):
+        head, tail = split(aux_t[t])
+        head, tail = head.astype(F32), tail.astype(F32)
+        full = jnp.concatenate(
+            [
+                head,
+                tail,
+                head,
+                counts[pl.ds(t, 8, stride=traj), :],
+                jnp.zeros((D - 3 * AUX - 8, nodes), F32),
+            ],
+            0,
+        )
+        back = full.T
+        ahead, behind = raw[0, t, pl.ds(0, RIM), :], raw[0, t, pl.ds(nodes - RIM, RIM), :]
+        hs[0, 0, t] = jnp.where(near_row < HALO, ahead, pltpu.roll(back[:RIM], HALO, 0))
+        hs[1, 0, t] = jnp.where(
+            near_row >= RIM - HALO, behind, pltpu.roll(back[nodes - RIM :], RIM - HALO, 0)
+        )
+        xa[t, pl.ds(0, nodes), :] = back.astype(BF16)
 
     pl.semaphore_wait(barrier, len(greeted))
 
@@ -360,9 +385,6 @@
         back = div(p, GROUPS)
         return rs.at[back, :, cut], rr.at[back + 1, :, cut]
 
-    e1[...] = jnp.zeros_like(e1)
-    for acc in (acc_n2, acc_agg, acc_nx, acc_e2, acc_x, acc_bn, acc_be):
-        acc[...] = jnp.zeros_like(acc)
 
     def multiply(j, _):
         for c in range(per):
@@ -417,7 +439,6 @@
         w_ep[l, pl.ds(0, D), :] = pair(w_self.T)
         w_ep[l, pl.ds(D, D), :] = pair(w_far.T)
 
-    phases = LAYERS * GROUPS
     kinds = (
         (0, GROUPS, pl.ds(0, 2 * per)),
         (GROUPS, phases, pl.ds(0, 4 * per)),
@@ -483,19 +504,6 @@
         fin[at, 2] = u * (1.0 / total)
         fin[at, 3] = jnp.where(event < phases, scale, 1.0) * c * (1.0 / total)
 
-    fin[pl.ds(0, GROUPS), 0] = jnp.zeros((GROUPS, per, D), F32)
-    fin[pl.ds(0, GROUPS), 1] = jnp.ones((GROUPS, per, D), F32)
-    rr[0] = jnp.zeros(rr.shape[1:], F32)
-    for stage in range(len(stages)):
-        for low, high, unused in (
-            (0, GROUPS, pl.ds(2 * per, 2 * per)),
-            (phases, phases + GROUPS, pl.ds(0, 2 * per)),
-        ):
-            cut = pl.ds(low, high - low)
-            stat[stage][cut, unused, :] = jnp.zeros((GROUPS, 2 * per, D), F32)
-            arrive = stat_recv[stage]
-            arrive[cut, :, unused, :] = jnp.zeros((GROUPS, arrive.shape[1], 2 * per, D), F32)
-
     def rows_of(buf, l, t, start, size):
         return buf[l, pl.ds(t, per), pl.ds(start, size), :].reshape(per * size, buf.shape[-1])
 
@@ -625,10 +633,11 @@
 
         @pl.when(p + 1 == GROUPS)
         def _():
+            stat_forward(p - 1)
             ready()
             weave("", enter(p + 1))
 
-        @pl.when(p > 0)
+        @pl.when((p > 0) & (p + 1 != GROUPS))
         def _():
             stat_forward(p - 1)
 
@@ -809,14 +818,10 @@
 
         @pl.when(p == GROUPS)
         def _():
+            unit_second(unit.at[1], acc_e2.at[1])
             edge_unit(1, unit.at[1])
-            sum_step(1, 0)
-            sum_step(0, 1)
-
-        @pl.when(p == phases - 1)
-        def _():
-            sum_step(0, 3)
-            sum_step(1, 2)
+
+        sum_hook(SUMS_MID, p)
 
         @pl.when(p + 1 < phases)
         def _():
@@ -841,17 +846,12 @@
         @pl.when(p == GROUPS - 2)
         def _():
             node_unit(1, unit.at[0])
-            sum_step(0, 0)
-
-        @pl.when(p == phases - 3)
-        def _():
-            sum_step(0, 2)
-            sum_step(1, 1)
 
         @pl.when(p == phases - 2)
         def _():
             node_unit(0, unit.at[2])
-            sum_step(2, 0)
+
+        sum_hook(SUMS_END, p)
 
         return 0
 
@@ -866,85 +866,120 @@
     def fold8(value):
         return jnp.sum(value, 0, keepdims=True)
 
+    def unit_second(out, acc):
+        out[pl.ds(0, D), :] = quarter(acc, D)
+
     def node_unit(l, out):
-        out[pl.ds(0, D), :] = quarter(acc_nx.at[l], D)
-        out[pl.ds(D, D), :] = quarter(acc_agg.at[l], D)
-        out[pl.ds(2 * D, D), :] = quarter(acc_n2.at[l], D)
+        unit_second(out, acc_n2.at[l])
+        out[pl.ds(UNIT_FIRST, D), :] = quarter(acc_nx.at[l], D)
+        out[pl.ds(UNIT_FIRST + D, D), :] = quarter(acc_agg.at[l], D)
         side = acc_nx[l, pl.ds(2 * D, AUX), :] + acc_nx[l, pl.ds(2 * D + AUX, AUX), :]
         out[pl.ds(UNIT_AUX, AUX), :] = halves(side)
-        out[pl.ds(UNIT_BIAS, 1), :] = fold8(acc_bn[l])
+        out[pl.ds(UNIT_AUX + A_SECOND, 1), :] = fold8(acc_bn[l])
 
     def edge_unit(l, out):
         both = acc_x[l, pl.ds(0, D), :] + acc_x[l, pl.ds(D, D), :]
-        out[pl.ds(0, D), :] = both[:, :D]
-        out[pl.ds(D, D), :] = both[:, D:]
-        out[pl.ds(2 * D, D), :] = quarter(acc_e2.at[l], D)
+        out[pl.ds(UNIT_FIRST, D), :] = both[:, :D]
+        out[pl.ds(UNIT_FIRST + D, D), :] = both[:, D:]
         side = acc_x[l, pl.ds(2 * D, AUX), :] + acc_x[l, pl.ds(2 * D + AUX, AUX), :]
         row = lax.broadcasted_iota(jnp.int32, (AUX, D), 0)
         both = side[:, :D] - side[:, D:]
         out[pl.ds(UNIT_AUX, AUX), :] = jnp.where(
             row < TW, both, jnp.where(row == A_PLACE, both * (1.0 / HALO), side[:, :D])
         )
-        out[pl.ds(UNIT_BIAS, 1), :] = fold8(acc_be[l])
-
-    shares = links.shares
-    seg_rows = unit.shape[1] // shares
-    mine = pl.multiple_of(links.share_digit() * seg_rows, 8)
-    mine = pl.ds(mine, seg_rows)
-    steps = 2 + len(swaps)
+        out[pl.ds(UNIT_AUX + A_SECOND, 1), :] = fold8(acc_be[l])
+
+    shares = len(links.share_stages)
+    pieces = [1]
+    for stage in range(shares):
+        pieces.append(pieces[-1] * links.share_size(stage))
+    lead, unit_rows = unit_sizes(graph)
+    sums = (
+        (0, 0, unit_rows),
+        (1, 0, unit_rows),
+        (2, 0, unit_rows),
+        (3, 0, lead),
+        (3, lead, unit_rows - lead),
+    )
+    steps = 2 * shares + len(swaps)
 
     def sum_step(n, step):
+        u, start, rows = sums[n]
+
+        def segment(stage, digit=None):
+            place = start
+            for k in range(stage):
+                mine = links.share_digit(k) if digit is None or k < stage - 1 else digit
+                place = place + mine * (rows // pieces[k + 1])
+            return pl.ds(pl.multiple_of(place, 8), rows // pieces[stage])
+
+        def part(stage):
+            return pl.ds(start // pieces[stage], rows // pieces[stage])
+
+        def others(stage):
+            return range(1, links.share_size(stage))
+
+        last = part(shares)
+        done = step - 1
         value = None
-        if step == 1:
-            arrived(unit_recv.at[n], share_rsem.at[n])
-            value = unit[n, mine, :]
-            for shift in range(1, shares):
-                value = value + unit_recv[n, shift - 1]
-        elif 1 < step < steps:
-            stage = step - 2
-            arrived(swap_recv[stage].at[n], swap_rsem[stage].at[n])
-            value = swap[stage][n]
+        if 0 <= done < shares:
+            into = unit_recv[done].at[u, :, part(done + 1)]
+            arrived(into, share_rsem.at[done, n])
+            value = unit[u, segment(done + 1), :]
+            for shift in others(done):
+                value = value + into[shift - 1]
+        elif 0 <= done < shares + len(swaps):
+            stage = done - shares
+            into = swap_recv[stage].at[u, :, last]
+            arrived(into, swap_rsem[stage].at[n])
+            value = swap[stage][u, last, :]
             for shift in range(1, swaps[stage][1]):
-                value = value + swap_recv[stage][n, shift - 1]
-        elif step == steps:
-            arrived(unit_recv.at[n], share_rsem.at[4 + n])
-        if step == 0:
-            for shift in range(1, shares):
-                peer, digit = links.share_peer(shift)
-                cut = pl.ds(pl.multiple_of(digit * seg_rows, 8), seg_rows)
+                value = value + into[shift - 1]
+        elif done >= 0:
+            stage = steps - 1 - done
+            arrived(unit_recv[stage].at[u, :, part(stage + 1)], share_rsem.at[shares + stage, n])
+        if step < shares:
+            if value is not None:
+                unit[u, segment(step), :] = value
+            for shift in others(step):
+                peer, digit = links.share_peer(step, shift)
                 remote(
-                    unit.at[n, cut],
-                    unit_recv.at[n, shift - 1],
-                    share_ssem.at[0],
-                    share_rsem.at[n],
+                    unit.at[u, segment(step + 1, digit)],
+                    unit_recv[step].at[u, shift - 1, part(step + 1)],
+                    share_ssem.at[step],
+                    share_rsem.at[step, n],
                     peer,
                 ).start()
-        elif step < steps - 1:
-            stage = step - 1
-            swap[stage][n] = value
+        elif step < shares + len(swaps):
+            stage = step - shares
+            swap[stage][u, last, :] = value
             stride, size = swaps[stage]
             for shift in range(1, size):
                 remote(
-                    swap[stage].at[n],
-                    swap_recv[stage].at[n, shift - 1],
+                    swap[stage].at[u, last],
+                    swap_recv[stage].at[u, shift - 1, last],
                     swap_ssem[stage].at[0],
                     swap_rsem[stage].at[n],
                     links.digit_peer(stride, size, shift),
                 ).start()
-        elif step == steps - 1:
-            unit_all[n, mine, :] = value
-            for shift in range(1, shares):
+        elif step < steps:
+            if value is not None:
+                unit_all[u, segment(shares), :] = value
+            stage = steps - 1 - step
+            for shift in others(stage):
+                mine = segment(stage + 1)
                 remote(
-                    unit_all.at[n, mine],
-                    unit_all.at[n, mine],
-                    share_ssem.at[1],
-                    share_rsem.at[4 + n],
-                    links.share_peer(shift)[0],
+                    unit_all.at[u, mine],
+                    unit_all.at[u, mine],
+                    share_ssem.at[shares + stage],
+                    share_rsem.at[shares + stage, n],
+                    links.share_peer(stage, shift)[0],
                 ).start()
 
-    rest = unit.shape[1] - UNIT_ROWS + 8
-    for n in range(4):
-        unit[n, pl.ds(UNIT_ROWS - 8, rest), :] = jnp.zeros((rest, D), F32)
+    def sum_hook(table, p):
+        for phase, n, step in table:
+            pl.when(p == phase)(functools.partial(sum_step, n, step))
+
     lane = lax.broadcasted_iota(jnp.int32, (RIM, D), 1)
     moved = jnp.where((lane == A_PLACE) | (lane == 2 * AUX + A_PLACE), float(nodes), 0.0)
     arrived(first[1], rim_rsem.at[0])
@@ -964,26 +999,30 @@
     stat_finish(GROUPS)
     weave("", back_node(0))
     lax.fori_loop(0, phases, backward, 0)
+    unit_second(unit.at[3], acc_e2.at[0])
+    sum_step(3, 0)
     weave("", leave_weights(phases - 1))
     edge_unit(0, unit.at[3])
-    sum_step(3, 0)
+    sum_step(4, 0)
     weave("", leave_state(phases - 1))
     ring_send(*grad_rims(phases - 1), GROUPS + phases, 1)
-    sum_step(2, 1)
-    sum_step(1, 3)
-    sum_step(3, 1)
-    for g in range(GROUPS):
-        arrived(grad_rims(phases - GROUPS + g)[1], rim_rsem.at[phases + 1 + g])
-        for c in range(per):
-            t = g * per + c
-            dst[t, pl.ds(0, RIM), :] += rr[LAYERS, 1, t]
-            dst[t, pl.ds(nodes - RIM, RIM), :] += rr[LAYERS, 0, t]
-    for step in range(2, steps + 1):
-        sum_step(2, step)
-        sum_step(3, step)
-    for step in range(4, steps + 1):
-        sum_step(0, step)
-        sum_step(1, step)
+    done = {n: 0 for n in range(len(sums))}
+    for table in (SUMS_MID, SUMS_END):
+        for _, n, step in table:
+            done[n] = max(done[n], step)
+    for turn in range(2 * steps):
+        for n in SUMS_TURNS[min(turn, len(SUMS_TURNS) - 1)]:
+            if done[n] < steps:
+                done[n] += 1
+                sum_step(n, done[n])
+        if turn:
+            continue
+        for g in range(GROUPS):
+            arrived(grad_rims(phases - GROUPS + g)[1], rim_rsem.at[phases + 1 + g])
+            for c in range(per):
+                t = g * per + c
+                dst[t, pl.ds(0, RIM), :] += rr[LAYERS, 1, t]
+                dst[t, pl.ds(nodes - RIM, RIM), :] += rr[LAYERS, 0, t]
 
     arrived(hr, rim_ssem.at[0])
     arrived(rs, rim_ssem.at[1])
@@ -991,13 +1030,15 @@
         arrived(stat_recv[stage].at[pl.ds(0, phases)], stat_ssem[stage].at[0])
     for stage in range(len(swaps)):
         arrived(swap_recv[stage], swap_ssem[stage].at[0])
-    for way in range(2):
-        arrived(unit_recv, share_ssem.at[way])
-
-
-def unit_size(graph):
+    for stage in range(shares):
+        for way in range(2):
+            arrived(unit_recv[stage], share_ssem.at[way * shares + stage])
+
+
+def unit_sizes(graph):
     share = 8 * 4 * graph
-    return -(-UNIT_ROWS // share) * share
+    lead = -(-UNIT_FIRST // share) * share
+    return lead, lead + -(-(UNIT_ROWS - UNIT_FIRST) // share) * share
 
 
 def assemble(
@@ -1027,18 +1068,18 @@
         copy.start()
     for l in range(LAYERS):
         node, edge = units.at[2 * (LAYERS - 1 - l)], units.at[2 * (LAYERS - 1 - l) + 1]
-        g_nw1[pl.ds(0, 2 * D), l, :] = node[pl.ds(0, 2 * D), :]
+        for unit, first, bias1, second, bias2 in (
+            (node, g_nw1, g_nb1, g_nw2, g_nb2),
+            (edge, g_ew1, g_eb1, g_ew2, g_eb2),
+        ):
+            first[pl.ds(0, 2 * D), l, :] = unit[pl.ds(UNIT_FIRST, 2 * D), :]
+            bias1[pl.ds(l, 1), :] = unit[pl.ds(UNIT_AUX + A_ONE, 1), :]
+            second[l] = unit[pl.ds(0, D), :]
+            bias2[pl.ds(l, 1), :] = unit[pl.ds(UNIT_AUX + A_SECOND, 1), :]
         g_nw1[pl.ds(2 * D, NPAR), l, :] = node[pl.ds(UNIT_AUX + A_THETA, NPAR), :]
-        g_nb1[pl.ds(l, 1), :] = node[pl.ds(UNIT_AUX + A_ONE, 1), :]
-        g_nw2[l] = node[pl.ds(2 * D, D), :]
-        g_nb2[pl.ds(l, 1), :] = node[pl.ds(UNIT_BIAS, 1), :]
-        g_ew1[pl.ds(0, 2 * D), l, :] = edge[pl.ds(0, 2 * D), :]
         g_ew1[pl.ds(2 * D, TW), l, :] = edge[pl.ds(UNIT_AUX, TW), :]
         g_ew1[pl.ds(2 * D + TW, 1), l, :] = edge[pl.ds(UNIT_AUX + A_PLACE, 1), :]
         g_ew1[pl.ds(2 * D + TW + 1, NPAR), l, :] = edge[pl.ds(UNIT_AUX + A_THETA, NPAR), :]
-        g_eb1[pl.ds(l, 1), :] = edge[pl.ds(UNIT_AUX + A_ONE, 1), :]
-        g_ew2[l] = edge[pl.ds(2 * D, D), :]
-        g_eb2[pl.ds(l, 1), :] = edge[pl.ds(UNIT_BIAS, 1), :]
     for copy in copies:
         copy.wait()
 
@@ -1074,7 +1115,7 @@
     stages = digit_stages(blk, STAT_SIZES)
     swaps = digit_stages(blk // 4, (4,))
     shares = 4 * graph
-    rows = unit_size(graph)
+    _, rows = unit_sizes(graph)
     seg = rows // shares
     events = 3 * GROUPS
 
@@ -1110,7 +1151,7 @@
         b(D, K * D),
         f(8 * traj, nodes),
         f(traj, K * nodes, D),
-        f(per, AUX, nodes),
+        f(traj, AUX, nodes),
         b(L, traj, ext, 2 * D),
         b(traj, ext, D),
         f(L, traj, nodes, D),
@@ -1139,12 +1180,11 @@
         f(L, 2, traj, RIM, D),
         f(L + 1, 2, traj, RIM, D),
         f(4, rows, D),
-        f(4, shares - 1, seg, D),
         pltpu.SemaphoreType.DMA((16,)),
         pltpu.SemaphoreType.DMA((2,)),
         pltpu.SemaphoreType.DMA((1 + 3 * GROUPS,)),
-        pltpu.SemaphoreType.DMA((2,)),
-        pltpu.SemaphoreType.DMA((8,)),
+        pltpu.SemaphoreType.DMA((4,)),
+        pltpu.SemaphoreType.DMA((4, 5)),
     ]
     scratch += [f(events + GROUPS, 4 * per, D) for _ in stages]
     scratch += [f(events, size - 1, 4 * per, D) for _, size in stages]
@@ -1153,7 +1193,8 @@
     scratch += [f(4, seg, D) for _ in swaps]
     scratch += [f(4, size - 1, seg, D) for _, size in swaps]
     scratch += [pltpu.SemaphoreType.DMA((1,)) for _ in swaps]
-    scratch += [pltpu.SemaphoreType.DMA((4,)) for _ in swaps]
+    scratch += [pltpu.SemaphoreType.DMA((5,)) for _ in swaps]
+    scratch += [f(4, 1, rows // 2, D), f(4, 2 * graph - 1, seg, D)]
     hbm = any_space
     mid = pl.pallas_call(
         functools.partial(kernel_body, blk, graph),

time: 70.5 us -> 67.2 us (0.953)
  Pallas kernels: 69.7 us -> 66.4 us
    pallas_call x1, Pallas kernels: 67.3 us -> 64 us  [on_device(): pl.pallas_call(functools.partial(kernel_body, blk, graph), out_shape=[f(L...]
where the time goes in v4:
time: 67.2 us; the launch traced here: 67 us
  Pallas kernels  66.4 us (99%)
    pallas_call x1, Pallas kernels, on_device(): pl.pallas_call(functools.partial(kernel_body, blk, graph), out_shape=[f(L...  64 us
    pallas_call x1, Pallas kernels, on_device(): pl.pallas_call(assemble, out_shape=[jax.ShapeDtypeStruct(shape, F32) for...  2.34 us

profile of v4, /device:TPU:0, one launch (start us, length us, event | category | flops | bytes accessed | tf_op | source)
XLA Modules:
  0.0 67.0 jit_solution(9346251437182240889)
XLA Ops:
  0.6 64.0 %processor.1 = (f32[3,16,128,128]{3,2,1,0:T(8,128)S(1)}, f32[16,128,128]{2,1,0:T(8,128)S(1)}, f32[4,448,128]{2,1,0:T(8,128)S(1)}) custom-call(f32[16,128,128]{2,1,0:T(8,128)} %state_hbm.1, f32[400,128]{1,0:T(8,128)} %bitcast.13, s32[96,128]{1,0:T(8,128)} %bitcast.14, s32[16]{0:T(128)} %id_hbm.1, f32[3,8]{1,0:T(4,128)} %bitcast.15, f32[16,128,128]{2,1,0:T(8,128)} %cot_hbm.1, ...), custom_call_target="tpu_custom_call" | custom-call | tf_op jit(solution)/shard_map/processor/pallas_call | solution.py:1199
  64.7 2.3 %assemble.1 = (f32[16,128,128]{2,1,0:T(8,128)}, f32[16,128,128]{2,1,0:T(8,128)}, f32[285,2,128]{2,1,0:T(2,128)}, f32[2,128]{1,0:T(2,128)}, f32[2,128,128]{2,1,0:...) custom-call(f32[3,16,128,128]{3,2,1,0:T(8,128)S(1)} %get-tuple-eleme, ...), custom_call_target="tpu_custom_call" | custom-call | tf_op jit(solution)/shard_map/assemble/pallas_call | solution.py:1238

commit v5 on v4

--- a/solution.py
+++ b/solution.py
@@ -33,12 +33,12 @@
 SUMS_MID = ((3, 0, 1), (4, 1, 0), (5, 1, 1), (5, 0, 2), (7, 2, 1), (7, 1, 2))
 SUMS_END = ((2, 0, 0), (6, 0, 3), (6, 2, 0))
 SUMS_TURNS = ((3, 4, 2, 0), (3, 4, 1), (2, 3, 4, 1, 0))
-ORDER_NODE = "1012112001020020"
+ORDER_NODE = "0011000122210012011020"
 ORDER_EDGES = ""
-ORDER_ENTER = "002011220001111"
-ORDER_LEAVE = "1020101130001133"
+ORDER_ENTER = "02002011202000111112"
+ORDER_LEAVE = "10000300021013111131"
 ORDER_BACK = ""
-ORDER_BACK_NODE = "2020101222002211011"
+ORDER_BACK_NODE = "0200201222201222011110110"
 
 F32 = jnp.float32
 BF16 = jnp.bfloat16
@@ -267,11 +267,6 @@
     ]
     unit_recv = staged
 
-    barrier = pltpu.get_barrier_semaphore()
-    greeted = links.greeted()
-    for peer in greeted:
-        pl.semaphore_signal(barrier, inc=1, device_id=peer, device_id_type=MESH)
-
     parts = [
         (offset_hbm, offset_in),
         (field_hbm, field_in),
@@ -292,6 +287,11 @@
     loads = [pltpu.make_async_copy(src, to, load_sem.at[i]) for i, (src, to) in enumerate(parts)]
     for load in loads:
         load.start()
+
+    barrier = pltpu.get_barrier_semaphore()
+    greeted = links.greeted()
+    for peer in greeted:
+        pl.semaphore_signal(barrier, inc=1, device_id=peer, device_id_type=MESH)
 
     rows = lax.broadcasted_iota(jnp.int32, (D, K * D), 0)
     cols = lax.broadcasted_iota(jnp.int32, (D, K * D), 1)
@@ -428,16 +428,21 @@
         w_in[l, pl.ds(3 * D + 3 * AUX, AUX), :] = jnp.zeros((AUX, 3 * D), BF16)
         second = 0.5 * ew2[l]
         w_e2[l] = doubled(second)
-        w_e2t[l] = doubled(second.T)
         w_agg[l] = doubled(0.5 * n_agg)
         w_n2[l] = doubled(0.5 * nw2[l])
-        w_n2t[l] = doubled(nw2[l].T)
-        head, tail = split(jnp.concatenate([n_self.T, 0.5 * n_agg.T], 1))
-        w_np[l, pl.ds(0, D), :] = head
-        w_np[l, pl.ds(D, D), :] = head
-        w_np[l, pl.ds(2 * D, D), :] = tail
-        w_ep[l, pl.ds(0, D), :] = pair(w_self.T)
-        w_ep[l, pl.ds(D, D), :] = pair(w_far.T)
+
+    def back_weights():
+        for l in range(LAYERS):
+            w_e2t[l] = doubled(0.5 * ew2[l].T)
+            w_n2t[l] = doubled(nw2[l].T)
+            n_self = nw1[l, pl.ds(0, D), :]
+            n_agg = nw1[l, pl.ds(D, D), :]
+            head, tail = split(jnp.concatenate([n_self.T, 0.5 * n_agg.T], 1))
+            w_np[l, pl.ds(0, D), :] = head
+            w_np[l, pl.ds(D, D), :] = head
+            w_np[l, pl.ds(2 * D, D), :] = tail
+            w_ep[l, pl.ds(0, D), :] = pair(ew1[l, pl.ds(0, D), :].T)
+            w_ep[l, pl.ds(D, D), :] = pair(ew1[l, pl.ds(D, D), :].T)
 
     kinds = (
         (0, GROUPS, pl.ds(0, 2 * per)),
@@ -510,7 +515,7 @@
     def enter(p):
         l, g = div(p, GROUPS), rem(p, GROUPS)
         base = g * per
-        slot = rem(p, 2)
+        slot = rem(p, GROUPS)
         for c in range(per):
             t = base + c
             mean = fin[p, 0, pl.ds(c, 1), :]
@@ -520,6 +525,8 @@
             near = (near - mean) * scale
             yh[t] = near
             xs[l, t, pl.ds(nodes, 2 * RIM), :] = pair(near)
+            if c == per // 2 - 1:
+                yield
         x = rows_of(xs, l, base, 0, ext)
         side = xa[pl.ds(base, per)].reshape(per * ext, D)
         yield
@@ -535,7 +542,46 @@
                 at + nodes + RIM : at + ext, D : 2 * D
             ]
             n_buf[slot, c] = p4[at : at + nodes, 2 * D :]
-        yield
+            if c % 2:
+                yield
+
+    def first_main(g):
+        base = g * per
+        for c in range(per):
+            xs[0, base + c, pl.ds(0, nodes), :] = pair(raw[0, base + c])
+        x = rows_of(xs, 0, base, 0, nodes)
+        side = xa[pl.ds(base, per), pl.ds(0, nodes), :].reshape(per * nodes, D)
+        product = dot(x, w_in[0, pl.ds(0, 2 * D), :])
+        product = product + dot(
+            jnp.concatenate([x[:, :D], side], 1), w_in[0, pl.ds(2 * D, 2 * D), :]
+        )
+        for c in range(per):
+            part = product[c * nodes : (c + 1) * nodes]
+            a_buf[0, base + c] = part[:, :D]
+            r_buf[0, base + c, pl.ds(RIM, nodes), :] = part[:, D : 2 * D]
+            n_buf[g, c] = part[:, 2 * D :]
+
+    def first_rims():
+        lane = lax.broadcasted_iota(jnp.int32, (RIM, D), 1)
+        moved = jnp.where((lane == A_PLACE) | (lane == 2 * AUX + A_PLACE), float(nodes), 0.0)
+        near = []
+        for t in range(traj):
+            side = jnp.concatenate(
+                [
+                    pltpu.roll(hr[1, 0, t], HALO, 0) - moved,
+                    pltpu.roll(hr[0, 0, t], RIM - HALO, 0) + moved,
+                ],
+                0,
+            ).astype(BF16)
+            xa[t, pl.ds(nodes, 2 * RIM), :] = side
+            head, tail = split(jnp.concatenate([hr[1, 0, t], hr[0, 0, t]], 0))
+            xs[0, t, pl.ds(nodes, 2 * RIM), :] = jnp.concatenate([head, tail], 1)
+            near.append(jnp.concatenate([head, tail, head, side], 1))
+        product = dot(jnp.concatenate(near, 0), w_in[0, :, pl.ds(D, D)])
+        for t in range(traj):
+            at = t * 2 * RIM
+            r_buf[0, t, pl.ds(0, RIM), :] = product[at : at + RIM]
+            r_buf[0, t, pl.ds(RIM + nodes, RIM), :] = product[at + RIM : at + 2 * RIM]
 
     def edges(p, s):
         l, g = div(p, GROUPS), rem(p, GROUPS)
@@ -545,9 +591,8 @@
         for i, o in enumerate(OFFSETS):
             half = a_buf[l, t] + r_buf[l, t, pl.ds(RIM + o, nodes), :]
             hidden.append(pair(half * (1.0 + jnp.tanh(half))))
-            if i == K // 2 - 1:
+            if i % 2:
                 yield
-        yield
         product = dot(jnp.concatenate(hidden, 0), w_e2[l])
         yield
         summed = None
@@ -558,7 +603,7 @@
             message = scaled * half
             summed = message if summed is None else summed + message
             slope[l, t, pl.ds(i * nodes, nodes), :] = scaled + message * (1.0 - tanh)
-            if i == K // 2 - 1:
+            if i % 2 and i < K - 1:
                 yield
         dag[rem(p, 2), s] = summed * (1.0 / K)
         yield
@@ -567,12 +612,13 @@
         l, g = div(p, GROUPS), rem(p, GROUPS)
         base = g * per
         slot = rem(p, 2)
+        here = rem(p, GROUPS)
         node2 = 0.5 * nb2[pl.ds(l, 1), :]
         both = pair(dag[slot].reshape(per * nodes, D))
         agg2[l, pl.ds(base, per)] = both.reshape(per, nodes, 2 * D)
         product = dot(both, w_agg[l])
         yield
-        half = n_buf[slot].reshape(per * nodes, D) + halves(product)
+        half = n_buf[here].reshape(per * nodes, D) + halves(product)
         act, rise = swish_parts(half)
         sn1[l, pl.ds(base, per)] = (0.5 * rise).reshape(per, nodes, D)
         both = pair(act)
@@ -600,28 +646,34 @@
                 yield
 
     def forward(p, _):
-        @pl.when(p > 0)
+        border = p == GROUPS
+
+        @pl.when((p > 0) & jnp.logical_not(border))
         def _():
             weave(ORDER_NODE, edges(p, 0), edges(p, 1), node(p - 1))
 
-        @pl.when(p == 0)
+        @pl.when((p == 0) | border)
         def _():
             weave(ORDER_EDGES, edges(p, 0), edges(p, 1))
 
-        @pl.when(p > 0)
+        @pl.when((p > 0) & jnp.logical_not(border))
         def _():
             stat_send(p - 1, 0)
 
-        @pl.when((p > 0) & (p <= GROUPS))
+        @pl.when((p > 0) & (p < GROUPS))
         def _():
             ring_send(*layer_rims(p - 1), p)
+
+        @pl.when(border)
+        def _():
+            stat_forward(p - 1)
 
         def ready():
             stat_finish(p + 1 - GROUPS)
             arrived(layer_rims(p + 1 - GROUPS)[1], rim_rsem.at[p + 2 - GROUPS])
 
         pl.when((p + 1 > GROUPS) & (p + 1 < phases))(ready)
-        alone = (p + 1 == GROUPS) | (p + 1 == phases)
+        alone = (p + 1 <= GROUPS) | (p + 1 == phases)
 
         @pl.when(jnp.logical_not(alone))
         def _():
@@ -633,11 +685,14 @@
 
         @pl.when(p + 1 == GROUPS)
         def _():
+            weave("", node(p))
+            stat_send(p, 0)
+            ring_send(*layer_rims(p), p + 1)
             stat_forward(p - 1)
             ready()
             weave("", enter(p + 1))
 
-        @pl.when((p > 0) & (p + 1 != GROUPS))
+        @pl.when((p > 0) & (p + 1 != GROUPS) & jnp.logical_not(border))
         def _():
             stat_forward(p - 1)
 
@@ -671,6 +726,8 @@
             acc_bn[l] += jnp.sum(first.reshape(nodes // 8, 8, D), 0)
             deltas.append(delta)
             firsts.append(first)
+            if c == per // 2 - 1:
+                yield
         d2 = pair(jnp.concatenate(firsts, 0))
         yield
         x = rows_of(xs, l, base, 0, nodes)
@@ -690,7 +747,7 @@
             dag[rem(p, 2), c] = product[at : at + nodes, D:] * (1.0 / K)
         acc_agg[l] += dot_t(agg2[l, pl.ds(base, per)].reshape(size, 2 * D), d1)
         yield
-        acc_nx[l] += dot_t(jnp.concatenate([x, side], 1), d1)
+        acc_nx[l] += dot_t(jnp.concatenate([x, side[:, : 2 * AUX]], 1), d1)
         yield
 
     def back_edges(p, s):
@@ -709,7 +766,7 @@
             delta = coming * slope[l, t, pl.ds(i * nodes, nodes), :]
             bias = delta if bias is None else bias + delta
             deltas.append(pair(delta))
-            if i == K // 2 - 1:
+            if i % 2 and i < K - 1:
                 yield
         d2 = jnp.concatenate(deltas, 0)
         acc_be[l] += jnp.sum(bias.reshape(nodes // 8, 8, D), 0)
@@ -723,6 +780,8 @@
             d1 = halves(product[i * nodes : (i + 1) * nodes]) * rises[i]
             near = d1 if near is None else near + d1
             mine[i, pl.ds(RIM, nodes), :] = d1
+            if i == K // 2 - 1:
+                yield
         yield
         far = None
         left = None
@@ -754,7 +813,7 @@
         slot = rem(p, 2)
         x = rows_of(xs, l, base, 0, ext)
         side = xa[pl.ds(base, per)].reshape(size, D)
-        inputs = jnp.concatenate([x, side], 1)
+        inputs = jnp.concatenate([x, side[:, : 2 * AUX]], 1)
         high = dxh[slot].reshape(size, 2 * D)
         low = dxl[slot].reshape(size, 2 * D)
         acc_x[l] += dot_t(
@@ -823,25 +882,33 @@
 
         sum_hook(SUMS_MID, p)
 
-        @pl.when(p + 1 < phases)
-        def _():
+        def ready():
             stat_finish(GROUPS + p + 1)
 
-        @pl.when((p + 1 >= GROUPS) & (p + 1 < phases))
-        def _():
+        def rims_ready():
             arrived(grad_rims(p + 1 - GROUPS)[1], rim_rsem.at[p + 2])
 
-        @pl.when(p + 1 < phases)
+        alone = (p + 1 == GROUPS) | (p + 1 == phases)
+        pl.when(jnp.logical_not(alone))(ready)
+        pl.when((p + 1 > GROUPS) & (p + 1 < phases))(rims_ready)
+
+        @pl.when(jnp.logical_not(alone))
         def _():
             weave(ORDER_BACK_NODE, back_edges(p, 2), back_edges(p, 3), back_node(p + 1))
 
-        @pl.when(p + 1 == phases)
+        @pl.when(alone)
         def _():
             weave(ORDER_BACK, back_edges(p, 2), back_edges(p, 3))
 
         @pl.when((p > 0) & (p <= GROUPS))
         def _():
             stat_forward(phases + p - 1)
+
+        @pl.when(p + 1 == GROUPS)
+        def _():
+            ready()
+            rims_ready()
+            weave("", back_node(p + 1))
 
         @pl.when(p == GROUPS - 2)
         def _():
@@ -980,22 +1047,14 @@
         for phase, n, step in table:
             pl.when(p == phase)(functools.partial(sum_step, n, step))
 
-    lane = lax.broadcasted_iota(jnp.int32, (RIM, D), 1)
-    moved = jnp.where((lane == A_PLACE) | (lane == 2 * AUX + A_PLACE), float(nodes), 0.0)
+    for g in range(GROUPS):
+        first_main(g)
     arrived(first[1], rim_rsem.at[0])
-    for t in range(traj):
-        side = jnp.concatenate(
-            [
-                pltpu.roll(hr[1, 0, t], HALO, 0) - moved,
-                pltpu.roll(hr[0, 0, t], RIM - HALO, 0) + moved,
-            ],
-            0,
-        )
-        xa[t, pl.ds(nodes, 2 * RIM), :] = side.astype(BF16)
-    weave("", enter(0))
+    first_rims()
     lax.fori_loop(0, phases, forward, 0)
     weave("", node(phases - 1))
     stat_send(phases - 1, 0)
+    back_weights()
     stat_finish(GROUPS)
     weave("", back_node(0))
     lax.fori_loop(0, phases, backward, 0)
@@ -1156,7 +1215,7 @@
         b(traj, ext, D),
         f(L, traj, nodes, D),
         f(L, traj, ext, D),
-        f(2, per, nodes, D),
+        f(GROUPS, per, nodes, D),
         f(L, traj, K * nodes, D),
         b(L, traj, nodes, 2 * D),
         b(L, traj, nodes, 2 * D),
@@ -1169,9 +1228,9 @@
         b(2, per, ext, 2 * D),
         f(L, 2 * D, 2 * D),
         f(L, 2 * D, 2 * D),
-        f(L, 3 * D, 2 * D),
+        f(L, 2 * D + 2 * AUX, 2 * D),
         f(L, 2 * D, 2 * D),
-        f(L, 3 * D, 2 * D),
+        f(L, 2 * D + 2 * AUX, 2 * D),
         f(L, 8, D),
         f(L, 8, D),
         f(events + GROUPS, 4, per, D),

time: 67.2 us -> 66 us (0.982)
  Pallas kernels: 66.4 us -> 65.2 us
    pallas_call x1, Pallas kernels: 64 us -> 62.8 us  [on_device(): pl.pallas_call(functools.partial(kernel_body, blk, graph), out_shape=[f(L...]
where the time goes in v5:
time: 66 us; the launch traced here: 65.8 us
  Pallas kernels  65.2 us (99%)
  between operations  0.66 us (1%)
    pallas_call x1, Pallas kernels, on_device(): pl.pallas_call(functools.partial(kernel_body, blk, graph), out_shape=[f(L...  62.8 us
    pallas_call x1, Pallas kernels, on_device(): pl.pallas_call(assemble, out_shape=[jax.ShapeDtypeStruct(shape, F32) for...  2.34 us

profile of v5, /device:TPU:0, one launch (start us, length us, event | category | flops | bytes accessed | tf_op | source)
XLA Modules:
  0.0 65.8 jit_solution(11913127250116940258)
XLA Ops:
  0.6 62.8 %processor.1 = (f32[3,16,128,128]{3,2,1,0:T(8,128)S(1)}, f32[16,128,128]{2,1,0:T(8,128)S(1)}, f32[4,448,128]{2,1,0:T(8,128)S(1)}) custom-call(f32[16,128,128]{2,1,0:T(8,128)} %state_hbm.1, f32[400,128]{1,0:T(8,128)} %bitcast.13, s32[96,128]{1,0:T(8,128)} %bitcast.14, s32[16]{0:T(128)} %id_hbm.1, f32[3,8]{1,0:T(4,128)} %bitcast.15, f32[16,128,128]{2,1,0:T(8,128)} %cot_hbm.1, ...), custom_call_target="tpu_custom_call" | custom-call | tf_op jit(solution)/shard_map/processor/pallas_call | solution.py:1258
  63.5 2.3 %assemble.1 = (f32[16,128,128]{2,1,0:T(8,128)}, f32[16,128,128]{2,1,0:T(8,128)}, f32[285,2,128]{2,1,0:T(2,128)}, f32[2,128]{1,0:T(2,128)}, f32[2,128,128]{2,1,0:...) custom-call(f32[3,16,128,128]{3,2,1,0:T(8,128)S(1)} %get-tuple-eleme, ...), custom_call_target="tpu_custom_call" | custom-call | tf_op jit(solution)/shard_map/assemble/pallas_call | solution.py:1297

commit v6 on v5

--- a/solution.py
+++ b/solution.py
@@ -34,11 +34,11 @@
 SUMS_END = ((2, 0, 0), (6, 0, 3), (6, 2, 0))
 SUMS_TURNS = ((3, 4, 2, 0), (3, 4, 1), (2, 3, 4, 1, 0))
 ORDER_NODE = "0011000122210012011020"
-ORDER_EDGES = ""
+ORDER_EDGES = "00001000111111"
 ORDER_ENTER = "02002011202000111112"
-ORDER_LEAVE = "10000300021013111131"
-ORDER_BACK = ""
-ORDER_BACK_NODE = "0200201222201222011110110"
+ORDER_LEAVE = "00003000211013111131"
+ORDER_BACK = "1010001110001101"
+ORDER_BACK_NODE = "0201102202221122200111010"
 
 F32 = jnp.float32
 BF16 = jnp.bfloat16
@@ -148,6 +148,10 @@
 
 def rem(value, by):
     return value % by if isinstance(value, int) else lax.rem(value, jnp.int32(by))
+
+
+def negated(condition):
+    return not condition if isinstance(condition, bool) else jnp.logical_not(condition)
 
 
 def weave(order, *parts):
@@ -648,7 +652,7 @@
     def forward(p, _):
         border = p == GROUPS
 
-        @pl.when((p > 0) & jnp.logical_not(border))
+        @pl.when((p > 0) & negated(border))
         def _():
             weave(ORDER_NODE, edges(p, 0), edges(p, 1), node(p - 1))
 
@@ -656,7 +660,7 @@
         def _():
             weave(ORDER_EDGES, edges(p, 0), edges(p, 1))
 
-        @pl.when((p > 0) & jnp.logical_not(border))
+        @pl.when((p > 0) & negated(border))
         def _():
             stat_send(p - 1, 0)
 
@@ -675,7 +679,7 @@
         pl.when((p + 1 > GROUPS) & (p + 1 < phases))(ready)
         alone = (p + 1 <= GROUPS) | (p + 1 == phases)
 
-        @pl.when(jnp.logical_not(alone))
+        @pl.when(negated(alone))
         def _():
             weave(ORDER_ENTER, edges(p, 2), edges(p, 3), enter(p + 1))
 
@@ -692,7 +696,7 @@
             ready()
             weave("", enter(p + 1))
 
-        @pl.when((p > 0) & (p + 1 != GROUPS) & jnp.logical_not(border))
+        @pl.when((p > 0) & (p + 1 != GROUPS) & negated(border))
         def _():
             stat_forward(p - 1)
 
@@ -889,10 +893,10 @@
             arrived(grad_rims(p + 1 - GROUPS)[1], rim_rsem.at[p + 2])
 
         alone = (p + 1 == GROUPS) | (p + 1 == phases)
-        pl.when(jnp.logical_not(alone))(ready)
+        pl.when(negated(alone))(ready)
         pl.when((p + 1 > GROUPS) & (p + 1 < phases))(rims_ready)
 
-        @pl.when(jnp.logical_not(alone))
+        @pl.when(negated(alone))
         def _():
             weave(ORDER_BACK_NODE, back_edges(p, 2), back_edges(p, 3), back_node(p + 1))
 
@@ -1051,13 +1055,15 @@
         first_main(g)
     arrived(first[1], rim_rsem.at[0])
     first_rims()
-    lax.fori_loop(0, phases, forward, 0)
+    for p in range(phases):
+        forward(p, 0)
     weave("", node(phases - 1))
     stat_send(phases - 1, 0)
     back_weights()
     stat_finish(GROUPS)
     weave("", back_node(0))
-    lax.fori_loop(0, phases, backward, 0)
+    for p in range(phases):
+        backward(p, 0)
     unit_second(unit.at[3], acc_e2.at[0])
     sum_step(3, 0)
     weave("", leave_weights(phases - 1))

time: 66 us -> 63.7 us (0.965)
  Pallas kernels: 65.2 us -> 62.7 us
    pallas_call x1, Pallas kernels: 62.8 us -> 60.4 us  [on_device(): pl.pallas_call(functools.partial(kernel_body, blk, graph), out_shape=[f(L...]
where the time goes in v6:
time: 63.7 us; the launch traced here: 63.6 us
  Pallas kernels  62.7 us (98%)
  between operations  0.84 us (1%)
    pallas_call x1, Pallas kernels, on_device(): pl.pallas_call(functools.partial(kernel_body, blk, graph), out_shape=[f(L...  60.4 us
    pallas_call x1, Pallas kernels, on_device(): pl.pallas_call(assemble, out_shape=[jax.ShapeDtypeStruct(shape, F32) for...  2.34 us

profile of v6, /device:TPU:0, one launch (start us, length us, event | category | flops | bytes accessed | tf_op | source)
XLA Modules:
  0.0 63.6 jit_solution(17773411849322610741)
XLA Ops:
  0.6 60.4 %processor.1 = (f32[3,16,128,128]{3,2,1,0:T(8,128)S(1)}, f32[16,128,128]{2,1,0:T(8,128)S(1)}, f32[4,448,128]{2,1,0:T(8,128)S(1)}) custom-call(f32[16,128,128]{2,1,0:T(8,128)} %state_hbm.1, f32[400,128]{1,0:T(8,128)} %bitcast.13, s32[96,128]{1,0:T(8,128)} %bitcast.14, s32[16]{0:T(128)} %id_hbm.1, f32[3,8]{1,0:T(4,128)} %bitcast.15, f32[16,128,128]{2,1,0:T(8,128)} %cot_hbm.1, ...), custom_call_target="tpu_custom_call" | custom-call | tf_op jit(solution)/shard_map/processor/pallas_call | solution.py:1264
  61.0 2.3 %assemble.1 = (f32[16,128,128]{2,1,0:T(8,128)}, f32[16,128,128]{2,1,0:T(8,128)}, f32[285,2,128]{2,1,0:T(2,128)}, f32[2,128]{1,0:T(2,128)}, f32[2,128,128]{2,1,0:...) custom-call(f32[3,16,128,128]{3,2,1,0:T(8,128)S(1)} %get-tuple-eleme, ...), custom_call_target="tpu_custom_call" | custom-call | tf_op jit(solution)/shard_map/assemble/pallas_call | solution.py:1303

commit v7 on v6

--- a/solution.py
+++ b/solution.py
@@ -30,6 +30,7 @@
 UNIT_AUX = 3 * D
 UNIT_ROWS = UNIT_AUX + AUX
 STAT_SIZES = (2, 8)
+HAND_ON = 12
 SUMS_MID = ((3, 0, 1), (4, 1, 0), (5, 1, 1), (5, 0, 2), (7, 2, 1), (7, 1, 2))
 SUMS_END = ((2, 0, 0), (6, 0, 3), (6, 2, 0))
 SUMS_TURNS = ((3, 4, 2, 0), (3, 4, 1), (2, 3, 4, 1, 0))
@@ -307,18 +308,6 @@
     for u in range(4):
         rest = unit.shape[1] - UNIT_ROWS
         unit[u, pl.ds(UNIT_ROWS, rest), :] = jnp.zeros((rest, D), F32)
-    fin[pl.ds(0, GROUPS), 0] = jnp.zeros((GROUPS, per, D), F32)
-    fin[pl.ds(0, GROUPS), 1] = jnp.ones((GROUPS, per, D), F32)
-    rr[0] = jnp.zeros(rr.shape[1:], F32)
-    for stage in range(len(stages)):
-        for low, high, unused in (
-            (0, GROUPS, pl.ds(2 * per, 2 * per)),
-            (phases, phases + GROUPS, pl.ds(0, 2 * per)),
-        ):
-            cut = pl.ds(low, high - low)
-            stat[stage][cut, unused, :] = jnp.zeros((GROUPS, 2 * per, D), F32)
-            arrive = stat_recv[stage]
-            arrive[cut, :, unused, :] = jnp.zeros((GROUPS, arrive.shape[1], 2 * per, D), F32)
     place = lax.broadcasted_iota(jnp.int32, (1, nodes), 1).astype(F32) - nodes / 2
     loads[0].wait()
     offs = [offset_in[pl.ds(k * traj, traj), :] for k in range(K)]
@@ -486,32 +475,45 @@
         parts = [stat[stage].at[event]] + [
             stat_recv[stage].at[event, shift - 1] for shift in range(1, size)
         ]
-        m, m2, u, c = [[part[pl.ds(q * per, per), :] for part in parts] for q in range(4)]
-        mean = sum(m[1:], m[0]) * (1.0 / size)
-        gaps = [value - mean for value in m]
-        spread2 = sum((gap * gap for gap in gaps[1:]), gaps[0] * gaps[0])
-        m2_all = sum(m2[1:], m2[0]) + spread2 * float(nodes * stride)
-        u_all = sum(u[1:], u[0])
-        c_all = sum(c[1:], c[0])
-        for gap, value in zip(gaps, u):
-            c_all = c_all + gap * value
+        forward_rows, gradient_rows = event < phases, event >= GROUPS
+
+        def row(q):
+            return [part[pl.ds(q * per, per), :] for part in parts]
+
+        mean = m2_all = u_all = c_all = None
+        if gradient_rows:
+            u, c = row(2), row(3)
+            u_all = sum(u[1:], u[0])
+            c_all = sum(c[1:], c[0])
+        if forward_rows:
+            m, m2 = row(0), row(1)
+            mean = sum(m[1:], m[0]) * (1.0 / size)
+            gaps = [value - mean for value in m]
+            spread2 = sum((gap * gap for gap in gaps[1:]), gaps[0] * gaps[0])
+            m2_all = sum(m2[1:], m2[0]) + spread2 * float(nodes * stride)
+            if gradient_rows:
+                for gap, value in zip(gaps, u):
+                    c_all = c_all + gap * value
         return mean, m2_all, u_all, c_all
 
     def stat_forward(event):
         for stage in range(1, len(stages)):
             merged = stat_merge(event, stage - 1)
             for q, value in enumerate(merged):
-                stat[stage][event, pl.ds(q * per, per), :] = value
+                if value is not None:
+                    stat[stage][event, pl.ds(q * per, per), :] = value
             stat_send(event, stage)
 
     def stat_finish(event):
         mean, m2, u, c = stat_merge(event, len(stages) - 1)
-        scale = lax.rsqrt(m2 * (1.0 / total) + EPSILON)
         at = event + GROUPS
-        fin[at, 0] = mean
-        fin[at, 1] = scale
-        fin[at, 2] = u * (1.0 / total)
-        fin[at, 3] = jnp.where(event < phases, scale, 1.0) * c * (1.0 / total)
+        if mean is not None:
+            scale = lax.rsqrt(m2 * (1.0 / total) + EPSILON)
+            fin[at, 0] = mean
+            fin[at, 1] = scale
+        if u is not None:
+            fin[at, 2] = u * (1.0 / total)
+            fin[at, 3] = c * (1.0 / total) if mean is None else scale * c * (1.0 / total)
 
     def rows_of(buf, l, t, start, size):
         return buf[l, pl.ds(t, per), pl.ds(start, size), :].reshape(per * size, buf.shape[-1])
@@ -634,27 +636,42 @@
         sn2[l, pl.ds(base, per)] = (0.5 * rise).reshape(per, nodes, D)
         for c in range(per):
             t = base + c
-            before = (raw[l, t] - fin[p, 0, pl.ds(c, 1), :]) * fin[p, 1, pl.ds(c, 1), :]
+            before = raw[l, t]
+            if l > 0:
+                before = (before - fin[p, 0, pl.ds(c, 1), :]) * fin[p, 1, pl.ds(c, 1), :]
             new = before + act[c * nodes : (c + 1) * nodes]
             raw[l + 1, t] = new
-            hs[0, 1 + l, t] = new[:RIM]
-            hs[1, 1 + l, t] = new[nodes - RIM :]
             mean = jnp.sum(new, 0, keepdims=True) * (1.0 / nodes)
             gap = new - mean
-            up = dst[t]
             stat[0][p, pl.ds(c, 1), :] = mean
             stat[0][p, pl.ds(per + c, 1), :] = jnp.sum(gap * gap, 0, keepdims=True)
-            stat[0][p, pl.ds(2 * per + c, 1), :] = jnp.sum(up, 0, keepdims=True)
-            stat[0][p, pl.ds(3 * per + c, 1), :] = jnp.sum(up * gap, 0, keepdims=True)
+            if l < LAYERS - 1:
+                hs[0, 1, t] = new[:RIM]
+                hs[1, 1, t] = new[nodes - RIM :]
+            else:
+                up = dst[t]
+                stat[0][p, pl.ds(2 * per + c, 1), :] = jnp.sum(up, 0, keepdims=True)
+                stat[0][p, pl.ds(3 * per + c, 1), :] = jnp.sum(up * gap, 0, keepdims=True)
             if c % 2:
                 yield
 
+    def hand_on(event):
+        if event is not None:
+            stat_forward(event)
+        yield
+
     def forward(p, _):
         border = p == GROUPS
 
         @pl.when((p > 0) & negated(border))
         def _():
-            weave(ORDER_NODE, edges(p, 0), edges(p, 1), node(p - 1))
+            weave(
+                ORDER_NODE[:HAND_ON] + "3" + ORDER_NODE[HAND_ON:],
+                edges(p, 0),
+                edges(p, 1),
+                node(p - 1),
+                hand_on(p - 2 if 1 < p < GROUPS else None),
+            )
 
         @pl.when((p == 0) | border)
         def _():
@@ -696,7 +713,7 @@
             ready()
             weave("", enter(p + 1))
 
-        @pl.when((p > 0) & (p + 1 != GROUPS) & negated(border))
+        @pl.when(p > GROUPS)
         def _():
             stat_forward(p - 1)
 
@@ -715,16 +732,18 @@
             mu = fin[source, 2, pl.ds(c, 1), :]
             cross = fin[source, 3, pl.ds(c, 1), :]
             y = (raw[l + 1, t] - fin[own, 0, pl.ds(c, 1), :]) * scale
-            raw[l + 1, t] = y
             up = dst[t]
-            up = jnp.concatenate(
-                [
-                    up[:RIM] + rr[back, 1, t],
-                    up[RIM : nodes - RIM],
-                    up[nodes - RIM :] + rr[back, 0, t],
-                ],
-                0,
-            )
+            if l == LAYERS - 1:
+                raw[l + 1, t] = y
+            else:
+                up = jnp.concatenate(
+                    [
+                        up[:RIM] + rr[back, 1, t],
+                        up[RIM : nodes - RIM],
+                        up[nodes - RIM :] + rr[back, 0, t],
+                    ],
+                    0,
+                )
             delta = scale * (up - mu - y * cross)
             first = delta * sn2[l, t]
             acc_bn[l] += jnp.sum(first.reshape(nodes // 8, 8, D), 0)
@@ -845,13 +864,14 @@
             rims = product[at + nodes : at + ext]
             rs[back, 0, t] = rims[:RIM]
             rs[back, 1, t] = rims[RIM:]
-            y = (raw[l, t] - fin[own, 0, pl.ds(c, 1), :]) * fin[own, 1, pl.ds(c, 1), :]
-            stat[0][event, pl.ds(2 * per + c, 1), :] = jnp.sum(new, 0, keepdims=True) + jnp.sum(
-                rims, 0, keepdims=True
-            )
-            stat[0][event, pl.ds(3 * per + c, 1), :] = jnp.sum(
-                new * y, 0, keepdims=True
-            ) + jnp.sum(rims * yh[t], 0, keepdims=True)
+            if l > 0:
+                y = (raw[l, t] - fin[own, 0, pl.ds(c, 1), :]) * fin[own, 1, pl.ds(c, 1), :]
+                stat[0][event, pl.ds(2 * per + c, 1), :] = jnp.sum(
+                    new, 0, keepdims=True
+                ) + jnp.sum(rims, 0, keepdims=True)
+                stat[0][event, pl.ds(3 * per + c, 1), :] = jnp.sum(
+                    new * y, 0, keepdims=True
+                ) + jnp.sum(rims * yh[t], 0, keepdims=True)
             if c % 2:
                 yield
 
@@ -1240,7 +1260,7 @@
         f(L, 8, D),
         f(L, 8, D),
         f(events + GROUPS, 4, per, D),
-        f(2, 1 + L, traj, RIM, D),
+        f(2, L, traj, RIM, D),
         f(2, 2, traj, RIM, D),
         f(L, 2, traj, RIM, D),
         f(L + 1, 2, traj, RIM, D),
@@ -1251,7 +1271,7 @@
         pltpu.SemaphoreType.DMA((4,)),
         pltpu.SemaphoreType.DMA((4, 5)),
     ]
-    scratch += [f(events + GROUPS, 4 * per, D) for _ in stages]
+    scratch += [f(events, 4 * per, D) for _ in stages]
     scratch += [f(events, size - 1, 4 * per, D) for _, size in stages]
     scratch += [pltpu.SemaphoreType.DMA((1,)) for _ in stages]
     scratch += [pltpu.SemaphoreType.DMA((events,)) for _ in stages]

time: 63.7 us -> 63.2 us (level)
  no operation moved by 1% of the time
where the time goes in v7:
time: 63.2 us; the launch traced here: 63 us
  Pallas kernels  62.2 us (98%)
  between operations  0.84 us (1%)
    pallas_call x1, Pallas kernels, on_device(): pl.pallas_call(functools.partial(kernel_body, blk, graph), out_shape=[f(L...  59.8 us
    pallas_call x1, Pallas kernels, on_device(): pl.pallas_call(assemble, out_shape=[jax.ShapeDtypeStruct(shape, F32) for...  2.34 us

profile of v7, /device:TPU:0, one launch (start us, length us, event | category | flops | bytes accessed | tf_op | source)
XLA Modules:
  0.0 63.0 jit_solution(16609358354748673850)
XLA Ops:
  0.6 59.8 %processor.1 = (f32[3,16,128,128]{3,2,1,0:T(8,128)S(1)}, f32[16,128,128]{2,1,0:T(8,128)S(1)}, f32[4,448,128]{2,1,0:T(8,128)S(1)}) custom-call(f32[16,128,128]{2,1,0:T(8,128)} %state_hbm.1, f32[400,128]{1,0:T(8,128)} %bitcast.13, s32[96,128]{1,0:T(8,128)} %bitcast.14, s32[16]{0:T(128)} %id_hbm.1, f32[3,8]{1,0:T(4,128)} %bitcast.15, f32[16,128,128]{2,1,0:T(8,128)} %cot_hbm.1, ...), custom_call_target="tpu_custom_call" | custom-call | tf_op jit(solution)/shard_map/processor/pallas_call | solution.py:1284
  60.5 2.3 %assemble.1 = (f32[16,128,128]{2,1,0:T(8,128)}, f32[16,128,128]{2,1,0:T(8,128)}, f32[285,2,128]{2,1,0:T(2,128)}, f32[2,128]{1,0:T(2,128)}, f32[2,128,128]{2,1,0:...) custom-call(f32[3,16,128,128]{3,2,1,0:T(8,128)S(1)} %get-tuple-eleme, ...), custom_call_target="tpu_custom_call" | custom-call | tf_op jit(solution)/shard_map/assemble/pallas_call | solution.py:1323
